TPU v7x, 32 devices: a whole 2x2x4 slice. The times are simulated.
32 devices in a mesh: parts: 1, train: 32 (over z, y, x, core).
Axes of the slice: x: 2, y: 2, z: 4, core: 2. Of those that a mesh axis runs over, the one named last changes fastest.
Arguments:
- train_layer_input: bfloat16 [16384, 4096], P(('parts', 'train')), may hold values from -6 to 6
- train_output_gradient: bfloat16 [16384, 4096], P(('parts', 'train')), may hold values from -6 to 6
- train_example_index: int32 [32, 512], P(('parts', 'train')), may hold values from 0 to 31, never falling along the last dimension, each value on 1 to 32 neighbouring positions
- eval_layer_input: bfloat16 [4096, 4096], P(('parts', 'train')), may hold values from -6 to 6
- eval_output_gradient: bfloat16 [4096, 4096], P(('parts', 'train')), may hold values from -6 to 6
- eval_rollout_index: int32 [32, 128], P(('parts', 'train')), may hold values from 0 to 15, never falling along the last dimension, each value on 1 to 16 neighbouring positions
- adapter_down: bfloat16 [4096, 16], replicated, may hold values from -0.09375 to 0.09375
- adapter_up: bfloat16 [16, 4096], replicated, may hold values from -0.09375 to 0.09375
- gradient_projector: bfloat16 [4096, 256], P('train'), may hold values from -0.09375 to 0.09375
- input_projector: bfloat16 [4096, 256], P('train'), may hold values from -0.09375 to 0.09375
- paired_eval_index: int32 [32, 16], P('parts'), may hold values from 0 to 31, all different within a row
- live_slot_count: int32 [32], P('parts'), may hold values from 1 to 16, as said below
Outputs:
- scores: float32 [32, 16, 32, 16], P(('parts', 'train'))
Inputs may be any that keep to these rules, and one draw needn't show every extreme that they name: Each train block's slots name distinct eval blocks; slots from live_slot_count onward are unused; some train block uses all 16 slots.
All inputs are finite; a program needn't handle non-finite values.
Results may differ from a plain program's by a relative error of at most 0.004.
Values may be sent and summed in bfloat16 or wider, within the bound.
No kernel may reach another device: no remote copies, remote signals or barrier semaphores. Data moves between devices by JAX's collectives and lax.ppermute only.
A program may use at most 128 MiB of HBM per device.

v0:
```python
import jax
import jax.numpy as jnp
from jax import lax
from jax.sharding import PartitionSpec as P

K = 8192
TRAIN_EXAMPLES = 32
EVAL_ROLLOUTS = 16
SLOTS = 16


def example_features(hidden_down, backward_up, grad_proj, input_proj, segment_index, item_number):
    onehot = (segment_index[None, :] == jnp.arange(item_number, dtype=jnp.int32)[:, None]).astype(
        jnp.float32
    )
    weighted_a = onehot[:, :, None] * hidden_down[None, :, :]
    weighted_b = onehot[:, :, None] * backward_up[None, :, :]
    part_b = jnp.einsum("etr,tk->erk", weighted_a, grad_proj, precision=lax.Precision.HIGHEST)
    part_a = jnp.einsum("etr,tk->erk", weighted_b, input_proj, precision=lax.Precision.HIGHEST)
    raw = jnp.concatenate(
        [part_b.reshape(item_number, -1), part_a.reshape(item_number, -1)], axis=1
    )
    raw = raw * lax.rsqrt(jnp.mean(raw * raw, axis=1, keepdims=True) + 1e-06)
    return raw.astype(jnp.bfloat16)


def per_device(
    train_layer_input,
    train_output_gradient,
    train_example_index,
    eval_layer_input,
    eval_output_gradient,
    eval_rollout_index,
    adapter_down,
    adapter_up,
    gradient_projector,
    input_projector,
    paired_eval_index,
    live_slot_count,
):
    grad_piece = lax.all_gather(gradient_projector, "train", axis=0, tiled=True)
    input_piece = lax.all_gather(input_projector, "train", axis=0, tiled=True)

    def partial_product(acts, weights):
        return jnp.dot(acts, weights, preferred_element_type=jnp.float32)

    train_gproj = partial_product(train_output_gradient, grad_piece)
    train_iproj = partial_product(train_layer_input, input_piece)
    eval_gproj = partial_product(eval_output_gradient, grad_piece)
    eval_iproj = partial_product(eval_layer_input, input_piece)
    train_feats = example_features(
        jnp.dot(train_layer_input, adapter_down, preferred_element_type=jnp.float32),
        jnp.dot(train_output_gradient, adapter_up.T, preferred_element_type=jnp.float32),
        train_gproj,
        train_iproj,
        train_example_index[0],
        TRAIN_EXAMPLES,
    )
    eval_feats = example_features(
        jnp.dot(eval_layer_input, adapter_down, preferred_element_type=jnp.float32),
        jnp.dot(eval_output_gradient, adapter_up.T, preferred_element_type=jnp.float32),
        eval_gproj,
        eval_iproj,
        eval_rollout_index[0],
        EVAL_ROLLOUTS,
    )
    factor = 1.0 / K**0.5
    mine = lax.axis_index("train")
    live = (jnp.arange(SLOTS, dtype=jnp.int32) < live_slot_count[mine]).astype(jnp.float32)
    chosen = lax.dynamic_index_in_dim(paired_eval_index, mine, 0, keepdims=False)
    target = chosen[:, None] * EVAL_ROLLOUTS + jnp.arange(EVAL_ROLLOUTS, dtype=jnp.int32)[None, :]
    piece = lax.all_gather(eval_feats, "train", axis=0, tiled=True)
    height = piece.shape[0]
    product = jnp.einsum("ik,rk->ir", train_feats, piece, preferred_element_type=jnp.float32)
    picker = (target[:, :, None] == jnp.arange(height, dtype=jnp.int32)[None, None, :]).astype(
        jnp.float32
    )
    tiles = jnp.einsum("ir,sjr->sij", product, picker, precision=lax.Precision.HIGHEST)
    tiles = tiles[None]
    return tiles * factor * live[None, :, None, None]


def solution(mesh):
    in_specs = (
        P(("parts", "train"), None),
        P(("parts", "train"), None),
        P(("parts", "train"), None),
        P(("parts", "train"), None),
        P(("parts", "train"), None),
        P(("parts", "train"), None),
        P(),
        P(),
        P("train", None),
        P("train", None),
        P("parts", None),
        P("parts"),
    )
    out_specs = P(("parts", "train"), None, None, None)
    return jax.shard_map(
        per_device, mesh=mesh, in_specs=in_specs, out_specs=out_specs, check_vma=False
    )
```

profile of v0, /device:TPU:0, one launch (start us, length us, event | category | flops | bytes accessed | tf_op | source)
XLA Modules:
  0.0 221.0 jit_solution(14490016703583669548)
XLA Ops:
  6.5 0.0 copy-start
  6.5 0.0 copy-start.1
  6.5 0.0 all-gather.6.cloned.1.call-start
  6.5 0.7 all-gather.6.cloned.1.call-update
  7.3 0.0 all-gather.4.cloned.1.call-start
  7.3 0.7 all-gather.4.cloned.1.call-update
  8.0 0.0 all-gather.8.cloned.1.call-start
  8.1 0.7 fusion.20
  8.7 0.0 copy-done
  8.7 1.3 fusion.23
  10.0 1.6 fusion.24
  11.6 57.7 %all-gather.6.cloned.1.call-done = bf16[4096,256]{1,0:T(8,128)(2,1)} async-done(((bf16[128,256]{1,0:T(8,128)(2,1)}), bf16[4096,256]{1,0:T(8,128)(2,1)}) %all-gather.6.cloned.1.call-update) | async-done | bytes 2097168 | tf_op jit(solution)/shard_map/all_gather | solution.py:42
  69.3 2.0 convolution_bitcast_fusion.2
  71.4 0.0 copy-start.9
  71.4 0.0 copy-start.7
  71.4 0.0 copy-start.8
  71.4 0.0 copy-start.6
  71.4 0.4 fusion.11
  71.8 0.2 copy.16
  71.9 55.5 %all-gather.4.cloned.1.call-done = bf16[4096,256]{1,0:T(8,128)(2,1)} async-done(((bf16[128,256]{1,0:T(8,128)(2,1)}), bf16[4096,256]{1,0:T(8,128)(2,1)}) %all-gather.4.cloned.1.call-update) | async-done | bytes 2097168 | tf_op jit(solution)/shard_map/all_gather | solution.py:41
  127.4 0.0 copy-done.1
  127.4 2.0 convolution_bitcast_fusion.3
  129.5 0.4 fusion.13
  129.8 0.2 copy.15
  130.0 0.0 copy-start.4
  130.1 0.2 multiply_reduce_fusion.1
  130.3 0.8 multiply_convert_fusion.2
  131.1 0.0 all-gather.8.cloned.1.call-update
  131.1 0.0 copy-done.9
  131.1 0.0 copy-start.3
  131.1 0.6 dynamic_slice.8
  131.7 0.0 copy-done.7
  131.7 0.2 multiply_reduce_fusion.2
  131.9 1.0 compare_select_fusion
  132.9 0.1 iota_add_fusion
  133.0 0.0 copy-done.8
  133.0 0.0 copy-done.6
  133.0 0.0 copy-start.2
  133.0 3.5 %fusion.21 = f32[512,16]{0,1:T(8,128)S(1)} fusion(bf16[512,4096]{1,0:T(8,128)(2,1)} %param.12, bf16[4096,16]{0,1:T(8,128)(2,1)S(1)} %copy-done.6), kind=kOutput, calls=%fused_computation.43 | convolution fusion | flops 67108864 | bytes 4358144 | tf_op jit(solution)/shard_map/dot_general | solution.py:52
  136.6 0.0 copy-done.3
  136.6 2.1 fusion.22
  138.7 0.0 copy-done.4
  138.7 0.0 copy-done.2
  138.7 0.0 copy-start.5
  138.7 1.3 convolution_bitcast_fusion
  140.0 1.0 fusion.1
  141.0 0.3 copy.14
  141.3 0.0 copy-done.5
  141.3 1.2 convolution_bitcast_fusion.1
  142.6 1.0 fusion.3
  143.6 0.3 copy.13
  144.0 0.2 multiply_reduce_fusion
  144.2 63.3 %all-gather.8.cloned.1.call-done = bf16[512,8192]{1,0:T(8,128)(2,1)} async-done(((bf16[16,8192]{1,0:T(8,128)(2,1)}), bf16[512,8192]{1,0:T(8,128)(2,1)}) %all-gather.8.cloned.1.call-update) | async-done | bytes 8388624 | tf_op jit(solution)/shard_map/all_gather | solution.py:72
  207.5 6.0 %convolution_bitcast_fusion.4 = f32[32,512,1]{1,0,2:T(8,128)S(1)} fusion(bf16[512,8192]{1,0:T(8,128)(2,1)} %all-gather.8.cloned.1.call-done, f32[32,8192]{1,0:T(8,128)S(1)} %constant_dynamic-update-slice_fusion, f32[32]{0:T(128)S(1)} %add_rsqrt_fusion.1), kind=kOutput, calls=%fused_computation.6 | convolution fusion | flops 268959744 | bytes 9502848 | tf_op jit(solution)/shard_map/ik,rk->ir/dot_general | solution.py:74
  213.4 1.1 fusion
  (7 shorter events, 0.1 us)
Async XLA Ops:
  6.5 2.2 copy-start
  6.5 120.9 %copy-start.1 = (bf16[128,4096]{1,0:T(8,128)(2,1)S(1)}, bf16[128,4096]{1,0:T(8,128)(2,1)}, u32[]{:S(2)}) copy-start(bf16[128,4096]{1,0:T(8,128)(2,1)} %param.16) | copy-start | bytes 3145732
  6.5 62.8 %all-gather.6.cloned.1.call-start = ((), (), s32[]{:S(2)}) async-start(), calls=%async_computation.1 | async-start | bytes 2162688 | tf_op jit(solution)/shard_map/all_gather | solution.py:42
  7.3 120.2 %all-gather.4.cloned.1.call-start = ((), (), s32[]{:S(2)}) async-start(), calls=%async_computation | async-start | bytes 2162688 | tf_op jit(solution)/shard_map/all_gather | solution.py:41
  8.0 199.5 %all-gather.8.cloned.1.call-start = ((), (), s32[]{:S(2)}) async-start(), calls=%async_computation.2 | async-start | bytes 8650752 | tf_op jit(solution)/shard_map/all_gather | solution.py:72
  71.4 59.7 %copy-start.9 = (s32[32]{0:T(128)S(1)}, s32[32]{0:T(128)}, u32[]{:S(2)}) copy-start(s32[32]{0:T(128)} %param.23) | copy-start | bytes 388
  71.4 60.3 %copy-start.7 = (s32[32,16]{0,1:T(8,128)S(1)}, s32[32,16]{0,1:T(8,128)}, u32[]{:S(2)}) copy-start(s32[32,16]{0,1:T(8,128)} %param.22) | copy-start | bytes 6148
  71.4 61.6 %copy-start.8 = (s32[1,512]{1,0:T(1,128)S(1)}, s32[1,512]{1,0:T(1,128)}, u32[]{:S(2)}) copy-start(s32[1,512]{1,0:T(1,128)} %param.14) | copy-start | bytes 6148
  71.4 61.6 %copy-start.6 = (bf16[4096,16]{0,1:T(8,128)(2,1)S(1)}, bf16[4096,16]{0,1:T(8,128)(2,1)}, u32[]{:S(2)}) copy-start(bf16[4096,16]{0,1:T(8,128)(2,1)} %param.18) | copy-start | bytes 393220
  130.0 8.6 %copy-start.4 = (bf16[4096,256]{1,0:T(8,128)(2,1)S(1)}, bf16[4096,256]{1,0:T(8,128)(2,1)}, u32[]{:S(2)}) copy-start(bf16[4096,256]{1,0:T(8,128)(2,1)} %all-gather.6.cloned.1.call-done) | copy-start | bytes 6291460
  131.1 5.5 %copy-start.3 = (bf16[512,4096]{1,0:T(8,128)(2,1)S(1)}, bf16[512,4096]{1,0:T(8,128)(2,1)}, u32[]{:S(2)}) copy-start(bf16[512,4096]{1,0:T(8,128)(2,1)} %param.13) | copy-start | bytes 12582916
  133.0 5.6 %copy-start.2 = (bf16[512,4096]{1,0:T(8,128)(2,1)S(1)}, bf16[512,4096]{1,0:T(8,128)(2,1)}, u32[]{:S(2)}) copy-start(bf16[512,4096]{1,0:T(8,128)(2,1)} %param.12) | copy-start | bytes 12582916
  138.7 2.6 %copy-start.5 = (bf16[4096,256]{1,0:T(8,128)(2,1)S(1)}, bf16[4096,256]{1,0:T(8,128)(2,1)}, u32[]{:S(2)}) copy-start(bf16[4096,256]{1,0:T(8,128)(2,1)} %all-gather.4.cloned.1.call-done) | copy-start | bytes 6291460
Sparse Core Ops, SparseCore 0:
  10.2 59.0 all-gather.5
  72.2 55.2 all-gather.3
  131.2 76.1 all-gather.7
where the time goes:
time: 221 us
  waiting for transfers between devices  178 us (81%)
  matrix products  24.9 us (11%)
  between operations  13.4 us (6%)
  other arithmetic  3.17 us (1%)
    all_gather x1, waiting for transfers between devices, per_device(): piece = lax.all_gather(eval_feats, 'train', axis=0, tiled=True)  63.3 us
    all_gather x1, waiting for transfers between devices, per_device(): input_piece = lax.all_gather(input_projector, 'train', axis=0, tiled=True)  57.7 us
    all_gather x1, waiting for transfers between devices, per_device(): grad_piece = lax.all_gather(gradient_projector, 'train', axis=0, tiled=True)  55.5 us
    dot_general x4, matrix products, partial_product(): return jnp.dot(acts, weights, preferred_element_type=jnp.float32)  6.59 us
    dot_general x1, matrix products, per_device(): jnp.einsum('ik,rk->ir', train_feats, piece, preferred_element_type=jnp.fl...  5.96 us
  transfers between devices with their start and end apart: 3, of which 3 were waited for; matrix products, arithmetic and copies ran while one was open for 9% of the time, Pallas kernels for 0%

commit v1 on v0

v1 whole, which is shorter than its diff:
```python
import functools

import jax
import jax.numpy as jnp
from jax import lax
from jax.experimental import pallas as pl
from jax.experimental.pallas import tpu as pltpu
from jax.sharding import PartitionSpec as P

RANK = 16
PW = 256
K = 2 * RANK * PW
TRAIN_EXAMPLES = 32
EVAL_ROLLOUTS = 16
SLOTS = 16
EPS = 1e-06

VMEM = pl.BlockSpec(memory_space=pltpu.VMEM)
SMEM = pl.BlockSpec(memory_space=pltpu.SMEM)
ANY = pl.BlockSpec(memory_space=pl.ANY)
BF16 = jnp.bfloat16
F32 = jnp.float32
NT = (((1,), (1,)), ((), ()))
PARAMS = pltpu.CompilerParams(vmem_limit_bytes=56 * 1024 * 1024)


def xor_permute(block, mask, n):
    return lax.ppermute(block, "train", [(i, i ^ mask) for i in range(n)])


def gather_blocks(block, n):
    if n != 32:
        whole = lax.all_gather(block, "train", axis=0, tiled=True)
        return [(whole, list(range(n)))], False
    ways = [(0, (2, 4)), (8, (4, 2)), (16, (2, 4)), (24, (4, 2))]
    rows = [block] + [xor_permute(block, mask, n) for mask, _ in ways[1:]]
    pieces = []
    for own, (start, order) in zip(rows, ways):
        held, masks = own, [start]
        for mask in order:
            held = jnp.concatenate([held, xor_permute(held, mask, n)], axis=0)
            masks = masks + [m ^ mask for m in masks]
        pieces.append((held, masks))
    pieces += [(xor_permute(held, 1, n), [m ^ 1 for m in masks]) for held, masks in pieces]
    return pieces, True


def split(value):
    high = value.astype(BF16)
    return high, (value - high.astype(F32)).astype(BF16)


def dot3(left, right):
    lh, ll = split(left)
    rh, rl = split(right)
    dot = functools.partial(jnp.dot, preferred_element_type=F32)
    return dot(lh, rh) + (dot(lh, rl) + dot(ll, rh))


def one_hot(index_row, count):
    steps = lax.broadcasted_iota(jnp.int32, (count, index_row.shape[1]), 0)
    return (index_row == steps).astype(F32)


def weighted(rows, picked):
    ranks, tokens = rows.shape
    return (rows[:, None, :] * picked[None, :, :]).reshape(ranks * picked.shape[0], tokens)


def fetch(masks_of, refs, base, held, sem):
    copies = []
    for ref, masks in zip(refs, masks_of):
        for s, mask in enumerate(masks):
            copies.append(pltpu.make_async_copy(ref.at[s], held.at[base ^ mask], sem))
    for copy in copies:
        copy.start()
    pltpu.make_async_copy(held, held, sem).wait()


def squares(raw, items):
    each = jnp.sum(raw * raw, axis=1, keepdims=True)
    return jnp.sum(each.reshape(RANK, items, 1), axis=0)


def eval_kernel(masks_of, base_ref, x_ref, g_ref, hidden_ref, back_ref, index_ref, *rest):
    refs, (pack_ref, table_ref, held, sem) = rest[: len(masks_of)], rest[len(masks_of) :]
    fetch(masks_of, refs, base_ref[0], held, sem)
    count, height, _ = held.shape
    part = (height - 8) // 2
    width = count * part
    grad = jnp.dot(g_ref[...], held[:, 0:part, :].reshape(width, PW), preferred_element_type=F32)
    inp = jnp.dot(x_ref[...], held[:, part : 2 * part, :].reshape(width, PW), preferred_element_type=F32)
    picked = one_hot(index_ref[...], EVAL_ROLLOUTS)
    hidden, back = hidden_ref[...], back_ref[...]
    total = squares(dot3(weighted(hidden, picked), grad), EVAL_ROLLOUTS)
    total = total + squares(dot3(weighted(back, picked), inp), EVAL_ROLLOUTS)
    scale = lax.rsqrt(total * (1.0 / K) + EPS)
    per_token = jnp.sum(picked * scale, axis=0, keepdims=True)
    tokens = x_ref.shape[0]
    pack_ref[0, 0:tokens, :] = grad.astype(BF16)
    pack_ref[0, tokens : 2 * tokens, :] = inp.astype(BF16)
    pack_ref[0, 2 * tokens : 2 * tokens + RANK, 0:tokens] = (hidden * per_token).astype(BF16)
    pack_ref[0, 2 * tokens : 2 * tokens + RANK, tokens : 2 * tokens] = (back * per_token).astype(BF16)
    table_ref[...] = held[:, 2 * part : 2 * part + 8, 0:tokens].astype(F32)


def train_kernel(masks_of, base_ref, x_ref, g_ref, hidden_ref, back_ref, index_ref, *rest):
    refs, (feats_ref, held, sem) = rest[: len(masks_of)], rest[len(masks_of) :]
    fetch(masks_of, refs, base_ref[0], held, sem)
    count, height, _ = held.shape
    part = (height - 8) // 2
    width = count * part
    picked = one_hot(index_ref[...], TRAIN_EXAMPLES)
    grad = jnp.dot(g_ref[...], held[:, 0:part, :].reshape(width, PW), preferred_element_type=F32)
    raw_a = dot3(weighted(hidden_ref[...], picked), grad)
    inp = jnp.dot(x_ref[...], held[:, part : 2 * part, :].reshape(width, PW), preferred_element_type=F32)
    raw_b = dot3(weighted(back_ref[...], picked), inp)
    total = squares(raw_a, TRAIN_EXAMPLES) + squares(raw_b, TRAIN_EXAMPLES)
    scale = lax.rsqrt(total * (1.0 / K) + EPS)[None]
    shape = (RANK, TRAIN_EXAMPLES, PW)
    feats_ref[0] = (raw_a.reshape(shape) * scale).reshape(RANK * TRAIN_EXAMPLES, PW).astype(BF16)
    feats_ref[1] = (raw_b.reshape(shape) * scale).reshape(RANK * TRAIN_EXAMPLES, PW).astype(BF16)


def score_kernel(masks_of, base_ref, chosen_ref, live_ref, feats_ref, table_ref, *rest):
    refs, (out_ref, held, sem) = rest[: len(masks_of)], rest[len(masks_of) :]
    base = base_ref[0]
    for slot in range(SLOTS):
        mask = chosen_ref[slot] ^ base
        for ref, masks in zip(refs, masks_of):
            for s, own in enumerate(masks):

                @pl.when(mask == own)
                def _():
                    pltpu.make_async_copy(ref.at[s], held.at[slot], sem).start()

    pltpu.make_async_copy(held, held, sem).wait()
    tokens = (held.shape[1] - RANK) // 2
    shape = (RANK, TRAIN_EXAMPLES, 2 * tokens)
    dot = functools.partial(lax.dot_general, dimension_numbers=NT, preferred_element_type=F32)
    for pair in range(0, SLOTS, 2):
        two = slice(pair, pair + 2)
        grad = held[two, 0:tokens, :].reshape(2 * tokens, PW)
        inp = held[two, tokens : 2 * tokens, :].reshape(2 * tokens, PW)
        coef = held[two, 2 * tokens : 2 * tokens + RANK, :].astype(F32)
        hidden = jnp.concatenate([coef[0, :, 0:tokens], coef[1, :, 0:tokens]], axis=1)
        back = jnp.concatenate([coef[0, :, tokens:], coef[1, :, tokens:]], axis=1)
        mixed = jnp.sum(dot(feats_ref[0], grad).reshape(shape) * hidden[:, None, :], axis=0)
        mixed = mixed + jnp.sum(dot(feats_ref[1], inp).reshape(shape) * back[:, None, :], axis=0)
        high, low = split(mixed)
        for k in range(2):
            slot = pair + k
            index_row = table_ref[chosen_ref[slot], 0:1, :].astype(jnp.int32)
            picked = one_hot(index_row, EVAL_ROLLOUTS).astype(BF16)
            lanes = slice(k * tokens, (k + 1) * tokens)
            tile = dot(high[:, lanes], picked) + dot(low[:, lanes], picked)
            factor = jnp.where(slot < live_ref[0], 1.0 / K**0.5, 0.0)
            out_ref[0, slot] = tile * factor


def per_device(
    n,
    train_layer_input,
    train_output_gradient,
    train_example_index,
    eval_layer_input,
    eval_output_gradient,
    eval_rollout_index,
    adapter_down,
    adapter_up,
    gradient_projector,
    input_projector,
    paired_eval_index,
    live_slot_count,
):
    mine = lax.axis_index("train")
    tokens = eval_layer_input.shape[0]
    index_rows = jnp.pad(eval_rollout_index.astype(BF16), ((0, 7), (0, PW - tokens)))
    block = jnp.concatenate([gradient_projector, input_projector, index_rows], axis=0)[None]
    pieces, relative = gather_blocks(block, n)
    base = jnp.where(relative, mine, 0).astype(jnp.int32).reshape(1)
    arrays = [array for array, _ in pieces]
    masks_of = [masks for _, masks in pieces]

    def down(x):
        return lax.dot_general(adapter_down, x, (((0,), (1,)), ((), ())), preferred_element_type=F32)

    def up(g):
        return lax.dot_general(adapter_up, g, NT, preferred_element_type=F32)

    held = [pltpu.VMEM((n,) + block.shape[1:], BF16), pltpu.SemaphoreType.DMA]
    pack, table = pl.pallas_call(
        functools.partial(eval_kernel, masks_of),
        out_shape=[
            jax.ShapeDtypeStruct((1, 2 * tokens + RANK, PW), BF16),
            jax.ShapeDtypeStruct((n, 8, tokens), F32),
        ],
        in_specs=[SMEM] + [VMEM] * 5 + [ANY] * len(arrays),
        out_specs=[VMEM] * 2,
        scratch_shapes=held,
        compiler_params=PARAMS,
        cost_estimate=pl.CostEstimate(flops=10**9, bytes_accessed=7 * 2**20, transcendentals=0),
        name="eval_factors",
    )(
        base,
        eval_layer_input,
        eval_output_gradient,
        down(eval_layer_input),
        up(eval_output_gradient),
        eval_rollout_index,
        *arrays,
    )
    eval_pieces, _ = gather_blocks(pack, n)
    feats = pl.pallas_call(
        functools.partial(train_kernel, masks_of),
        out_shape=jax.ShapeDtypeStruct((2, RANK * TRAIN_EXAMPLES, PW), BF16),
        in_specs=[SMEM] + [VMEM] * 5 + [ANY] * len(arrays),
        out_specs=VMEM,
        scratch_shapes=held,
        compiler_params=PARAMS,
        cost_estimate=pl.CostEstimate(flops=4 * 10**9, bytes_accessed=12 * 2**20, transcendentals=0),
        name="train_features",
    )(
        base,
        train_layer_input,
        train_output_gradient,
        down(train_layer_input),
        up(train_output_gradient),
        train_example_index,
        *arrays,
    )
    chosen = lax.dynamic_index_in_dim(paired_eval_index, mine, 0, keepdims=False)
    live = lax.dynamic_index_in_dim(live_slot_count, mine, 0, keepdims=True)
    eval_arrays = [array for array, _ in eval_pieces]
    return pl.pallas_call(
        functools.partial(score_kernel, masks_of),
        out_shape=jax.ShapeDtypeStruct((1, SLOTS, TRAIN_EXAMPLES, EVAL_ROLLOUTS), F32),
        in_specs=[SMEM] * 3 + [VMEM] * 2 + [ANY] * len(eval_arrays),
        out_specs=VMEM,
        scratch_shapes=[pltpu.VMEM((SLOTS,) + pack.shape[1:], BF16), pltpu.SemaphoreType.DMA],
        compiler_params=PARAMS,
        cost_estimate=pl.CostEstimate(flops=2 * 10**9, bytes_accessed=3 * 2**20, transcendentals=0),
        name="score_tiles",
    )(base, chosen, live, feats, table, *eval_arrays)


def solution(mesh):
    in_specs = (
        P(("parts", "train"), None),
        P(("parts", "train"), None),
        P(("parts", "train"), None),
        P(("parts", "train"), None),
        P(("parts", "train"), None),
        P(("parts", "train"), None),
        P(),
        P(),
        P("train", None),
        P("train", None),
        P("parts", None),
        P("parts"),
    )
    out_specs = P(("parts", "train"), None, None, None)
    return jax.shard_map(
        functools.partial(per_device, mesh.shape["train"]),
        mesh=mesh,
        in_specs=in_specs,
        out_specs=out_specs,
        check_vma=False,
    )
```

time: 221 us -> 108 us (0.49)
  waiting for transfers between devices: 178 us -> 32.9 us
  starting transfers between devices: 0.08 us -> 32.2 us
  Pallas kernels: 0 us -> 25.8 us
  matrix products: 24.9 us -> 5.57 us
  between operations: 13.4 us -> 0.44 us
  local copies, waits for them, and re-layouts: 1.69 us -> 8.84 us
    all_gather x3 -> x0, waiting for transfers between devices: 176 us -> none  [the longest x1 63.3 us: per_device(): piece = lax.all_gather(eval_feats, 'train', axis=0, tiled=True)]
    ppermute x0 -> x30, waiting for transfers between devices: none -> 32.9 us  [xor_permute(): return lax.ppermute(block, 'train', [(i, i ^ mask) for i in range(n)])]
    ppermute x0 -> x30, starting transfers between devices: none -> 32.2 us  [xor_permute(): return lax.ppermute(block, 'train', [(i, i ^ mask) for i in range(n)])]
    pallas_call x0 -> x3, Pallas kernels: none -> 25.8 us  [the longest x1 12.9 us: per_device(): pl.pallas_call(functools.partial(train_kernel, masks_of), out_shape=jax.S...]
    dot_general x14 -> x4, matrix products: 24.9 us -> 5.57 us  [the longest x2 2.79 us: up(): return lax.dot_general(adapter_up, g, NT, preferred_element_type=F32)]
    unnamed x26 -> x52, local copies, waits for them, and re-layouts: 1.04 us -> 4.17 us
  transfers between devices with their start and end apart: 3 -> 30, of which waited for: 3 -> 9; matrix products, arithmetic and copies ran while one was open for 9% -> 11% of each run, Pallas kernels for 0% -> 12%
where the time goes in v1:
time: 108 us
  waiting for transfers between devices  32.9 us (30%)
  starting transfers between devices  32.2 us (30%)
  Pallas kernels  25.8 us (24%)
  local copies, waits for them, and re-layouts  8.84 us (8%)
  matrix products  5.57 us (5%)
  other arithmetic  1.97 us (2%)
    ppermute x30, waiting for transfers between devices, xor_permute(): return lax.ppermute(block, 'train', [(i, i ^ mask) for i in range(n)])  32.9 us
    ppermute x30, starting transfers between devices, xor_permute(): return lax.ppermute(block, 'train', [(i, i ^ mask) for i in range(n)])  32.2 us
    pallas_call x1, Pallas kernels, per_device(): pl.pallas_call(functools.partial(train_kernel, masks_of), out_shape=jax.S...  12.9 us
    pallas_call x1, Pallas kernels, per_device(): pl.pallas_call(functools.partial(score_kernel, masks_of), out_shape=jax.S...  7.16 us
    pallas_call x1, Pallas kernels, per_device(): pl.pallas_call(functools.partial(eval_kernel, masks_of), out_shape=[jax.S...  5.68 us
    unnamed x52, local copies, waits for them, and re-layouts  4.17 us
    dot_general x2, matrix products, up(): return lax.dot_general(adapter_up, g, NT, preferred_element_type=F32)  2.79 us
    dot_general x2, matrix products, down(): lax.dot_general(adapter_down, x, (((0,), (1,)), ((), ())), preferred_elem...  2.78 us
  transfers between devices with their start and end apart: 30, of which 9 were waited for; matrix products, arithmetic and copies ran while one was open for 11% of the time, Pallas kernels for 12%

profile of v1, /device:TPU:0, one launch (start us, length us, event | category | flops | bytes accessed | tf_op | source)
XLA Modules:
  0.0 107.8 jit_solution(9918318702621899957)
XLA Ops:
  0.0 0.8 convert_element_type.5
  0.8 0.9 fusion.2
  1.7 3.0 %collective-permute-start = (bf16[1,264,256]{2,1,0:T(8,128)(2,1)S(1)}, bf16[1,264,256]{2,1,0:T(8,128)(2,1)S(1)}, u32[]{:S(2)}, u32[]{:S(2)}) collective-permute-start(bf16[1,264,256]{2,1,0:T(8,128)(2,1)S(1)} %fusion.2), channel_id=1, source_target_pairs={{0,2},{1,3},{2,0},{3,1},{4,6},{5,7},{6,4},{7,5},{8,10},{9,11},{10,... | collective-permute-start | bytes 405512 | tf_op jit(solution)/shard_map/ppermute | solution.py:28
  4.7 3.6 %collective-permute-start.8 = (bf16[1,264,256]{2,1,0:T(8,128)(2,1)S(1)}, bf16[1,264,256]{2,1,0:T(8,128)(2,1)S(1)}, u32[]{:S(2)}, u32[]{:S(2)}) collective-permute-start(bf16[1,264,256]{2,1,0:T(8,128)(2,1)S(1)} %fusion.2), channel_id=1, source_target_pairs={{0,24},{1,25},{2,26},{3,27},{4,28},{5,29},{6,30},{7,31},{8,16},{9,... | collective-permute-start | bytes 405512 | tf_op jit(solution)/shard_map/ppermute | solution.py:28
  8.3 0.8 collective-permute-start.2
  9.1 1.6 %collective-permute-start.1 = (bf16[2,264,256]{2,1,0:T(8,128)(2,1)S(1)}, bf16[2,264,256]{2,1,0:T(8,128)(2,1)S(1)}, u32[]{:S(2)}, u32[]{:S(2)}) collective-permute-start(bf16[2,264,256]{2,1,0:T(8,128)(2,1)S(1)} %pad_maximum_fusion.5), channel_id=1, source_target_pairs={{0,4},{1,5},{2,6},{3,7},{4,0},{5,1},{6,2},{7,3},{8,12},{9,13},{10,... | collective-permute-start | bytes 811016 | tf_op jit(solution)/shard_map/ppermute | solution.py:28
  10.7 2.4 %collective-permute-done.8 = bf16[1,264,256]{2,1,0:T(8,128)(2,1)S(1)} collective-permute-done((bf16[1,264,256]{2,1,0:T(8,128)(2,1)S(1)}, bf16[1,264,256]{2,1,0:T(8,128)(2,1)S(1)}, u32[]{:S(2)}, u32[]{:S(2)}) %collective-permute-start.8) | collective-permute-done | bytes 135200 | tf_op jit(solution)/shard_map/ppermute | solution.py:28
  13.1 1.5 %collective-permute-start.9 = (bf16[1,264,256]{2,1,0:T(8,128)(2,1)S(1)}, bf16[1,264,256]{2,1,0:T(8,128)(2,1)S(1)}, u32[]{:S(2)}, u32[]{:S(2)}) collective-permute-start(bf16[1,264,256]{2,1,0:T(8,128)(2,1)S(1)} %collective-permute-done.8), channel_id=1, source_target_pairs={{0,4},{1,5},{2,6},{3,7},{4,0},{5,1},{6,2},{7,3},{8,12},{9,13},{10,... | collective-permute-start | bytes 405512 | tf_op jit(solution)/shard_map/ppermute | solution.py:28
  14.6 4.9 %collective-permute-done.5 = bf16[1,264,256]{2,1,0:T(8,128)(2,1)S(1)} collective-permute-done((bf16[1,264,256]{2,1,0:T(8,128)(2,1)S(1)}, bf16[1,264,256]{2,1,0:T(8,128)(2,1)S(1)}, u32[]{:S(2)}, u32[]{:S(2)}) %collective-permute-start.5) | collective-permute-done | bytes 135200 | tf_op jit(solution)/shard_map/ppermute | solution.py:28
  19.5 0.5 collective-permute-start.6
  20.0 0.7 constant_dynamic-update-slice_fusion.5
  20.7 0.0 collective-permute-done.2
  20.7 1.5 %collective-permute-start.3 = (bf16[1,264,256]{2,1,0:T(8,128)(2,1)S(1)}, bf16[1,264,256]{2,1,0:T(8,128)(2,1)S(1)}, u32[]{:S(2)}, u32[]{:S(2)}) collective-permute-start(bf16[1,264,256]{2,1,0:T(8,128)(2,1)S(1)} %collective-permute-done.2), channel_id=1, source_target_pairs={{0,4},{1,5},{2,6},{3,7},{4,0},{5,1},{6,2},{7,3},{8,12},{9,13},{10,... | collective-permute-start | bytes 405512 | tf_op jit(solution)/shard_map/ppermute | solution.py:28
  22.2 0.7 constant_dynamic-update-slice_fusion.2
  22.9 1.6 %collective-permute-start.10 = (bf16[2,264,256]{2,1,0:T(8,128)(2,1)S(1)}, bf16[2,264,256]{2,1,0:T(8,128)(2,1)S(1)}, u32[]{:S(2)}, u32[]{:S(2)}) collective-permute-start(bf16[2,264,256]{2,1,0:T(8,128)(2,1)S(1)} %pad_maximum_fusion.8), channel_id=1, source_target_pairs={{0,2},{1,3},{2,0},{3,1},{4,6},{5,7},{6,4},{7,5},{8,10},{9,11},{10,... | collective-permute-start | bytes 811016 | tf_op jit(solution)/shard_map/ppermute | solution.py:28
  24.4 0.4 collective-permute-done.6
  24.9 2.6 %collective-permute-start.7 = (bf16[2,264,256]{2,1,0:T(8,128)(2,1)S(1)}, bf16[2,264,256]{2,1,0:T(8,128)(2,1)S(1)}, u32[]{:S(2)}, u32[]{:S(2)}) collective-permute-start(bf16[2,264,256]{2,1,0:T(8,128)(2,1)S(1)} %pad_maximum_fusion.7), channel_id=1, source_target_pairs={{0,4},{1,5},{2,6},{3,7},{4,0},{5,1},{6,2},{7,3},{8,12},{9,13},{10,... | collective-permute-start | bytes 811016 | tf_op jit(solution)/shard_map/ppermute | solution.py:28
  27.5 0.0 collective-permute-done.3
  27.5 1.0 collective-permute-start.4
  28.5 0.7 constant_dynamic-update-slice_fusion.4
  29.2 0.7 constant_dynamic-update-slice_fusion.1
  29.9 0.0 collective-permute-done.1
  29.9 0.1 pad_maximum_fusion.rest_0_
  29.9 0.1 collective-permute-start.11
  30.0 6.1 %collective-permute-done.4 = bf16[2,264,256]{2,1,0:T(8,128)(2,1)S(1)} collective-permute-done((bf16[2,264,256]{2,1,0:T(8,128)(2,1)S(1)}, bf16[2,264,256]{2,1,0:T(8,128)(2,1)S(1)}, u32[]{:S(2)}, u32[]{:S(2)}) %collective-permute-start.4) | collective-permute-done | bytes 270368 | tf_op jit(solution)/shard_map/ppermute | solution.py:28
  36.1 0.7 constant_dynamic-update-slice_fusion.rest_1_
  36.8 0.0 collective-permute-start.12
  36.8 0.7 constant_dynamic-update-slice_fusion.3.rest_2_
  37.5 0.5 collective-permute-start.13
  38.1 0.1 collective-permute-start.14
  38.2 0.0 copy-start.1
  38.2 1.0 fusion.5.hidden_ref
  39.2 1.0 fusion.6.back_ref
  40.2 0.3 collective-permute-done.14.rest_7_
  40.5 5.7 %eval_factors.1 = (bf16[1,272,256]{2,1,0:T(8,128)(2,1)}, f32[32,8,128]{2,1,0:T(8,128)}) custom-call(s32[1]{0:T(128)} %bitcast.base_ref, bf16[128,4096]{1,0:T(8,128)(2,1)} %x_ref.3, bf16[128,4096]{1,0:T(8,128)(2,1)} %g_ref.3, f32[16,128]{1,0:T(8,128)} %fusion.5.hidden_ref, f32[16,128]{1,0:T(8,128)} %fusion.6.back_ref, s32[1,128]{1,0:T(1,128)} %index_ref.3, ...), custom_call_target="tpu_custom_call" | custom-call | flops 1000000000 | bytes 7340032 | tf_op jit(solution)/shard_map/eval_factors/pallas_call | solution.py:192
  46.2 1.2 %collective-permute-start.15 = (bf16[1,272,256]{2,1,0:T(8,128)(2,1)}, bf16[1,272,256]{2,1,0:T(8,128)(2,1)S(1)}, u32[]{:S(2)}, u32[]{:S(2)}) collective-permute-start(bf16[1,272,256]{2,1,0:T(8,128)(2,1)} %get-tuple-element.8), channel_id=1, source_target_pairs={{0,2},{1,3},{2,0},{3,1},{4,6},{5,7},{6,4},{7,5},{8,10},{9,11},{10,... | collective-permute-start | bytes 417800 | tf_op jit(solution)/shard_map/ppermute | solution.py:28
  47.4 1.8 %fusion.3.hidden_ref = f32[16,512]{1,0:T(8,128)} fusion(bf16[4096,16]{0,1:T(8,128)(2,1)S(1)} %copy-done, bf16[512,4096]{1,0:T(8,128)(2,1)S(1)} %copy-done.1), kind=kOutput, calls=%fused_computation.35 | convolution fusion | flops 67108864 | bytes 4358144 | tf_op jit(solution)/shard_map/dot_general | solution.py:186
  49.2 0.7 dynamic_slice.9.live_ref
  49.9 0.7 dynamic-slice_reduce_fusion.chosen_ref
  50.6 1.9 %collective-permute-start.23 = (bf16[1,272,256]{2,1,0:T(8,128)(2,1)S(1)}, bf16[1,272,256]{2,1,0:T(8,128)(2,1)S(1)}, u32[]{:S(2)}, u32[]{:S(2)}) collective-permute-start(bf16[1,272,256]{2,1,0:T(8,128)(2,1)S(1)} %copy-done.7), channel_id=1, source_target_pairs={{0,24},{1,25},{2,26},{3,27},{4,28},{5,29},{6,30},{7,31},{8,16},{9,... | collective-permute-start | bytes 417800 | tf_op jit(solution)/shard_map/ppermute | solution.py:28
  52.5 2.5 %collective-permute-start.17 = (bf16[1,272,256]{2,1,0:T(8,128)(2,1)S(1)}, bf16[1,272,256]{2,1,0:T(8,128)(2,1)S(1)}, u32[]{:S(2)}, u32[]{:S(2)}) collective-permute-start(bf16[1,272,256]{2,1,0:T(8,128)(2,1)S(1)} %copy-done.7), channel_id=1, source_target_pairs={{0,8},{1,9},{2,10},{3,11},{4,12},{5,13},{6,14},{7,15},{8,0},{9,1},... | collective-permute-start | bytes 417800 | tf_op jit(solution)/shard_map/ppermute | solution.py:28
  55.0 1.0 collective-permute-start.16
  56.1 3.0 %collective-permute-done.23 = bf16[1,272,256]{2,1,0:T(8,128)(2,1)S(1)} collective-permute-done((bf16[1,272,256]{2,1,0:T(8,128)(2,1)S(1)}, bf16[1,272,256]{2,1,0:T(8,128)(2,1)S(1)}, u32[]{:S(2)}, u32[]{:S(2)}) %collective-permute-start.23) | collective-permute-done | bytes 139296 | tf_op jit(solution)/shard_map/ppermute | solution.py:28
  59.1 0.9 collective-permute-start.24
  60.0 4.4 %collective-permute-done.20 = bf16[1,272,256]{2,1,0:T(8,128)(2,1)S(1)} collective-permute-done((bf16[1,272,256]{2,1,0:T(8,128)(2,1)S(1)}, bf16[1,272,256]{2,1,0:T(8,128)(2,1)S(1)}, u32[]{:S(2)}, u32[]{:S(2)}) %collective-permute-start.20) | collective-permute-done | bytes 139296 | tf_op jit(solution)/shard_map/ppermute | solution.py:28
  64.5 1.3 %collective-permute-start.21 = (bf16[1,272,256]{2,1,0:T(8,128)(2,1)S(1)}, bf16[1,272,256]{2,1,0:T(8,128)(2,1)S(1)}, u32[]{:S(2)}, u32[]{:S(2)}) collective-permute-start(bf16[1,272,256]{2,1,0:T(8,128)(2,1)S(1)} %collective-permute-done.20), channel_id=1, source_target_pairs={{0,2},{1,3},{2,0},{3,1},{4,6},{5,7},{6,4},{7,5},{8,10},{9,11},{10,... | collective-permute-start | bytes 417800 | tf_op jit(solution)/shard_map/ppermute | solution.py:28
  65.8 0.8 collective-permute-start.18
  66.7 1.2 %collective-permute-start.25 = (bf16[2,272,256]{2,1,0:T(8,128)(2,1)S(1)}, bf16[2,272,256]{2,1,0:T(8,128)(2,1)S(1)}, u32[]{:S(2)}, u32[]{:S(2)}) collective-permute-start(bf16[2,272,256]{2,1,0:T(8,128)(2,1)S(1)} %pad_maximum_fusion.4), channel_id=1, source_target_pairs={{0,2},{1,3},{2,0},{3,1},{4,6},{5,7},{6,4},{7,5},{8,10},{9,11},{10,... | collective-permute-start | bytes 835592 | tf_op jit(solution)/shard_map/ppermute | solution.py:28
  67.9 3.0 %collective-permute-done.21 = bf16[1,272,256]{2,1,0:T(8,128)(2,1)S(1)} collective-permute-done((bf16[1,272,256]{2,1,0:T(8,128)(2,1)S(1)}, bf16[1,272,256]{2,1,0:T(8,128)(2,1)S(1)}, u32[]{:S(2)}, u32[]{:S(2)}) %collective-permute-start.21) | collective-permute-done | bytes 139296 | tf_op jit(solution)/shard_map/ppermute | solution.py:28
  71.0 1.3 %collective-permute-start.22 = (bf16[2,272,256]{2,1,0:T(8,128)(2,1)S(1)}, bf16[2,272,256]{2,1,0:T(8,128)(2,1)S(1)}, u32[]{:S(2)}, u32[]{:S(2)}) collective-permute-start(bf16[2,272,256]{2,1,0:T(8,128)(2,1)S(1)} %pad_maximum_fusion.3), channel_id=1, source_target_pairs={{0,4},{1,5},{2,6},{3,7},{4,0},{5,1},{6,2},{7,3},{8,12},{9,13},{10,... | collective-permute-start | bytes 835592 | tf_op jit(solution)/shard_map/ppermute | solution.py:28
  72.3 1.0 collective-permute-start.19
  73.4 0.1 collective-permute-start.26
  73.4 8.4 %collective-permute-done.19 = bf16[2,272,256]{2,1,0:T(8,128)(2,1)S(1)} collective-permute-done((bf16[2,272,256]{2,1,0:T(8,128)(2,1)S(1)}, bf16[2,272,256]{2,1,0:T(8,128)(2,1)S(1)}, u32[]{:S(2)}, u32[]{:S(2)}) %collective-permute-start.19) | collective-permute-done | bytes 278560 | tf_op jit(solution)/shard_map/ppermute | solution.py:28
  81.8 0.1 collective-permute-start.27
  82.0 0.5 collective-permute-start.28
  82.6 0.1 collective-permute-start.29
  82.6 1.8 %fusion.4.back_ref = f32[16,512]{1,0:T(8,128)} fusion(bf16[16,4096]{1,0:T(8,128)(2,1)S(1)} %copy-done.8, bf16[512,4096]{1,0:T(8,128)(2,1)S(1)} %copy-done.2), kind=kOutput, calls=%fused_computation.36 | convolution fusion | flops 67108864 | bytes 4358144 | tf_op jit(solution)/shard_map/dot_general | solution.py:189
  84.5 12.9 %train_features.1.feats_ref = bf16[2,512,256]{2,1,0:T(8,128)(2,1)} custom-call(s32[1]{0:T(128)} %bitcast.base_ref, bf16[512,4096]{1,0:T(8,128)(2,1)} %x_ref.2, bf16[512,4096]{1,0:T(8,128)(2,1)} %g_ref.2, f32[16,512]{1,0:T(8,128)} %fusion.3.hidden_ref, f32[16,512]{1,0:T(8,128)} %fusion.4.back_ref, s32[1,512]{1,0:T(1,128)} %index_ref.2, ...), custom_call_target="tpu_custom_call" | custom-call | flops 4000000000 | bytes 12582912 | tf_op jit(solution)/shard_map/train_features/pallas_call | solution.py:214
  97.5 0.7 copy-done.14
  98.2 0.2 copy-done.15
  98.4 0.2 copy-done.16
  98.6 0.2 copy-done.17
  98.8 7.2 %score_tiles.1 = f32[1,16,32,16]{3,2,1,0:T(8,128)} custom-call(s32[1]{0:T(128)} %bitcast.base_ref, s32[16]{0:T(128)} %dynamic-slice_reduce_fusion.chosen_ref, s32[1]{0:T(128)} %dynamic_slice.9.live_ref, bf16[2,512,256]{2,1,0:T(8,128)(2,1)} %train_features.1.feats_ref, f32[32,8,128]{2,1,0:T(8,128)} %get-tuple-element.7.table_ref, ...), custom_call_target="tpu_custom_call" | custom-call | flops 2000000000 | bytes 3145728 | tf_op jit(solution)/shard_map/score_tiles/pallas_call | solution.py:235
  106.0 1.7 %copy.14 = f32[1,16,32,16]{2,3,1,0:T(8,128)} copy(f32[1,16,32,16]{3,2,1,0:T(8,128)} %score_tiles.1) | data formatting | bytes 65536 | tf_op jit(solution)/shard_map/score_tiles/pallas_call | solution.py:235
  (76 shorter events, 0.5 us)
Async XLA Ops:
  0.0 38.2 %copy-start = (bf16[4096,16]{0,1:T(8,128)(2,1)S(1)}, bf16[4096,16]{0,1:T(8,128)(2,1)}, u32[]{:S(2)}) copy-start(bf16[4096,16]{0,1:T(8,128)(2,1)} %param.18) | copy-start | bytes 393220
  0.0 38.2 %copy-start.3 = (bf16[128,4096]{1,0:T(8,128)(2,1)S(1)}, bf16[128,4096]{1,0:T(8,128)(2,1)}, u32[]{:S(2)}) copy-start(bf16[128,4096]{1,0:T(8,128)(2,1)} %x_ref.3) | copy-start | bytes 3145732
  0.0 39.2 %copy-start.8 = (bf16[16,4096]{1,0:T(8,128)(2,1)S(1)}, bf16[16,4096]{1,0:T(8,128)(2,1)}, u32[]{:S(2)}) copy-start(bf16[16,4096]{1,0:T(8,128)(2,1)} %param.19) | copy-start | bytes 393220
  0.0 39.2 %copy-start.4 = (bf16[128,4096]{1,0:T(8,128)(2,1)S(1)}, bf16[128,4096]{1,0:T(8,128)(2,1)}, u32[]{:S(2)}) copy-start(bf16[128,4096]{1,0:T(8,128)(2,1)} %g_ref.3) | copy-start | bytes 3145732
  1.7 7.4 %collective-permute-start = (bf16[1,264,256]{2,1,0:T(8,128)(2,1)S(1)}, bf16[1,264,256]{2,1,0:T(8,128)(2,1)S(1)}, u32[]{:S(2)}, u32[]{:S(2)}) collective-permute-start(bf16[1,264,256]{2,1,0:T(8,128)(2,1)S(1)} %fusion.2), channel_id=1, source_target_pairs={{0,2},{1,3},{2,0},{3,1},{4,6},{5,7},{6,4},{7,5},{8,10},{9,11},{10,... | collective-permute-start | bytes 405512 | tf_op jit(solution)/shard_map/ppermute | solution.py:28
  4.7 8.4 %collective-permute-start.8 = (bf16[1,264,256]{2,1,0:T(8,128)(2,1)S(1)}, bf16[1,264,256]{2,1,0:T(8,128)(2,1)S(1)}, u32[]{:S(2)}, u32[]{:S(2)}) collective-permute-start(bf16[1,264,256]{2,1,0:T(8,128)(2,1)S(1)} %fusion.2), channel_id=1, source_target_pairs={{0,24},{1,25},{2,26},{3,27},{4,28},{5,29},{6,30},{7,31},{8,16},{9,... | collective-permute-start | bytes 405512 | tf_op jit(solution)/shard_map/ppermute | solution.py:28
  8.3 11.1 %collective-permute-start.5 = (bf16[1,264,256]{2,1,0:T(8,128)(2,1)S(1)}, bf16[1,264,256]{2,1,0:T(8,128)(2,1)S(1)}, u32[]{:S(2)}, u32[]{:S(2)}) collective-permute-start(bf16[1,264,256]{2,1,0:T(8,128)(2,1)S(1)} %fusion.2), channel_id=1, source_target_pairs={{0,16},{1,17},{2,18},{3,19},{4,20},{5,21},{6,22},{7,23},{8,24},{9,... | collective-permute-start | bytes 405512 | tf_op jit(solution)/shard_map/ppermute | solution.py:28
  8.3 12.3 %collective-permute-start.2 = (bf16[1,264,256]{2,1,0:T(8,128)(2,1)S(1)}, bf16[1,264,256]{2,1,0:T(8,128)(2,1)S(1)}, u32[]{:S(2)}, u32[]{:S(2)}) collective-permute-start(bf16[1,264,256]{2,1,0:T(8,128)(2,1)S(1)} %fusion.2), channel_id=1, source_target_pairs={{0,8},{1,9},{2,10},{3,11},{4,12},{5,13},{6,14},{7,15},{8,0},{9,1},... | collective-permute-start | bytes 405512 | tf_op jit(solution)/shard_map/ppermute | solution.py:28
  9.1 20.7 %collective-permute-start.1 = (bf16[2,264,256]{2,1,0:T(8,128)(2,1)S(1)}, bf16[2,264,256]{2,1,0:T(8,128)(2,1)S(1)}, u32[]{:S(2)}, u32[]{:S(2)}) collective-permute-start(bf16[2,264,256]{2,1,0:T(8,128)(2,1)S(1)} %pad_maximum_fusion.5), channel_id=1, source_target_pairs={{0,4},{1,5},{2,6},{3,7},{4,0},{5,1},{6,2},{7,3},{8,12},{9,13},{10,... | collective-permute-start | bytes 811016 | tf_op jit(solution)/shard_map/ppermute | solution.py:28
  13.1 9.8 %collective-permute-start.9 = (bf16[1,264,256]{2,1,0:T(8,128)(2,1)S(1)}, bf16[1,264,256]{2,1,0:T(8,128)(2,1)S(1)}, u32[]{:S(2)}, u32[]{:S(2)}) collective-permute-start(bf16[1,264,256]{2,1,0:T(8,128)(2,1)S(1)} %collective-permute-done.8), channel_id=1, source_target_pairs={{0,4},{1,5},{2,6},{3,7},{4,0},{5,1},{6,2},{7,3},{8,12},{9,13},{10,... | collective-permute-start | bytes 405512 | tf_op jit(solution)/shard_map/ppermute | solution.py:28
  19.5 5.4 %collective-permute-start.6 = (bf16[1,264,256]{2,1,0:T(8,128)(2,1)S(1)}, bf16[1,264,256]{2,1,0:T(8,128)(2,1)S(1)}, u32[]{:S(2)}, u32[]{:S(2)}) collective-permute-start(bf16[1,264,256]{2,1,0:T(8,128)(2,1)S(1)} %collective-permute-done.5), channel_id=1, source_target_pairs={{0,2},{1,3},{2,0},{3,1},{4,6},{5,7},{6,4},{7,5},{8,10},{9,11},{10,... | collective-permute-start | bytes 405512 | tf_op jit(solution)/shard_map/ppermute | solution.py:28
  20.7 6.8 %collective-permute-start.3 = (bf16[1,264,256]{2,1,0:T(8,128)(2,1)S(1)}, bf16[1,264,256]{2,1,0:T(8,128)(2,1)S(1)}, u32[]{:S(2)}, u32[]{:S(2)}) collective-permute-start(bf16[1,264,256]{2,1,0:T(8,128)(2,1)S(1)} %collective-permute-done.2), channel_id=1, source_target_pairs={{0,4},{1,5},{2,6},{3,7},{4,0},{5,1},{6,2},{7,3},{8,12},{9,13},{10,... | collective-permute-start | bytes 405512 | tf_op jit(solution)/shard_map/ppermute | solution.py:28
  22.9 15.2 %collective-permute-start.10 = (bf16[2,264,256]{2,1,0:T(8,128)(2,1)S(1)}, bf16[2,264,256]{2,1,0:T(8,128)(2,1)S(1)}, u32[]{:S(2)}, u32[]{:S(2)}) collective-permute-start(bf16[2,264,256]{2,1,0:T(8,128)(2,1)S(1)} %pad_maximum_fusion.8), channel_id=1, source_target_pairs={{0,2},{1,3},{2,0},{3,1},{4,6},{5,7},{6,4},{7,5},{8,10},{9,11},{10,... | collective-permute-start | bytes 811016 | tf_op jit(solution)/shard_map/ppermute | solution.py:28
  24.9 11.9 %collective-permute-start.7 = (bf16[2,264,256]{2,1,0:T(8,128)(2,1)S(1)}, bf16[2,264,256]{2,1,0:T(8,128)(2,1)S(1)}, u32[]{:S(2)}, u32[]{:S(2)}) collective-permute-start(bf16[2,264,256]{2,1,0:T(8,128)(2,1)S(1)} %pad_maximum_fusion.7), channel_id=1, source_target_pairs={{0,4},{1,5},{2,6},{3,7},{4,0},{5,1},{6,2},{7,3},{8,12},{9,13},{10,... | collective-permute-start | bytes 811016 | tf_op jit(solution)/shard_map/ppermute | solution.py:28
  27.5 8.5 %collective-permute-start.4 = (bf16[2,264,256]{2,1,0:T(8,128)(2,1)S(1)}, bf16[2,264,256]{2,1,0:T(8,128)(2,1)S(1)}, u32[]{:S(2)}, u32[]{:S(2)}) collective-permute-start(bf16[2,264,256]{2,1,0:T(8,128)(2,1)S(1)} %pad_maximum_fusion.6), channel_id=1, source_target_pairs={{0,2},{1,3},{2,0},{3,1},{4,6},{5,7},{6,4},{7,5},{8,10},{9,11},{10,... | collective-permute-start | bytes 811016 | tf_op jit(solution)/shard_map/ppermute | solution.py:28
  29.9 10.6 %copy-start.5 = (bf16[4,264,256]{2,1,0:T(8,128)(2,1)}, bf16[4,264,256]{2,1,0:T(8,128)(2,1)S(1)}, u32[]{:S(2)}) copy-start(bf16[4,264,256]{2,1,0:T(8,128)(2,1)S(1)} %pad_maximum_fusion.rest_0_) | copy-start | bytes 1622020
  29.9 10.2 %collective-permute-start.11 = (bf16[4,264,256]{2,1,0:T(8,128)(2,1)S(1)}, bf16[4,264,256]{2,1,0:T(8,128)(2,1)}, u32[]{:S(2)}, u32[]{:S(2)}) collective-permute-start(bf16[4,264,256]{2,1,0:T(8,128)(2,1)S(1)} %pad_maximum_fusion.rest_0_), channel_id=1, source_target_pairs={{0,1},{1,0},{2,3},{3,2},{4,5},{5,4},{6,7},{7,6},{8,9},{9,8},{10,11... | collective-permute-start | bytes 1622024 | tf_op jit(solution)/shard_map/ppermute | solution.py:28
  36.8 3.4 %collective-permute-start.12 = (bf16[4,264,256]{2,1,0:T(8,128)(2,1)}, bf16[4,264,256]{2,1,0:T(8,128)(2,1)}, u32[]{:S(2)}, u32[]{:S(2)}) collective-permute-start(bf16[4,264,256]{2,1,0:T(8,128)(2,1)} %constant_dynamic-update-slice_fusion.rest_1_), channel_id=1, source_target_pairs={{0,1},{1,0},{2,3},{3,2},{4,5},{5,4},{6,7},{7,6},{8,9},{9,8},{10,11... | collective-permute-start | bytes 1622024 | tf_op jit(solution)/shard_map/ppermute | solution.py:28
  37.5 2.6 %collective-permute-start.13 = (bf16[4,264,256]{2,1,0:T(8,128)(2,1)}, bf16[4,264,256]{2,1,0:T(8,128)(2,1)}, u32[]{:S(2)}, u32[]{:S(2)}) collective-permute-start(bf16[4,264,256]{2,1,0:T(8,128)(2,1)} %constant_dynamic-update-slice_fusion.3.rest_2_), channel_id=1, source_target_pairs={{0,1},{1,0},{2,3},{3,2},{4,5},{5,4},{6,7},{7,6},{8,9},{9,8},{10,11... | collective-permute-start | bytes 1622024 | tf_op jit(solution)/shard_map/ppermute | solution.py:28
  38.1 2.4 %copy-start.6 = (bf16[4,264,256]{2,1,0:T(8,128)(2,1)}, bf16[4,264,256]{2,1,0:T(8,128)(2,1)S(1)}, u32[]{:S(2)}) copy-start(bf16[4,264,256]{2,1,0:T(8,128)(2,1)S(1)} %constant_dynamic-update-slice_fusion.6.rest_3_) | copy-start | bytes 1622020
  38.1 2.4 %collective-permute-start.14 = (bf16[4,264,256]{2,1,0:T(8,128)(2,1)S(1)}, bf16[4,264,256]{2,1,0:T(8,128)(2,1)}, u32[]{:S(2)}, u32[]{:S(2)}) collective-permute-start(bf16[4,264,256]{2,1,0:T(8,128)(2,1)S(1)} %constant_dynamic-update-slice_fusion.6.rest_3_), channel_id=1, source_target_pairs={{0,1},{1,0},{2,3},{3,2},{4,5},{5,4},{6,7},{7,6},{8,9},{9,8},{10,11... | collective-permute-start | bytes 1622024 | tf_op jit(solution)/shard_map/ppermute | solution.py:28
  38.2 9.2 %copy-start.1 = (bf16[512,4096]{1,0:T(8,128)(2,1)S(1)}, bf16[512,4096]{1,0:T(8,128)(2,1)}, u32[]{:S(2)}) copy-start(bf16[512,4096]{1,0:T(8,128)(2,1)} %x_ref.2) | copy-start | bytes 12582916
  40.5 8.7 %copy-start.18 = (s32[32]{0:T(128)S(1)}, s32[32]{0:T(128)}, u32[]{:S(2)}) copy-start(s32[32]{0:T(128)} %param.23) | copy-start | bytes 388
  40.5 9.4 %copy-start.13 = (s32[32,16]{0,1:T(8,128)S(1)}, s32[32,16]{0,1:T(8,128)}, u32[]{:S(2)}) copy-start(s32[32,16]{0,1:T(8,128)} %param.22) | copy-start | bytes 6148
  46.2 4.4 %copy-start.7 = (bf16[1,272,256]{2,1,0:T(8,128)(2,1)S(1)}, bf16[1,272,256]{2,1,0:T(8,128)(2,1)}, u32[]{:S(2)}) copy-start(bf16[1,272,256]{2,1,0:T(8,128)(2,1)} %get-tuple-element.8) | copy-start | bytes 417796
  46.2 8.8 %collective-permute-start.15 = (bf16[1,272,256]{2,1,0:T(8,128)(2,1)}, bf16[1,272,256]{2,1,0:T(8,128)(2,1)S(1)}, u32[]{:S(2)}, u32[]{:S(2)}) collective-permute-start(bf16[1,272,256]{2,1,0:T(8,128)(2,1)} %get-tuple-element.8), channel_id=1, source_target_pairs={{0,2},{1,3},{2,0},{3,1},{4,6},{5,7},{6,4},{7,5},{8,10},{9,11},{10,... | collective-permute-start | bytes 417800 | tf_op jit(solution)/shard_map/ppermute | solution.py:28
  49.2 33.4 %copy-start.2 = (bf16[512,4096]{1,0:T(8,128)(2,1)S(1)}, bf16[512,4096]{1,0:T(8,128)(2,1)}, u32[]{:S(2)}) copy-start(bf16[512,4096]{1,0:T(8,128)(2,1)} %g_ref.2) | copy-start | bytes 12582916
  50.6 8.5 %collective-permute-start.23 = (bf16[1,272,256]{2,1,0:T(8,128)(2,1)S(1)}, bf16[1,272,256]{2,1,0:T(8,128)(2,1)S(1)}, u32[]{:S(2)}, u32[]{:S(2)}) collective-permute-start(bf16[1,272,256]{2,1,0:T(8,128)(2,1)S(1)} %copy-done.7), channel_id=1, source_target_pairs={{0,24},{1,25},{2,26},{3,27},{4,28},{5,29},{6,30},{7,31},{8,16},{9,... | collective-permute-start | bytes 417800 | tf_op jit(solution)/shard_map/ppermute | solution.py:28
  52.5 12.0 %collective-permute-start.20 = (bf16[1,272,256]{2,1,0:T(8,128)(2,1)S(1)}, bf16[1,272,256]{2,1,0:T(8,128)(2,1)S(1)}, u32[]{:S(2)}, u32[]{:S(2)}) collective-permute-start(bf16[1,272,256]{2,1,0:T(8,128)(2,1)S(1)} %copy-done.7), channel_id=1, source_target_pairs={{0,16},{1,17},{2,18},{3,19},{4,20},{5,21},{6,22},{7,23},{8,24},{9,... | collective-permute-start | bytes 417800 | tf_op jit(solution)/shard_map/ppermute | solution.py:28
  52.5 13.3 %collective-permute-start.17 = (bf16[1,272,256]{2,1,0:T(8,128)(2,1)S(1)}, bf16[1,272,256]{2,1,0:T(8,128)(2,1)S(1)}, u32[]{:S(2)}, u32[]{:S(2)}) collective-permute-start(bf16[1,272,256]{2,1,0:T(8,128)(2,1)S(1)} %copy-done.7), channel_id=1, source_target_pairs={{0,8},{1,9},{2,10},{3,11},{4,12},{5,13},{6,14},{7,15},{8,0},{9,1},... | collective-permute-start | bytes 417800 | tf_op jit(solution)/shard_map/ppermute | solution.py:28
  55.0 18.3 %collective-permute-start.16 = (bf16[2,272,256]{2,1,0:T(8,128)(2,1)S(1)}, bf16[2,272,256]{2,1,0:T(8,128)(2,1)S(1)}, u32[]{:S(2)}, u32[]{:S(2)}) collective-permute-start(bf16[2,272,256]{2,1,0:T(8,128)(2,1)S(1)} %pad_maximum_fusion.1), channel_id=1, source_target_pairs={{0,4},{1,5},{2,6},{3,7},{4,0},{5,1},{6,2},{7,3},{8,12},{9,13},{10,... | collective-permute-start | bytes 835592 | tf_op jit(solution)/shard_map/ppermute | solution.py:28
  59.1 7.6 %collective-permute-start.24 = (bf16[1,272,256]{2,1,0:T(8,128)(2,1)S(1)}, bf16[1,272,256]{2,1,0:T(8,128)(2,1)S(1)}, u32[]{:S(2)}, u32[]{:S(2)}) collective-permute-start(bf16[1,272,256]{2,1,0:T(8,128)(2,1)S(1)} %collective-permute-done.23), channel_id=1, source_target_pairs={{0,4},{1,5},{2,6},{3,7},{4,0},{5,1},{6,2},{7,3},{8,12},{9,13},{10,... | collective-permute-start | bytes 417800 | tf_op jit(solution)/shard_map/ppermute | solution.py:28
  64.5 6.5 %collective-permute-start.21 = (bf16[1,272,256]{2,1,0:T(8,128)(2,1)S(1)}, bf16[1,272,256]{2,1,0:T(8,128)(2,1)S(1)}, u32[]{:S(2)}, u32[]{:S(2)}) collective-permute-start(bf16[1,272,256]{2,1,0:T(8,128)(2,1)S(1)} %collective-permute-done.20), channel_id=1, source_target_pairs={{0,2},{1,3},{2,0},{3,1},{4,6},{5,7},{6,4},{7,5},{8,10},{9,11},{10,... | collective-permute-start | bytes 417800 | tf_op jit(solution)/shard_map/ppermute | solution.py:28
  65.8 6.4 %collective-permute-start.18 = (bf16[1,272,256]{2,1,0:T(8,128)(2,1)S(1)}, bf16[1,272,256]{2,1,0:T(8,128)(2,1)S(1)}, u32[]{:S(2)}, u32[]{:S(2)}) collective-permute-start(bf16[1,272,256]{2,1,0:T(8,128)(2,1)S(1)} %collective-permute-done.17), channel_id=1, source_target_pairs={{0,4},{1,5},{2,6},{3,7},{4,0},{5,1},{6,2},{7,3},{8,12},{9,13},{10,... | collective-permute-start | bytes 417800 | tf_op jit(solution)/shard_map/ppermute | solution.py:28
  66.7 15.8 %collective-permute-start.25 = (bf16[2,272,256]{2,1,0:T(8,128)(2,1)S(1)}, bf16[2,272,256]{2,1,0:T(8,128)(2,1)S(1)}, u32[]{:S(2)}, u32[]{:S(2)}) collective-permute-start(bf16[2,272,256]{2,1,0:T(8,128)(2,1)S(1)} %pad_maximum_fusion.4), channel_id=1, source_target_pairs={{0,2},{1,3},{2,0},{3,1},{4,6},{5,7},{6,4},{7,5},{8,10},{9,11},{10,... | collective-permute-start | bytes 835592 | tf_op jit(solution)/shard_map/ppermute | solution.py:28
  71.0 11.0 %collective-permute-start.22 = (bf16[2,272,256]{2,1,0:T(8,128)(2,1)S(1)}, bf16[2,272,256]{2,1,0:T(8,128)(2,1)S(1)}, u32[]{:S(2)}, u32[]{:S(2)}) collective-permute-start(bf16[2,272,256]{2,1,0:T(8,128)(2,1)S(1)} %pad_maximum_fusion.3), channel_id=1, source_target_pairs={{0,4},{1,5},{2,6},{3,7},{4,0},{5,1},{6,2},{7,3},{8,12},{9,13},{10,... | collective-permute-start | bytes 835592 | tf_op jit(solution)/shard_map/ppermute | solution.py:28
  72.3 9.5 %collective-permute-start.19 = (bf16[2,272,256]{2,1,0:T(8,128)(2,1)S(1)}, bf16[2,272,256]{2,1,0:T(8,128)(2,1)S(1)}, u32[]{:S(2)}, u32[]{:S(2)}) collective-permute-start(bf16[2,272,256]{2,1,0:T(8,128)(2,1)S(1)} %pad_maximum_fusion.2), channel_id=1, source_target_pairs={{0,2},{1,3},{2,0},{3,1},{4,6},{5,7},{6,4},{7,5},{8,10},{9,11},{10,... | collective-permute-start | bytes 835592 | tf_op jit(solution)/shard_map/ppermute | solution.py:28
  73.3 24.0 %copy-start.12 = (bf16[4,272,256]{2,1,0:T(8,128)(2,1)}, bf16[4,272,256]{2,1,0:T(8,128)(2,1)S(1)}, u32[]{:S(2)}) copy-start(bf16[4,272,256]{2,1,0:T(8,128)(2,1)S(1)} %constant_dynamic-update-slice_fusion.9.rest_0_) | copy-start | bytes 1671172
  73.4 24.1 %collective-permute-start.26 = (bf16[4,272,256]{2,1,0:T(8,128)(2,1)S(1)}, bf16[4,272,256]{2,1,0:T(8,128)(2,1)S(1)}, u32[]{:S(2)}, u32[]{:S(2)}) collective-permute-start(bf16[4,272,256]{2,1,0:T(8,128)(2,1)S(1)} %constant_dynamic-update-slice_fusion.9.rest_0_), channel_id=1, source_target_pairs={{0,1},{1,0},{2,3},{3,2},{4,5},{5,4},{6,7},{7,6},{8,9},{9,8},{10,11... | collective-permute-start | bytes 1671176 | tf_op jit(solution)/shard_map/ppermute | solution.py:28
  81.8 15.6 %copy-start.11 = (bf16[4,272,256]{2,1,0:T(8,128)(2,1)}, bf16[4,272,256]{2,1,0:T(8,128)(2,1)S(1)}, u32[]{:S(2)}) copy-start(bf16[4,272,256]{2,1,0:T(8,128)(2,1)S(1)} %constant_dynamic-update-slice_fusion.12.rest_1_) | copy-start | bytes 1671172
  81.8 15.6 %collective-permute-start.27 = (bf16[4,272,256]{2,1,0:T(8,128)(2,1)S(1)}, bf16[4,272,256]{2,1,0:T(8,128)(2,1)S(1)}, u32[]{:S(2)}, u32[]{:S(2)}) collective-permute-start(bf16[4,272,256]{2,1,0:T(8,128)(2,1)S(1)} %constant_dynamic-update-slice_fusion.12.rest_1_), channel_id=1, source_target_pairs={{0,1},{1,0},{2,3},{3,2},{4,5},{5,4},{6,7},{7,6},{8,9},{9,8},{10,11... | collective-permute-start | bytes 1671176 | tf_op jit(solution)/shard_map/ppermute | solution.py:28
  82.0 15.5 %copy-start.10 = (bf16[4,272,256]{2,1,0:T(8,128)(2,1)}, bf16[4,272,256]{2,1,0:T(8,128)(2,1)S(1)}, u32[]{:S(2)}) copy-start(bf16[4,272,256]{2,1,0:T(8,128)(2,1)S(1)} %constant_dynamic-update-slice_fusion.15.rest_2_) | copy-start | bytes 1671172
  82.0 15.5 %collective-permute-start.28 = (bf16[4,272,256]{2,1,0:T(8,128)(2,1)S(1)}, bf16[4,272,256]{2,1,0:T(8,128)(2,1)S(1)}, u32[]{:S(2)}, u32[]{:S(2)}) collective-permute-start(bf16[4,272,256]{2,1,0:T(8,128)(2,1)S(1)} %constant_dynamic-update-slice_fusion.15.rest_2_), channel_id=1, source_target_pairs={{0,1},{1,0},{2,3},{3,2},{4,5},{5,4},{6,7},{7,6},{8,9},{9,8},{10,11... | collective-permute-start | bytes 1671176 | tf_op jit(solution)/shard_map/ppermute | solution.py:28
  82.5 14.9 %copy-start.9 = (bf16[4,272,256]{2,1,0:T(8,128)(2,1)}, bf16[4,272,256]{2,1,0:T(8,128)(2,1)S(1)}, u32[]{:S(2)}) copy-start(bf16[4,272,256]{2,1,0:T(8,128)(2,1)S(1)} %constant_dynamic-update-slice_fusion.18.rest_3_) | copy-start | bytes 1671172
  82.6 14.9 %collective-permute-start.29 = (bf16[4,272,256]{2,1,0:T(8,128)(2,1)S(1)}, bf16[4,272,256]{2,1,0:T(8,128)(2,1)S(1)}, u32[]{:S(2)}, u32[]{:S(2)}) collective-permute-start(bf16[4,272,256]{2,1,0:T(8,128)(2,1)S(1)} %constant_dynamic-update-slice_fusion.18.rest_3_), channel_id=1, source_target_pairs={{0,1},{1,0},{2,3},{3,2},{4,5},{5,4},{6,7},{7,6},{8,9},{9,8},{10,11... | collective-permute-start | bytes 1671176 | tf_op jit(solution)/shard_map/ppermute | solution.py:28
  97.4 0.8 copy-start.14
  97.5 1.0 copy-start.15
  97.5 1.1 %copy-start.16 = (bf16[4,272,256]{2,1,0:T(8,128)(2,1)}, bf16[4,272,256]{2,1,0:T(8,128)(2,1)S(1)}, u32[]{:S(2)}) copy-start(bf16[4,272,256]{2,1,0:T(8,128)(2,1)S(1)} %collective-permute-done.28.rest_6_) | copy-start | bytes 1671172
  97.5 1.4 %copy-start.17 = (bf16[4,272,256]{2,1,0:T(8,128)(2,1)}, bf16[4,272,256]{2,1,0:T(8,128)(2,1)S(1)}, u32[]{:S(2)}) copy-start(bf16[4,272,256]{2,1,0:T(8,128)(2,1)S(1)} %collective-permute-done.29.rest_7_) | copy-start | bytes 1671172

commit v2 on v0

v2 whole, which is shorter than its diff:
```python
import functools

import jax
import jax.numpy as jnp
from jax import lax
from jax.experimental import pallas as pl
from jax.experimental.pallas import tpu as pltpu
from jax.sharding import PartitionSpec as P

RANK = 16
PW = 256
K = 2 * RANK * PW
TRAIN_EXAMPLES = 32
EVAL_ROLLOUTS = 16
SLOTS = 16
EPS = 1e-06

VMEM = pl.BlockSpec(memory_space=pltpu.VMEM)
SMEM = pl.BlockSpec(memory_space=pltpu.SMEM)
BF16 = jnp.bfloat16
F32 = jnp.float32
NT = (((1,), (1,)), ((), ()))


def gather_chunks(block, n, early, middle, late):
    if n != 32:
        whole = lax.all_gather(block, "train", axis=0, tiled=True)
        return None, [[(whole, list(range(n)))]], early, middle(early)

    def permute(held, mask):
        return lax.ppermute(held, "train", [(i, i ^ mask) for i in range(n)])

    orders = [(2, 4), (4, 2), (2, 4), (4, 2)]
    rows = [block] + [permute(block, mask) for mask in (8, 16, 24)]
    first, held, second, swapped = [permute(block, 2)], [], [], []
    first[0], rows[1], early = lax.optimization_barrier((first[0], rows[1], early))

    def join(chunk):
        held.append(jnp.concatenate([rows[chunk], first[chunk]], axis=0))

    def spread(chunk):
        second.append(permute(held[chunk], orders[chunk][1]))
        swapped.append(permute(held[chunk], 1))

    def finish(chunk):
        one, two = orders[chunk]
        return [
            (held[chunk], [0, one]),
            (second[chunk], [two, one ^ two]),
            (swapped[chunk], [1, one ^ 1]),
            (permute(second[chunk], 1), [two ^ 1, one ^ two ^ 1]),
        ]

    first.append(permute(rows[1], orders[1][0]))
    join(0)
    held[0], early = lax.optimization_barrier((held[0], early))
    spread(0)
    middle = middle(early)
    join(1)
    spread(1)
    rows[2], rows[3], middle = lax.optimization_barrier((rows[2], rows[3], middle))
    first.append(permute(rows[2], orders[2][0]))
    first.append(permute(rows[3], orders[3][0]))
    join(2)
    join(3)
    spread(2)
    spread(3)
    front = [finish(0), finish(1)]
    done = late(front, middle)
    second[2], second[3], done = lax.optimization_barrier((second[2], second[3], done))
    return (done, front), [finish(2), finish(3)], early, middle


def placed(n):
    mine = lax.axis_index("train").astype(jnp.int32)
    if n != 32:
        return jnp.zeros((2,), jnp.int32), n
    return jnp.stack([mine // 8, mine % 8]), 8


def plan(chunks, start):
    return (
        [(start + c, lows) for c, chunk in enumerate(chunks) for _, lows in chunk],
        [array for chunk in chunks for array, _ in chunk],
    )


def split(value):
    high = value.astype(BF16)
    return high, (value - high.astype(F32)).astype(BF16)


def dot3(left, right):
    lh, ll = split(left)
    rh, rl = split(right)
    dot = functools.partial(jnp.dot, preferred_element_type=F32)
    return dot(lh, rh) + (dot(lh, rl) + dot(ll, rh))


def one_hot(index_row, count):
    steps = lax.broadcasted_iota(jnp.int32, (count, index_row.shape[1]), 0)
    return (index_row == steps).astype(F32)


def weighted(rows, picked):
    ranks, tokens = rows.shape
    return (rows[:, None, :] * picked[None, :, :]).reshape(ranks * picked.shape[0], tokens)


def squares(raw, items):
    each = jnp.sum(raw * raw, axis=1, keepdims=True)
    return jnp.sum(each.reshape(RANK, items, 1), axis=0)


def project(steps, size, place_ref, x_ref, g_ref, refs, held, grad, inp):
    hi, lo = place_ref[0], place_ref[1]
    part = refs[0].shape[1] // 2
    start, width = steps[0][0], size * part
    for ref, (chunk, lows) in zip(refs, steps):
        for s, low in enumerate(lows):
            held[chunk - start, 0, lo ^ low] = ref[s, 0:part, :]
            held[chunk - start, 1, lo ^ low] = ref[s, part : 2 * part, :]
    for chunk in sorted({c for c, _ in steps}):
        columns = pl.ds(pl.multiple_of((hi ^ chunk) * width, width), width)
        more = jnp.dot(g_ref[:, columns], held[chunk - start, 0].reshape(width, PW), preferred_element_type=F32)
        grad = more if grad is None else grad + more
        more = jnp.dot(x_ref[:, columns], held[chunk - start, 1].reshape(width, PW), preferred_element_type=F32)
        inp = more if inp is None else inp + more
    return grad, inp


def begin_kernel(steps, size, place_ref, x_ref, g_ref, *rest):
    refs, (sums_ref, held) = rest[: len(steps)], rest[len(steps) :]
    grad, inp = project(steps, size, place_ref, x_ref, g_ref, refs, held, None, None)
    sums_ref[0] = grad
    sums_ref[1] = inp


def eval_kernel(steps, size, begun, place_ref, x_ref, g_ref, hidden_ref, back_ref, index_ref, *rest):
    refs, rest = rest[: len(steps)], rest[len(steps) :]
    pack_ref, held = rest[begun:]
    grad, inp = (rest[0][0], rest[0][1]) if begun else (None, None)
    grad, inp = project(steps, size, place_ref, x_ref, g_ref, refs, held, grad, inp)
    picked = one_hot(index_ref[...], EVAL_ROLLOUTS)
    hidden, back = hidden_ref[...], back_ref[...]
    total = squares(dot3(weighted(hidden, picked), grad), EVAL_ROLLOUTS)
    total = total + squares(dot3(weighted(back, picked), inp), EVAL_ROLLOUTS)
    scale = lax.rsqrt(total * (1.0 / K) + EPS)
    per_token = jnp.sum(picked * scale, axis=0, keepdims=True)
    tokens = x_ref.shape[0]
    base = 2 * tokens
    pack_ref[0, 0:tokens, :] = grad.astype(BF16)
    pack_ref[0, tokens:base, :] = inp.astype(BF16)
    pack_ref[0, base : base + RANK, 0:tokens] = (hidden * per_token).astype(BF16)
    pack_ref[0, base : base + RANK, tokens:base] = (back * per_token).astype(BF16)
    index = jnp.broadcast_to(index_ref[...].astype(F32), (RANK, tokens)).astype(BF16)
    pack_ref[0, base + RANK : base + 2 * RANK, 0:tokens] = index
    pack_ref[0, base + RANK : base + 2 * RANK, tokens:base] = index


def train_kernel(steps, size, side, place_ref, act_ref, factor_ref, index_ref, *rest):
    refs, rest = rest[: len(steps)], rest[len(steps) :]
    hi, lo = place_ref[0], place_ref[1]
    part = refs[0].shape[1] // 2
    held = rest[-1]
    for ref, (chunk, lows) in zip(refs, steps):
        for s, low in enumerate(lows):
            held[(hi ^ chunk) * size + (lo ^ low)] = ref[s, side * part : (side + 1) * part, :]
    width = held.shape[0] * part
    values = jnp.dot(act_ref[...], held[...].reshape(width, PW), preferred_element_type=F32)
    picked = one_hot(index_ref[...], TRAIN_EXAMPLES)
    raw = dot3(weighted(factor_ref[...], picked), values)
    total = squares(raw, TRAIN_EXAMPLES)
    if side == 0:
        rest[0][...] = raw
        rest[1][...] = total
        return
    raw_ref, total_ref, feats_ref = rest[:3]
    scale = lax.rsqrt((total_ref[...] + total) * (1.0 / K) + EPS)[None]
    shape = (RANK, TRAIN_EXAMPLES, PW)
    feats_ref[0] = (raw_ref[...].reshape(shape) * scale).reshape(RANK * TRAIN_EXAMPLES, PW).astype(BF16)
    feats_ref[1] = (raw.reshape(shape) * scale).reshape(RANK * TRAIN_EXAMPLES, PW).astype(BF16)


def make_tiles(steps, size, place_ref, feats_ref, refs, tiles_ref):
    hi, lo = place_ref[0], place_ref[1]
    tokens = refs[0].shape[1] // 2 - RANK
    base = 2 * tokens
    shape = (RANK, TRAIN_EXAMPLES, base)
    dot = functools.partial(lax.dot_general, dimension_numbers=NT, preferred_element_type=F32)
    for ref, (chunk, lows) in zip(refs, steps):
        for s in range(0, len(lows), 2):
            two = slice(s, s + 2)
            grad = ref[two, 0:tokens, :].reshape(base, PW)
            inp = ref[two, tokens:base, :].reshape(base, PW)
            coef = ref[two, base : base + RANK, :].astype(F32)
            hidden = jnp.concatenate([coef[0, :, 0:tokens], coef[1, :, 0:tokens]], axis=1)
            back = jnp.concatenate([coef[0, :, tokens:], coef[1, :, tokens:]], axis=1)
            mixed = jnp.sum(dot(feats_ref[0], grad).reshape(shape) * hidden[:, None, :], axis=0)
            mixed = mixed + jnp.sum(dot(feats_ref[1], inp).reshape(shape) * back[:, None, :], axis=0)
            high, low = split(mixed)
            for k in range(2):
                index = ref[s + k, base + RANK : base + 2 * RANK, 0:tokens].astype(F32)
                picked = one_hot(index[0:1].astype(jnp.int32), EVAL_ROLLOUTS).astype(BF16)
                lanes = slice(k * tokens, (k + 1) * tokens)
                tile = dot(picked, high[:, lanes]) + dot(picked, low[:, lanes])
                tiles_ref[(hi ^ chunk) * size + (lo ^ lows[s + k])] = tile


def tile_kernel(steps, size, place_ref, feats_ref, *rest):
    make_tiles(steps, size, place_ref, feats_ref, rest[: len(steps)], rest[len(steps)])


def score_kernel(steps, size, front, place_ref, chosen_ref, live_ref, feats_ref, *rest):
    refs, rest = rest[: len(steps)], rest[len(steps) :]
    out_ref, tiles = rest[-2:]
    make_tiles(steps, size, place_ref, feats_ref, refs, tiles)
    for chunk in range(front):
        for low in range(size):
            device = (place_ref[0] ^ chunk) * size + low
            tiles[device] = rest[0][device]
    for slot in range(SLOTS):
        factor = jnp.where(slot < live_ref[0], 1.0 / K**0.5, 0.0)
        out_ref[0, slot] = tiles[chosen_ref[slot]] * factor


def call(kernel, out_shape, scratch, flops, name, scalars, *arrays):
    return pl.pallas_call(
        kernel,
        out_shape=out_shape,
        in_specs=[SMEM] * len(scalars) + [VMEM] * len(arrays),
        out_specs=jax.tree.map(lambda _: VMEM, out_shape),
        scratch_shapes=scratch,
        compiler_params=pltpu.CompilerParams(vmem_limit_bytes=28 * 1024 * 1024),
        cost_estimate=pl.CostEstimate(flops=flops, bytes_accessed=4 * 2**20, transcendentals=0),
        name=name,
    )(*scalars, *arrays)


def per_device(
    n,
    train_layer_input,
    train_output_gradient,
    train_example_index,
    eval_layer_input,
    eval_output_gradient,
    eval_rollout_index,
    adapter_down,
    adapter_up,
    gradient_projector,
    input_projector,
    paired_eval_index,
    live_slot_count,
):
    place, size = placed(n)
    mine = lax.axis_index("train")
    tokens = eval_layer_input.shape[0]
    part = gradient_projector.shape[0]
    acts = (eval_layer_input, eval_output_gradient)
    sums = jax.ShapeDtypeStruct((2, tokens, PW), F32)
    tiles_shape = (n, EVAL_ROLLOUTS, TRAIN_EXAMPLES)

    def down(x):
        return lax.dot_general(adapter_down, x, (((0,), (1,)), ((), ())), preferred_element_type=F32)

    def up(g):
        return lax.dot_general(adapter_up, g, NT, preferred_element_type=F32)

    chosen = lax.dynamic_index_in_dim(paired_eval_index, mine, 0, keepdims=False)
    live = lax.dynamic_index_in_dim(live_slot_count, mine, 0, keepdims=True)
    early = (down(eval_layer_input), up(eval_output_gradient), chosen, live, train_layer_input, train_output_gradient)

    def middle(early):
        return down(early[4]), up(early[5])

    held = [pltpu.VMEM((2, 2, size, part, PW), BF16)]

    def begin(front, _):
        steps, arrays = plan(front, 0)
        kernel = functools.partial(begin_kernel, steps, size)
        return call(kernel, sums, held, 5 * 10**8, "eval_begin", [place], *acts, *arrays)

    block = jnp.concatenate([gradient_projector, input_projector], axis=0)[None]
    begun, back, early, middle = gather_chunks(block, n, early, middle, begin)
    front, extra = ([], []) if begun is None else (begun[1], [begun[0]])
    steps, arrays = plan(back, len(front))
    pack = call(
        functools.partial(eval_kernel, steps, size, len(extra)),
        jax.ShapeDtypeStruct((1, 2 * (tokens + RANK), PW), BF16),
        held,
        10**9,
        "eval_factors",
        [place],
        *acts,
        early[0],
        early[1],
        eval_rollout_index,
        *arrays,
        *extra,
    )
    steps, arrays = plan(front + back, 0)
    held = [pltpu.VMEM((n, part, PW), BF16)]
    rows = RANK * TRAIN_EXAMPLES
    raw = call(
        functools.partial(train_kernel, steps, size, 0),
        [jax.ShapeDtypeStruct((rows, PW), F32), jax.ShapeDtypeStruct((TRAIN_EXAMPLES, 1), F32)],
        held,
        2 * 10**9,
        "train_gradient_side",
        [place],
        train_output_gradient,
        middle[0],
        train_example_index,
        *arrays,
    )

    def finish_train(raw):
        return call(
            functools.partial(train_kernel, steps, size, 1),
            jax.ShapeDtypeStruct((2, rows, PW), BF16),
            held,
            2 * 10**9,
            "train_input_side",
            [place],
            train_layer_input,
            middle[1],
            train_example_index,
            *arrays,
            *raw,
        )

    def tile(front, feats):
        steps, arrays = plan(front, 0)
        kernel = functools.partial(tile_kernel, steps, size)
        shape = jax.ShapeDtypeStruct(tiles_shape, F32)
        return call(kernel, shape, [], 10**9, "front_tiles", [place], feats, *arrays)

    tiles, back, _, feats = gather_chunks(pack, n, raw, finish_train, tile)
    front, extra = ([], []) if tiles is None else (tiles[1], [tiles[0]])
    steps, arrays = plan(back, len(front))
    scores = call(
        functools.partial(score_kernel, steps, size, len(front)),
        jax.ShapeDtypeStruct((1, SLOTS, EVAL_ROLLOUTS, TRAIN_EXAMPLES), F32),
        [pltpu.VMEM(tiles_shape, F32)],
        10**9,
        "score_tiles",
        [place, early[2], early[3]],
        feats,
        *arrays,
        *extra,
    )
    return jnp.swapaxes(scores, 2, 3)


def solution(mesh):
    in_specs = (
        P(("parts", "train"), None),
        P(("parts", "train"), None),
        P(("parts", "train"), None),
        P(("parts", "train"), None),
        P(("parts", "train"), None),
        P(("parts", "train"), None),
        P(),
        P(),
        P("train", None),
        P("train", None),
        P("parts", None),
        P("parts"),
    )
    out_specs = P(("parts", "train"), None, None, None)
    return jax.shard_map(
        functools.partial(per_device, mesh.shape["train"]),
        mesh=mesh,
        in_specs=in_specs,
        out_specs=out_specs,
        check_vma=False,
    )
```

time: 221 us -> 93.7 us (0.42)
  waiting for transfers between devices: 178 us -> 26.6 us
  starting transfers between devices: 0.08 us -> 28.7 us
  Pallas kernels: 0 us -> 20.7 us
  matrix products: 24.9 us -> 9.23 us
  between operations: 13.4 us -> 0.32 us
  local copies, waits for them, and re-layouts: 1.69 us -> 6.82 us
    all_gather x3 -> x0, waiting for transfers between devices: 176 us -> none  [the longest x1 63.3 us: per_device(): piece = lax.all_gather(eval_feats, 'train', axis=0, tiled=True)]
    ppermute x0 -> x38, starting transfers between devices: none -> 28.7 us  [permute(): return lax.ppermute(held, 'train', [(i, i ^ mask) for i in range(n)])]
    ppermute x0 -> x38, waiting for transfers between devices: none -> 26.6 us  [permute(): return lax.ppermute(held, 'train', [(i, i ^ mask) for i in range(n)])]
    pallas_call x0 -> x6, Pallas kernels: none -> 20.7 us  [call(): pl.pallas_call(kernel, out_shape=out_shape, in_specs=[SMEM] * len(scalars...]
    dot_general x14 -> x4, matrix products: 24.9 us -> 9.23 us  [the longest x2 5.73 us: down(): lax.dot_general(adapter_down, x, (((0,), (1,)), ((), ())), preferred_elem...]
    unnamed x26 -> x36, local copies, waits for them, and re-layouts: 1.04 us -> 3.84 us
    dynamic_slice x1 -> x2, local copies, waits for them, and re-layouts: 0.59 us -> 2.92 us  [the longest x1 1.47 us: per_device(): lax.dynamic_index_in_dim(paired_eval_index, mine, 0, keepdims=False)]
  transfers between devices with their start and end apart: 3 -> 38, of which waited for: 3 -> 15; matrix products, arithmetic and copies ran while one was open for 9% -> 15% of each run, Pallas kernels for 0% -> 15%
where the time goes in v2:
time: 93.7 us; the launch traced here: 93.3 us
  starting transfers between devices  28.7 us (31%)
  waiting for transfers between devices  26.6 us (28%)
  Pallas kernels  20.7 us (22%)
  matrix products  9.23 us (10%)
  local copies, waits for them, and re-layouts  6.82 us (7%)
  other arithmetic  1.06 us (1%)
    ppermute x38, starting transfers between devices, permute(): return lax.ppermute(held, 'train', [(i, i ^ mask) for i in range(n)])  28.7 us
    ppermute x38, waiting for transfers between devices, permute(): return lax.ppermute(held, 'train', [(i, i ^ mask) for i in range(n)])  26.6 us
    pallas_call x6, Pallas kernels, call(): pl.pallas_call(kernel, out_shape=out_shape, in_specs=[SMEM] * len(scalars...  20.7 us
    dot_general x2, matrix products, down(): lax.dot_general(adapter_down, x, (((0,), (1,)), ((), ())), preferred_elem...  5.73 us
    unnamed x36, local copies, waits for them, and re-layouts  3.84 us
    dot_general x2, matrix products, up(): return lax.dot_general(adapter_up, g, NT, preferred_element_type=F32)  3.5 us
  transfers between devices with their start and end apart: 38, of which 15 were waited for; matrix products, arithmetic and copies ran while one was open for 15% of the time, Pallas kernels for 15%

profile of v2, /device:TPU:0, one launch (start us, length us, event | category | flops | bytes accessed | tf_op | source)
XLA Modules:
  0.0 93.3 jit_solution(6501948747674923077)
XLA Ops:
  0.0 0.9 maximum_bitcast_fusion
  0.9 5.1 %collective-permute-start.3 = (bf16[1,256,256]{2,1,0:T(8,128)(2,1)S(1)}, bf16[1,256,256]{2,1,0:T(8,128)(2,1)}, u32[]{:S(2)}, u32[]{:S(2)}) collective-permute-start(bf16[1,256,256]{2,1,0:T(8,128)(2,1)S(1)} %maximum_bitcast_fusion), channel_id=1, source_target_pairs={{0,24},{1,25},{2,26},{3,27},{4,28},{5,29},{6,30},{7,31},{8,16},{9,... | collective-permute-start | bytes 393224 | tf_op jit(solution)/shard_map/ppermute | solution.py:31
  6.0 0.6 collective-permute-start.1
  6.7 1.6 %collective-permute-start = (bf16[1,256,256]{2,1,0:T(8,128)(2,1)S(1)}, bf16[1,256,256]{2,1,0:T(8,128)(2,1)S(1)}, u32[]{:S(2)}, u32[]{:S(2)}) collective-permute-start(bf16[1,256,256]{2,1,0:T(8,128)(2,1)S(1)} %maximum_bitcast_fusion), channel_id=1, source_target_pairs={{0,2},{1,3},{2,0},{3,1},{4,6},{5,7},{6,4},{7,5},{8,10},{9,11},{10,... | collective-permute-start | bytes 393224 | tf_op jit(solution)/shard_map/ppermute | solution.py:31
  8.3 1.5 %dynamic_slice.9.live_ref = s32[1]{0:T(128)} dynamic-slice(s32[32]{0:T(128)} %param.23, s32[]{:T(128)S(6)} %select_n.19), dynamic_slice_sizes={1} | dynamic-slice | bytes 12 | tf_op jit(solution)/shard_map/jit(dynamic_index_in_dim)/dynamic_slice | solution.py:270
  9.8 1.5 %dynamic-slice_reduce_fusion.chosen_ref = s32[16]{0:T(128)} fusion(s32[32,16]{0,1:T(8,128)} %param.22, s32[]{:T(128)S(6)} %select_n.19), kind=kLoop, calls=%fused_computation.17 | loop fusion | bytes 132 | tf_op jit(solution)/shard_map/jit(dynamic_index_in_dim)/dynamic_slice | solution.py:269
  11.2 1.6 %fusion.hidden_ref = f32[16,128]{1,0:T(8,128)S(1)} fusion(bf16[4096,16]{0,1:T(8,128)(2,1)S(1)} %copy-done, bf16[128,4096]{1,0:T(8,128)(2,1)} %x_ref.3), kind=kOutput, calls=%fused_computation.19 | convolution fusion | flops 16777216 | bytes 1187840 | tf_op jit(solution)/shard_map/dot_general | solution.py:264
  12.8 1.7 %fusion.1.back_ref = f32[16,128]{1,0:T(8,128)S(1)} fusion(bf16[16,4096]{1,0:T(8,128)(2,1)} %param.19, bf16[128,4096]{1,0:T(8,128)(2,1)} %g_ref.3), kind=kOutput, calls=%fused_computation.20 | convolution fusion | flops 16777216 | bytes 1187840 | tf_op jit(solution)/shard_map/dot_general | solution.py:267
  14.6 4.1 %convolution_bitcast_fusion.1.factor_ref = f32[16,512]{1,0:T(8,128)} fusion(bf16[512,4096]{1,0:T(8,128)(2,1)} %act_ref.3, bf16[4096,16]{0,1:T(8,128)(2,1)S(1)} %copy-done), kind=kOutput, calls=%fused_computation.1 | convolution fusion | flops 67108864 | bytes 4358144 | tf_op jit(solution)/shard_map/dot_general | solution.py:264
  18.8 1.5 %collective-permute-start.11 = (bf16[1,256,256]{2,1,0:T(8,128)(2,1)S(1)}, bf16[1,256,256]{2,1,0:T(8,128)(2,1)S(1)}, u32[]{:S(2)}, u32[]{:S(2)}) collective-permute-start(bf16[1,256,256]{2,1,0:T(8,128)(2,1)S(1)} %collective-permute-done.1), channel_id=1, source_target_pairs={{0,4},{1,5},{2,6},{3,7},{4,0},{5,1},{6,2},{7,3},{8,12},{9,13},{10,... | collective-permute-start | bytes 393224 | tf_op jit(solution)/shard_map/ppermute | solution.py:31
  20.3 1.8 %convolution_bitcast_fusion.factor_ref = f32[16,512]{1,0:T(8,128)} fusion(bf16[512,4096]{1,0:T(8,128)(2,1)S(1)} %copy-done.1, bf16[16,4096]{1,0:T(8,128)(2,1)S(1)} %copy-done.14), kind=kOutput, calls=%fused_computation | convolution fusion | flops 67108864 | bytes 4358144 | tf_op jit(solution)/shard_map/dot_general | solution.py:267
  22.1 1.4 %collective-permute-start.4 = (bf16[1,256,256]{2,1,0:T(8,128)(2,1)}, bf16[1,256,256]{2,1,0:T(8,128)(2,1)S(1)}, u32[]{:S(2)}, u32[]{:S(2)}) collective-permute-start(bf16[1,256,256]{2,1,0:T(8,128)(2,1)} %collective-permute-done.2), channel_id=1, source_target_pairs={{0,2},{1,3},{2,0},{3,1},{4,6},{5,7},{6,4},{7,5},{8,10},{9,11},{10,... | collective-permute-start | bytes 393224 | tf_op jit(solution)/shard_map/ppermute | solution.py:31
  23.5 0.5 collective-permute-start.6
  24.0 1.5 %collective-permute-start.8 = (bf16[2,256,256]{2,1,0:T(8,128)(2,1)S(1)}, bf16[2,256,256]{2,1,0:T(8,128)(2,1)S(1)}, u32[]{:S(2)}, u32[]{:S(2)}) collective-permute-start(bf16[2,256,256]{2,1,0:T(8,128)(2,1)S(1)} %pad_maximum_fusion.1.rest_0_), channel_id=1, source_target_pairs={{0,4},{1,5},{2,6},{3,7},{4,0},{5,1},{6,2},{7,3},{8,12},{9,13},{10,... | collective-permute-start | bytes 786440 | tf_op jit(solution)/shard_map/ppermute | solution.py:31
  25.6 0.7 collective-permute-start.12
  26.3 0.9 constant_dynamic-update-slice_fusion.1
  27.2 0.1 collective-permute-start.9
  27.3 0.9 constant_dynamic-update-slice_fusion.3
  28.2 2.0 %collective-permute-done.6 = bf16[1,256,256]{2,1,0:T(8,128)(2,1)S(1)} collective-permute-done((bf16[1,256,256]{2,1,0:T(8,128)(2,1)}, bf16[1,256,256]{2,1,0:T(8,128)(2,1)S(1)}, u32[]{:S(2)}, u32[]{:S(2)}) %collective-permute-start.6) | collective-permute-done | bytes 131104 | tf_op jit(solution)/shard_map/ppermute | solution.py:31
  30.2 0.7 collective-permute-start.7
  30.9 2.3 %collective-permute-done.8.rest_1_ = bf16[2,256,256]{2,1,0:T(8,128)(2,1)S(1)} collective-permute-done((bf16[2,256,256]{2,1,0:T(8,128)(2,1)S(1)}, bf16[2,256,256]{2,1,0:T(8,128)(2,1)S(1)}, u32[]{:S(2)}, u32[]{:S(2)}) %collective-permute-start.8) | collective-permute-done | bytes 262176 | tf_op jit(solution)/shard_map/ppermute | solution.py:31
  33.2 0.5 collective-permute-start.14
  33.7 0.7 copy-done.6
  34.4 0.5 collective-permute-start.5
  34.9 0.1 pad_add_fusion.place_ref
  35.0 0.0 collective-permute-start.17
  35.0 0.1 collective-permute-done.10.rest_3_
  35.1 0.4 collective-permute-start.15
  35.6 1.2 %copy-done.7 = bf16[2,256,256]{2,1,0:T(8,128)(2,1)S(1)} copy-done((bf16[2,256,256]{2,1,0:T(8,128)(2,1)S(1)}, bf16[2,256,256]{2,1,0:T(8,128)(2,1)}, u32[]{:S(2)}) %copy-start.7) | copy-done | bytes 262168
  36.8 1.8 %eval_begin.1.rest_8_ = f32[2,128,256]{2,1,0:T(8,128)S(1)} custom-call(s32[2]{0:T(128)S(1)} %pad_add_fusion.place_ref, bf16[128,4096]{1,0:T(8,128)(2,1)S(1)} %copy-done.4, bf16[128,4096]{1,0:T(8,128)(2,1)S(1)} %copy-done.5, bf16[2,256,256]{2,1,0:T(8,128)(2,1)S(1)} %pad_maximum_fusion.1.rest_0_, bf16[2,256,256]{2,1,0:T(8,128)(2,1)S(1)} %collective-permute-done.8.rest_1_, ...), custom_call_target="tpu_custom_call" | custom-call | flops 500000000 | bytes 4194304 | tf_op jit(solution)/shard_map/eval_begin/pallas_call | solution.py:228
  38.6 0.5 collective-permute-done.7.rest_5_.rest_13_
  39.1 3.7 %collective-permute-done.5.rest_1_.rest_9_ = bf16[2,256,256]{2,1,0:T(8,128)(2,1)} collective-permute-done((bf16[2,256,256]{2,1,0:T(8,128)(2,1)S(1)}, bf16[2,256,256]{2,1,0:T(8,128)(2,1)}, u32[]{:S(2)}, u32[]{:S(2)}) %collective-permute-start.5) | collective-permute-done | bytes 262176 | tf_op jit(solution)/shard_map/ppermute | solution.py:31
  42.7 0.5 collective-permute-start.18
  43.2 1.2 %collective-permute-done.16.rest_3_.rest_11_ = bf16[2,256,256]{2,1,0:T(8,128)(2,1)S(1)} collective-permute-done((bf16[2,256,256]{2,1,0:T(8,128)(2,1)}, bf16[2,256,256]{2,1,0:T(8,128)(2,1)S(1)}, u32[]{:S(2)}, u32[]{:S(2)}) %collective-permute-start.16) | collective-permute-done | bytes 262176 | tf_op jit(solution)/shard_map/ppermute | solution.py:31
  44.5 0.4 collective-permute-done.18.rest_7_.rest_15_
  44.9 2.1 %eval_factors.1 = bf16[1,288,256]{2,1,0:T(8,128)(2,1)S(1)} custom-call(s32[2]{0:T(128)S(1)} %pad_add_fusion.place_ref, bf16[128,4096]{1,0:T(8,128)(2,1)S(1)} %copy-done.4, bf16[128,4096]{1,0:T(8,128)(2,1)S(1)} %copy-done.5, f32[16,128]{1,0:T(8,128)S(1)} %fusion.hidden_ref, f32[16,128]{1,0:T(8,128)S(1)} %fusion.1.back_ref, s32[1,128]{1,0:T(1,128)S(1)} %copy-done.12, ...), custom_call_target="tpu_custom_call" | custom-call | flops 1000000000 | bytes 4194304 | tf_op jit(solution)/shard_map/eval_factors/pallas_call | solution.py:228
  46.9 2.6 %collective-permute-start.22 = (bf16[1,288,256]{2,1,0:T(8,128)(2,1)S(1)}, bf16[1,288,256]{2,1,0:T(8,128)(2,1)S(1)}, u32[]{:S(2)}, u32[]{:S(2)}) collective-permute-start(bf16[1,288,256]{2,1,0:T(8,128)(2,1)S(1)} %eval_factors.1), channel_id=1, source_target_pairs={{0,8},{1,9},{2,10},{3,11},{4,12},{5,13},{6,14},{7,15},{8,0},{9,1},... | collective-permute-start | bytes 442376 | tf_op jit(solution)/shard_map/ppermute | solution.py:31
  49.6 0.6 collective-permute-start.21
  50.2 1.0 %collective-permute-start.20 = (bf16[1,288,256]{2,1,0:T(8,128)(2,1)S(1)}, bf16[1,288,256]{2,1,0:T(8,128)(2,1)S(1)}, u32[]{:S(2)}, u32[]{:S(2)}) collective-permute-start(bf16[1,288,256]{2,1,0:T(8,128)(2,1)S(1)} %eval_factors.1), channel_id=1, source_target_pairs={{0,24},{1,25},{2,26},{3,27},{4,28},{5,29},{6,30},{7,31},{8,16},{9,... | collective-permute-start | bytes 442376 | tf_op jit(solution)/shard_map/ppermute | solution.py:31
  51.2 0.5 collective-permute-start.19
  51.7 4.1 %train_gradient_side.1 = (f32[512,256]{1,0:T(8,128)S(1)}, f32[32,1]{1,0:T(8,128)S(1)}) custom-call(s32[2]{0:T(128)S(1)} %pad_add_fusion.place_ref, bf16[512,4096]{1,0:T(8,128)(2,1)S(1)} %copy-done.2, f32[16,512]{1,0:T(8,128)S(1)} %copy-done.10, s32[1,512]{1,0:T(1,128)S(1)} %copy-done.11, bf16[2,256,256]{2,1,0:T(8,128)(2,1)S(1)} %pad_maximum_fusion.1.rest_0_, ...), custom_call_target="tpu_custom_call" | custom-call | flops 2000000000 | bytes 4194304 | tf_op jit(solution)/shard_map/train_gradient_side/pallas_call | solution.py:228
  55.9 1.3 %collective-permute-start.30 = (bf16[1,288,256]{2,1,0:T(8,128)(2,1)S(1)}, bf16[1,288,256]{2,1,0:T(8,128)(2,1)S(1)}, u32[]{:S(2)}, u32[]{:S(2)}) collective-permute-start(bf16[1,288,256]{2,1,0:T(8,128)(2,1)S(1)} %collective-permute-done.22), channel_id=1, source_target_pairs={{0,4},{1,5},{2,6},{3,7},{4,0},{5,1},{6,2},{7,3},{8,12},{9,13},{10,... | collective-permute-start | bytes 442376 | tf_op jit(solution)/shard_map/ppermute | solution.py:31
  57.2 4.3 %train_input_side.1.feats_ref = bf16[2,512,256]{2,1,0:T(8,128)(2,1)S(1)} custom-call(s32[2]{0:T(128)S(1)} %pad_add_fusion.place_ref, bf16[512,4096]{1,0:T(8,128)(2,1)S(1)} %copy-done.3, f32[16,512]{1,0:T(8,128)S(1)} %copy-done.9, s32[1,512]{1,0:T(1,128)S(1)} %copy-done.11, bf16[2,256,256]{2,1,0:T(8,128)(2,1)S(1)} %pad_maximum_fusion.1.rest_0_, ...), custom_call_target="tpu_custom_call" | custom-call | flops 2000000000 | bytes 4194304 | tf_op jit(solution)/shard_map/train_input_side/pallas_call | solution.py:228
  61.4 3.3 %collective-permute-done.19 = bf16[1,288,256]{2,1,0:T(8,128)(2,1)S(1)} collective-permute-done((bf16[1,288,256]{2,1,0:T(8,128)(2,1)S(1)}, bf16[1,288,256]{2,1,0:T(8,128)(2,1)S(1)}, u32[]{:S(2)}, u32[]{:S(2)}) %collective-permute-start.19) | collective-permute-done | bytes 147488 | tf_op jit(solution)/shard_map/ppermute | solution.py:31
  64.8 1.4 %collective-permute-start.23 = (bf16[1,288,256]{2,1,0:T(8,128)(2,1)S(1)}, bf16[1,288,256]{2,1,0:T(8,128)(2,1)S(1)}, u32[]{:S(2)}, u32[]{:S(2)}) collective-permute-start(bf16[1,288,256]{2,1,0:T(8,128)(2,1)S(1)} %collective-permute-done.19), channel_id=1, source_target_pairs={{0,2},{1,3},{2,0},{3,1},{4,6},{5,7},{6,4},{7,5},{8,10},{9,11},{10,... | collective-permute-start | bytes 442376 | tf_op jit(solution)/shard_map/ppermute | solution.py:31
  66.2 0.5 collective-permute-start.25
  66.8 1.5 %collective-permute-start.27 = (bf16[2,288,256]{2,1,0:T(8,128)(2,1)S(1)}, bf16[2,288,256]{2,1,0:T(8,128)(2,1)S(1)}, u32[]{:S(2)}, u32[]{:S(2)}) collective-permute-start(bf16[2,288,256]{2,1,0:T(8,128)(2,1)S(1)} %pad_maximum_fusion.rest_0_), channel_id=1, source_target_pairs={{0,4},{1,5},{2,6},{3,7},{4,0},{5,1},{6,2},{7,3},{8,12},{9,13},{10,... | collective-permute-start | bytes 884744 | tf_op jit(solution)/shard_map/ppermute | solution.py:31
  68.3 0.7 collective-permute-start.31
  69.0 0.1 collective-permute-start.28
  69.1 3.9 %collective-permute-done.25 = bf16[1,288,256]{2,1,0:T(8,128)(2,1)S(1)} collective-permute-done((bf16[1,288,256]{2,1,0:T(8,128)(2,1)S(1)}, bf16[1,288,256]{2,1,0:T(8,128)(2,1)S(1)}, u32[]{:S(2)}, u32[]{:S(2)}) %collective-permute-start.25) | collective-permute-done | bytes 147488 | tf_op jit(solution)/shard_map/ppermute | solution.py:31
  73.0 0.7 collective-permute-start.26
  73.7 3.3 %collective-permute-done.27.rest_1_ = bf16[2,288,256]{2,1,0:T(8,128)(2,1)S(1)} collective-permute-done((bf16[2,288,256]{2,1,0:T(8,128)(2,1)S(1)}, bf16[2,288,256]{2,1,0:T(8,128)(2,1)S(1)}, u32[]{:S(2)}, u32[]{:S(2)}) %collective-permute-start.27) | collective-permute-done | bytes 294944 | tf_op jit(solution)/shard_map/ppermute | solution.py:31
  77.0 0.5 collective-permute-start.33
  77.5 0.6 collective-permute-start.24
  78.2 0.2 collective-permute-start.36
  78.4 0.2 collective-permute-done.29.rest_3_
  78.6 0.1 collective-permute-start.34
  78.7 0.3 collective-permute-done.33.rest_7_
  79.0 3.7 %front_tiles.1.rest_8_ = f32[32,16,32]{2,1,0:T(8,128)S(1)} custom-call(s32[2]{0:T(128)S(1)} %pad_add_fusion.place_ref, bf16[2,512,256]{2,1,0:T(8,128)(2,1)S(1)} %train_input_side.1.feats_ref, bf16[2,288,256]{2,1,0:T(8,128)(2,1)S(1)} %pad_maximum_fusion.rest_0_, bf16[2,288,256]{2,1,0:T(8,128)(2,1)S(1)} %collective-permute-done.27.rest_1_, ...), custom_call_target="tpu_custom_call" | custom-call | flops 1000000000 | bytes 4194304 | tf_op jit(solution)/shard_map/front_tiles/pallas_call | solution.py:228
  82.7 3.9 %collective-permute-done.24.rest_1_ = bf16[2,288,256]{2,1,0:T(8,128)(2,1)S(1)} collective-permute-done((bf16[2,288,256]{2,1,0:T(8,128)(2,1)S(1)}, bf16[2,288,256]{2,1,0:T(8,128)(2,1)S(1)}, u32[]{:S(2)}, u32[]{:S(2)}) %collective-permute-start.24) | collective-permute-done | bytes 294944 | tf_op jit(solution)/shard_map/ppermute | solution.py:31
  86.5 0.5 collective-permute-start.37
  87.0 1.1 %collective-permute-done.35.rest_3_ = bf16[2,288,256]{2,1,0:T(8,128)(2,1)S(1)} collective-permute-done((bf16[2,288,256]{2,1,0:T(8,128)(2,1)S(1)}, bf16[2,288,256]{2,1,0:T(8,128)(2,1)S(1)}, u32[]{:S(2)}, u32[]{:S(2)}) %collective-permute-start.35) | collective-permute-done | bytes 294944 | tf_op jit(solution)/shard_map/ppermute | solution.py:31
  88.1 0.4 collective-permute-done.37.rest_7_
  88.5 4.8 %score_tiles.1 = f32[1,16,16,32]{3,2,1,0:T(8,128)} custom-call(s32[2]{0:T(128)S(1)} %pad_add_fusion.place_ref, s32[16]{0:T(128)S(1)} %copy-done.13, s32[1]{0:T(128)} %dynamic_slice.9.live_ref, bf16[2,512,256]{2,1,0:T(8,128)(2,1)S(1)} %train_input_side.1.feats_ref, bf16[2,288,256]{2,1,0:T(8,128)(2,1)S(1)} %constant_dynamic-update-slice_fusion.6.rest_0_, ...), custom_call_target="tpu_custom_call" | custom-call | flops 1000000000 | bytes 4194304 | tf_op jit(solution)/shard_map/score_tiles/pallas_call | solution.py:228
  (70 shorter events, 0.3 us)
Async XLA Ops:
  0.0 11.2 %copy-start = (bf16[4096,16]{0,1:T(8,128)(2,1)S(1)}, bf16[4096,16]{0,1:T(8,128)(2,1)}, u32[]{:S(2)}) copy-start(bf16[4096,16]{0,1:T(8,128)(2,1)} %param.18) | copy-start | bytes 393220
  0.0 20.3 %copy-start.14 = (bf16[16,4096]{1,0:T(8,128)(2,1)S(1)}, bf16[16,4096]{1,0:T(8,128)(2,1)}, u32[]{:S(2)}) copy-start(bf16[16,4096]{1,0:T(8,128)(2,1)} %param.19) | copy-start | bytes 393220
  0.9 21.2 %collective-permute-start.3 = (bf16[1,256,256]{2,1,0:T(8,128)(2,1)S(1)}, bf16[1,256,256]{2,1,0:T(8,128)(2,1)}, u32[]{:S(2)}, u32[]{:S(2)}) collective-permute-start(bf16[1,256,256]{2,1,0:T(8,128)(2,1)S(1)} %maximum_bitcast_fusion), channel_id=1, source_target_pairs={{0,24},{1,25},{2,26},{3,27},{4,28},{5,29},{6,30},{7,31},{8,16},{9,... | collective-permute-start | bytes 393224 | tf_op jit(solution)/shard_map/ppermute | solution.py:31
  6.0 16.1 %collective-permute-start.2 = (bf16[1,256,256]{2,1,0:T(8,128)(2,1)S(1)}, bf16[1,256,256]{2,1,0:T(8,128)(2,1)}, u32[]{:S(2)}, u32[]{:S(2)}) collective-permute-start(bf16[1,256,256]{2,1,0:T(8,128)(2,1)S(1)} %maximum_bitcast_fusion), channel_id=1, source_target_pairs={{0,16},{1,17},{2,18},{3,19},{4,20},{5,21},{6,22},{7,23},{8,24},{9,... | collective-permute-start | bytes 393224 | tf_op jit(solution)/shard_map/ppermute | solution.py:31
  6.0 8.5 %collective-permute-start.1 = (bf16[1,256,256]{2,1,0:T(8,128)(2,1)S(1)}, bf16[1,256,256]{2,1,0:T(8,128)(2,1)S(1)}, u32[]{:S(2)}, u32[]{:S(2)}) collective-permute-start(bf16[1,256,256]{2,1,0:T(8,128)(2,1)S(1)} %maximum_bitcast_fusion), channel_id=1, source_target_pairs={{0,8},{1,9},{2,10},{3,11},{4,12},{5,13},{6,14},{7,15},{8,0},{9,1},... | collective-permute-start | bytes 393224 | tf_op jit(solution)/shard_map/ppermute | solution.py:31
  6.7 7.9 %collective-permute-start = (bf16[1,256,256]{2,1,0:T(8,128)(2,1)S(1)}, bf16[1,256,256]{2,1,0:T(8,128)(2,1)S(1)}, u32[]{:S(2)}, u32[]{:S(2)}) collective-permute-start(bf16[1,256,256]{2,1,0:T(8,128)(2,1)S(1)} %maximum_bitcast_fusion), channel_id=1, source_target_pairs={{0,2},{1,3},{2,0},{3,1},{4,6},{5,7},{6,4},{7,5},{8,10},{9,11},{10,... | collective-permute-start | bytes 393224 | tf_op jit(solution)/shard_map/ppermute | solution.py:31
  8.3 12.0 %copy-start.1 = (bf16[512,4096]{1,0:T(8,128)(2,1)S(1)}, bf16[512,4096]{1,0:T(8,128)(2,1)}, u32[]{:S(2)}) copy-start(bf16[512,4096]{1,0:T(8,128)(2,1)} %act_ref.2) | copy-start | bytes 12582916
  14.6 20.9 %copy-start.4 = (bf16[128,4096]{1,0:T(8,128)(2,1)S(1)}, bf16[128,4096]{1,0:T(8,128)(2,1)}, u32[]{:S(2)}) copy-start(bf16[128,4096]{1,0:T(8,128)(2,1)} %x_ref.3) | copy-start | bytes 3145732
  14.6 20.9 %copy-start.5 = (bf16[128,4096]{1,0:T(8,128)(2,1)S(1)}, bf16[128,4096]{1,0:T(8,128)(2,1)}, u32[]{:S(2)}) copy-start(bf16[128,4096]{1,0:T(8,128)(2,1)} %g_ref.3) | copy-start | bytes 3145732
  18.8 6.8 %collective-permute-start.11 = (bf16[1,256,256]{2,1,0:T(8,128)(2,1)S(1)}, bf16[1,256,256]{2,1,0:T(8,128)(2,1)S(1)}, u32[]{:S(2)}, u32[]{:S(2)}) collective-permute-start(bf16[1,256,256]{2,1,0:T(8,128)(2,1)S(1)} %collective-permute-done.1), channel_id=1, source_target_pairs={{0,4},{1,5},{2,6},{3,7},{4,0},{5,1},{6,2},{7,3},{8,12},{9,13},{10,... | collective-permute-start | bytes 393224 | tf_op jit(solution)/shard_map/ppermute | solution.py:31
  22.1 8.1 %collective-permute-start.4 = (bf16[1,256,256]{2,1,0:T(8,128)(2,1)}, bf16[1,256,256]{2,1,0:T(8,128)(2,1)S(1)}, u32[]{:S(2)}, u32[]{:S(2)}) collective-permute-start(bf16[1,256,256]{2,1,0:T(8,128)(2,1)} %collective-permute-done.2), channel_id=1, source_target_pairs={{0,2},{1,3},{2,0},{3,1},{4,6},{5,7},{6,4},{7,5},{8,10},{9,11},{10,... | collective-permute-start | bytes 393224 | tf_op jit(solution)/shard_map/ppermute | solution.py:31
  23.5 6.6 %collective-permute-start.6 = (bf16[1,256,256]{2,1,0:T(8,128)(2,1)}, bf16[1,256,256]{2,1,0:T(8,128)(2,1)S(1)}, u32[]{:S(2)}, u32[]{:S(2)}) collective-permute-start(bf16[1,256,256]{2,1,0:T(8,128)(2,1)} %collective-permute-done.3), channel_id=1, source_target_pairs={{0,4},{1,5},{2,6},{3,7},{4,0},{5,1},{6,2},{7,3},{8,12},{9,13},{10,... | collective-permute-start | bytes 393224 | tf_op jit(solution)/shard_map/ppermute | solution.py:31
  24.0 9.2 %collective-permute-start.8 = (bf16[2,256,256]{2,1,0:T(8,128)(2,1)S(1)}, bf16[2,256,256]{2,1,0:T(8,128)(2,1)S(1)}, u32[]{:S(2)}, u32[]{:S(2)}) collective-permute-start(bf16[2,256,256]{2,1,0:T(8,128)(2,1)S(1)} %pad_maximum_fusion.1.rest_0_), channel_id=1, source_target_pairs={{0,4},{1,5},{2,6},{3,7},{4,0},{5,1},{6,2},{7,3},{8,12},{9,13},{10,... | collective-permute-start | bytes 786440 | tf_op jit(solution)/shard_map/ppermute | solution.py:31
  25.6 7.6 %collective-permute-start.12 = (bf16[2,256,256]{2,1,0:T(8,128)(2,1)S(1)}, bf16[2,256,256]{2,1,0:T(8,128)(2,1)}, u32[]{:S(2)}, u32[]{:S(2)}) collective-permute-start(bf16[2,256,256]{2,1,0:T(8,128)(2,1)S(1)} %constant_dynamic-update-slice_fusion.4.rest_4_), channel_id=1, source_target_pairs={{0,2},{1,3},{2,0},{3,1},{4,6},{5,7},{6,4},{7,5},{8,10},{9,11},{10,... | collective-permute-start | bytes 786440 | tf_op jit(solution)/shard_map/ppermute | solution.py:31
  27.2 6.5 %collective-permute-start.9 = (bf16[2,256,256]{2,1,0:T(8,128)(2,1)S(1)}, bf16[2,256,256]{2,1,0:T(8,128)(2,1)S(1)}, u32[]{:S(2)}, u32[]{:S(2)}) collective-permute-start(bf16[2,256,256]{2,1,0:T(8,128)(2,1)S(1)} %pad_maximum_fusion.1.rest_0_), channel_id=1, source_target_pairs={{0,1},{1,0},{2,3},{3,2},{4,5},{5,4},{6,7},{7,6},{8,9},{9,8},{10,11... | collective-permute-start | bytes 786440 | tf_op jit(solution)/shard_map/ppermute | solution.py:31
  30.1 4.9 %collective-permute-start.13 = (bf16[2,256,256]{2,1,0:T(8,128)(2,1)S(1)}, bf16[2,256,256]{2,1,0:T(8,128)(2,1)}, u32[]{:S(2)}, u32[]{:S(2)}) collective-permute-start(bf16[2,256,256]{2,1,0:T(8,128)(2,1)S(1)} %constant_dynamic-update-slice_fusion.4.rest_4_), channel_id=1, source_target_pairs={{0,1},{1,0},{2,3},{3,2},{4,5},{5,4},{6,7},{7,6},{8,9},{9,8},{10,11... | collective-permute-start | bytes 786440 | tf_op jit(solution)/shard_map/ppermute | solution.py:31
  30.2 8.9 %collective-permute-start.7 = (bf16[2,256,256]{2,1,0:T(8,128)(2,1)S(1)}, bf16[2,256,256]{2,1,0:T(8,128)(2,1)}, u32[]{:S(2)}, u32[]{:S(2)}) collective-permute-start(bf16[2,256,256]{2,1,0:T(8,128)(2,1)S(1)} %constant_dynamic-update-slice_fusion.2.rest_4_.rest_12_), channel_id=1, source_target_pairs={{0,2},{1,3},{2,0},{3,1},{4,6},{5,7},{6,4},{7,5},{8,10},{9,11},{10,... | collective-permute-start | bytes 786440 | tf_op jit(solution)/shard_map/ppermute | solution.py:31
  33.2 2.0 %collective-permute-start.10 = (bf16[2,256,256]{2,1,0:T(8,128)(2,1)S(1)}, bf16[2,256,256]{2,1,0:T(8,128)(2,1)}, u32[]{:S(2)}, u32[]{:S(2)}) collective-permute-start(bf16[2,256,256]{2,1,0:T(8,128)(2,1)S(1)} %collective-permute-done.8.rest_1_), channel_id=1, source_target_pairs={{0,1},{1,0},{2,3},{3,2},{4,5},{5,4},{6,7},{7,6},{8,9},{9,8},{10,11... | collective-permute-start | bytes 786440 | tf_op jit(solution)/shard_map/ppermute | solution.py:31
  33.2 2.4 %collective-permute-start.14 = (bf16[2,256,256]{2,1,0:T(8,128)(2,1)}, bf16[2,256,256]{2,1,0:T(8,128)(2,1)}, u32[]{:S(2)}, u32[]{:S(2)}) collective-permute-start(bf16[2,256,256]{2,1,0:T(8,128)(2,1)} %collective-permute-done.12.rest_5_), channel_id=1, source_target_pairs={{0,1},{1,0},{2,3},{3,2},{4,5},{5,4},{6,7},{7,6},{8,9},{9,8},{10,11... | collective-permute-start | bytes 786440 | tf_op jit(solution)/shard_map/ppermute | solution.py:31
  33.7 0.7 copy-start.6
  34.4 8.3 %collective-permute-start.5 = (bf16[2,256,256]{2,1,0:T(8,128)(2,1)S(1)}, bf16[2,256,256]{2,1,0:T(8,128)(2,1)}, u32[]{:S(2)}, u32[]{:S(2)}) collective-permute-start(bf16[2,256,256]{2,1,0:T(8,128)(2,1)S(1)} %constant_dynamic-update-slice_fusion.rest_0_.rest_8_), channel_id=1, source_target_pairs={{0,4},{1,5},{2,6},{3,7},{4,0},{5,1},{6,2},{7,3},{8,12},{9,13},{10,... | collective-permute-start | bytes 786440 | tf_op jit(solution)/shard_map/ppermute | solution.py:31
  34.9 9.9 %copy-start.12 = (s32[1,128]{1,0:T(1,128)S(1)}, s32[1,128]{1,0:T(1,128)}, u32[]{:S(2)}) copy-start(s32[1,128]{1,0:T(1,128)} %index_ref.3) | copy-start | bytes 1540
  34.9 16.8 %copy-start.11 = (s32[1,512]{1,0:T(1,128)S(1)}, s32[1,512]{1,0:T(1,128)}, u32[]{:S(2)}) copy-start(s32[1,512]{1,0:T(1,128)} %index_ref.5) | copy-start | bytes 6148
  35.0 16.7 %copy-start.2 = (bf16[512,4096]{1,0:T(8,128)(2,1)S(1)}, bf16[512,4096]{1,0:T(8,128)(2,1)}, u32[]{:S(2)}) copy-start(bf16[512,4096]{1,0:T(8,128)(2,1)} %act_ref.2) | copy-start | bytes 12582916
  35.0 8.2 %collective-permute-start.17 = (bf16[2,256,256]{2,1,0:T(8,128)(2,1)S(1)}, bf16[2,256,256]{2,1,0:T(8,128)(2,1)S(1)}, u32[]{:S(2)}, u32[]{:S(2)}) collective-permute-start(bf16[2,256,256]{2,1,0:T(8,128)(2,1)S(1)} %constant_dynamic-update-slice_fusion.2.rest_4_.rest_12_), channel_id=1, source_target_pairs={{0,1},{1,0},{2,3},{3,2},{4,5},{5,4},{6,7},{7,6},{8,9},{9,8},{10,11... | collective-permute-start | bytes 786440 | tf_op jit(solution)/shard_map/ppermute | solution.py:31
  35.1 8.1 %collective-permute-start.15 = (bf16[2,256,256]{2,1,0:T(8,128)(2,1)S(1)}, bf16[2,256,256]{2,1,0:T(8,128)(2,1)S(1)}, u32[]{:S(2)}, u32[]{:S(2)}) collective-permute-start(bf16[2,256,256]{2,1,0:T(8,128)(2,1)S(1)} %constant_dynamic-update-slice_fusion.rest_0_.rest_8_), channel_id=1, source_target_pairs={{0,1},{1,0},{2,3},{3,2},{4,5},{5,4},{6,7},{7,6},{8,9},{9,8},{10,11... | collective-permute-start | bytes 786440 | tf_op jit(solution)/shard_map/ppermute | solution.py:31
  35.5 1.2 %copy-start.7 = (bf16[2,256,256]{2,1,0:T(8,128)(2,1)S(1)}, bf16[2,256,256]{2,1,0:T(8,128)(2,1)}, u32[]{:S(2)}) copy-start(bf16[2,256,256]{2,1,0:T(8,128)(2,1)} %copy-done.6) | copy-start | bytes 786436
  36.8 15.0 %copy-start.8 = (bf16[2,256,256]{2,1,0:T(8,128)(2,1)S(1)}, bf16[2,256,256]{2,1,0:T(8,128)(2,1)}, u32[]{:S(2)}) copy-start(bf16[2,256,256]{2,1,0:T(8,128)(2,1)} %copy-done.6) | copy-start | bytes 786436
  36.8 15.0 %copy-start.10 = (f32[16,512]{1,0:T(8,128)S(1)}, f32[16,512]{1,0:T(8,128)}, u32[]{:S(2)}) copy-start(f32[16,512]{1,0:T(8,128)} %convolution_bitcast_fusion.1.factor_ref) | copy-start | bytes 98308
  42.7 1.7 %collective-permute-start.16 = (bf16[2,256,256]{2,1,0:T(8,128)(2,1)}, bf16[2,256,256]{2,1,0:T(8,128)(2,1)S(1)}, u32[]{:S(2)}, u32[]{:S(2)}) collective-permute-start(bf16[2,256,256]{2,1,0:T(8,128)(2,1)} %collective-permute-done.5.rest_1_.rest_9_), channel_id=1, source_target_pairs={{0,1},{1,0},{2,3},{3,2},{4,5},{5,4},{6,7},{7,6},{8,9},{9,8},{10,11... | collective-permute-start | bytes 786440 | tf_op jit(solution)/shard_map/ppermute | solution.py:31
  42.7 2.1 %collective-permute-start.18 = (bf16[2,256,256]{2,1,0:T(8,128)(2,1)}, bf16[2,256,256]{2,1,0:T(8,128)(2,1)S(1)}, u32[]{:S(2)}, u32[]{:S(2)}) collective-permute-start(bf16[2,256,256]{2,1,0:T(8,128)(2,1)} %collective-permute-done.7.rest_5_.rest_13_), channel_id=1, source_target_pairs={{0,1},{1,0},{2,3},{3,2},{4,5},{5,4},{6,7},{7,6},{8,9},{9,8},{10,11... | collective-permute-start | bytes 786440 | tf_op jit(solution)/shard_map/ppermute | solution.py:31
  46.9 10.2 %copy-start.3 = (bf16[512,4096]{1,0:T(8,128)(2,1)S(1)}, bf16[512,4096]{1,0:T(8,128)(2,1)}, u32[]{:S(2)}) copy-start(bf16[512,4096]{1,0:T(8,128)(2,1)} %act_ref.3) | copy-start | bytes 12582916
  46.9 10.2 %copy-start.9 = (f32[16,512]{1,0:T(8,128)S(1)}, f32[16,512]{1,0:T(8,128)}, u32[]{:S(2)}) copy-start(f32[16,512]{1,0:T(8,128)} %convolution_bitcast_fusion.factor_ref) | copy-start | bytes 98308
  46.9 8.9 %collective-permute-start.22 = (bf16[1,288,256]{2,1,0:T(8,128)(2,1)S(1)}, bf16[1,288,256]{2,1,0:T(8,128)(2,1)S(1)}, u32[]{:S(2)}, u32[]{:S(2)}) collective-permute-start(bf16[1,288,256]{2,1,0:T(8,128)(2,1)S(1)} %eval_factors.1), channel_id=1, source_target_pairs={{0,8},{1,9},{2,10},{3,11},{4,12},{5,13},{6,14},{7,15},{8,0},{9,1},... | collective-permute-start | bytes 442376 | tf_op jit(solution)/shard_map/ppermute | solution.py:31
  49.6 6.2 %collective-permute-start.21 = (bf16[1,288,256]{2,1,0:T(8,128)(2,1)S(1)}, bf16[1,288,256]{2,1,0:T(8,128)(2,1)S(1)}, u32[]{:S(2)}, u32[]{:S(2)}) collective-permute-start(bf16[1,288,256]{2,1,0:T(8,128)(2,1)S(1)} %eval_factors.1), channel_id=1, source_target_pairs={{0,2},{1,3},{2,0},{3,1},{4,6},{5,7},{6,4},{7,5},{8,10},{9,11},{10,... | collective-permute-start | bytes 442376 | tf_op jit(solution)/shard_map/ppermute | solution.py:31
  50.2 11.3 %collective-permute-start.20 = (bf16[1,288,256]{2,1,0:T(8,128)(2,1)S(1)}, bf16[1,288,256]{2,1,0:T(8,128)(2,1)S(1)}, u32[]{:S(2)}, u32[]{:S(2)}) collective-permute-start(bf16[1,288,256]{2,1,0:T(8,128)(2,1)S(1)} %eval_factors.1), channel_id=1, source_target_pairs={{0,24},{1,25},{2,26},{3,27},{4,28},{5,29},{6,30},{7,31},{8,16},{9,... | collective-permute-start | bytes 442376 | tf_op jit(solution)/shard_map/ppermute | solution.py:31
  51.2 13.6 %collective-permute-start.19 = (bf16[1,288,256]{2,1,0:T(8,128)(2,1)S(1)}, bf16[1,288,256]{2,1,0:T(8,128)(2,1)S(1)}, u32[]{:S(2)}, u32[]{:S(2)}) collective-permute-start(bf16[1,288,256]{2,1,0:T(8,128)(2,1)S(1)} %eval_factors.1), channel_id=1, source_target_pairs={{0,16},{1,17},{2,18},{3,19},{4,20},{5,21},{6,22},{7,23},{8,24},{9,... | collective-permute-start | bytes 442376 | tf_op jit(solution)/shard_map/ppermute | solution.py:31
  55.9 12.4 %collective-permute-start.30 = (bf16[1,288,256]{2,1,0:T(8,128)(2,1)S(1)}, bf16[1,288,256]{2,1,0:T(8,128)(2,1)S(1)}, u32[]{:S(2)}, u32[]{:S(2)}) collective-permute-start(bf16[1,288,256]{2,1,0:T(8,128)(2,1)S(1)} %collective-permute-done.22), channel_id=1, source_target_pairs={{0,4},{1,5},{2,6},{3,7},{4,0},{5,1},{6,2},{7,3},{8,12},{9,13},{10,... | collective-permute-start | bytes 442376 | tf_op jit(solution)/shard_map/ppermute | solution.py:31
  61.4 27.1 %copy-start.13 = (s32[16]{0:T(128)S(1)}, s32[16]{0:T(128)}, u32[]{:S(2)}) copy-start(s32[16]{0:T(128)} %dynamic-slice_reduce_fusion.chosen_ref) | copy-start | bytes 196
  64.8 8.2 %collective-permute-start.23 = (bf16[1,288,256]{2,1,0:T(8,128)(2,1)S(1)}, bf16[1,288,256]{2,1,0:T(8,128)(2,1)S(1)}, u32[]{:S(2)}, u32[]{:S(2)}) collective-permute-start(bf16[1,288,256]{2,1,0:T(8,128)(2,1)S(1)} %collective-permute-done.19), channel_id=1, source_target_pairs={{0,2},{1,3},{2,0},{3,1},{4,6},{5,7},{6,4},{7,5},{8,10},{9,11},{10,... | collective-permute-start | bytes 442376 | tf_op jit(solution)/shard_map/ppermute | solution.py:31
  66.2 6.8 %collective-permute-start.25 = (bf16[1,288,256]{2,1,0:T(8,128)(2,1)S(1)}, bf16[1,288,256]{2,1,0:T(8,128)(2,1)S(1)}, u32[]{:S(2)}, u32[]{:S(2)}) collective-permute-start(bf16[1,288,256]{2,1,0:T(8,128)(2,1)S(1)} %collective-permute-done.20), channel_id=1, source_target_pairs={{0,4},{1,5},{2,6},{3,7},{4,0},{5,1},{6,2},{7,3},{8,12},{9,13},{10,... | collective-permute-start | bytes 442376 | tf_op jit(solution)/shard_map/ppermute | solution.py:31
  66.8 10.2 %collective-permute-start.27 = (bf16[2,288,256]{2,1,0:T(8,128)(2,1)S(1)}, bf16[2,288,256]{2,1,0:T(8,128)(2,1)S(1)}, u32[]{:S(2)}, u32[]{:S(2)}) collective-permute-start(bf16[2,288,256]{2,1,0:T(8,128)(2,1)S(1)} %pad_maximum_fusion.rest_0_), channel_id=1, source_target_pairs={{0,4},{1,5},{2,6},{3,7},{4,0},{5,1},{6,2},{7,3},{8,12},{9,13},{10,... | collective-permute-start | bytes 884744 | tf_op jit(solution)/shard_map/ppermute | solution.py:31
  68.3 8.7 %collective-permute-start.31 = (bf16[2,288,256]{2,1,0:T(8,128)(2,1)S(1)}, bf16[2,288,256]{2,1,0:T(8,128)(2,1)S(1)}, u32[]{:S(2)}, u32[]{:S(2)}) collective-permute-start(bf16[2,288,256]{2,1,0:T(8,128)(2,1)S(1)} %constant_dynamic-update-slice_fusion.10.rest_4_), channel_id=1, source_target_pairs={{0,2},{1,3},{2,0},{3,1},{4,6},{5,7},{6,4},{7,5},{8,10},{9,11},{10,... | collective-permute-start | bytes 884744 | tf_op jit(solution)/shard_map/ppermute | solution.py:31
  69.0 8.6 %collective-permute-start.28 = (bf16[2,288,256]{2,1,0:T(8,128)(2,1)S(1)}, bf16[2,288,256]{2,1,0:T(8,128)(2,1)S(1)}, u32[]{:S(2)}, u32[]{:S(2)}) collective-permute-start(bf16[2,288,256]{2,1,0:T(8,128)(2,1)S(1)} %pad_maximum_fusion.rest_0_), channel_id=1, source_target_pairs={{0,1},{1,0},{2,3},{3,2},{4,5},{5,4},{6,7},{7,6},{8,9},{9,8},{10,11... | collective-permute-start | bytes 884744 | tf_op jit(solution)/shard_map/ppermute | solution.py:31
  73.0 5.2 %collective-permute-start.32 = (bf16[2,288,256]{2,1,0:T(8,128)(2,1)S(1)}, bf16[2,288,256]{2,1,0:T(8,128)(2,1)S(1)}, u32[]{:S(2)}, u32[]{:S(2)}) collective-permute-start(bf16[2,288,256]{2,1,0:T(8,128)(2,1)S(1)} %constant_dynamic-update-slice_fusion.10.rest_4_), channel_id=1, source_target_pairs={{0,1},{1,0},{2,3},{3,2},{4,5},{5,4},{6,7},{7,6},{8,9},{9,8},{10,11... | collective-permute-start | bytes 884744 | tf_op jit(solution)/shard_map/ppermute | solution.py:31
  73.0 9.6 %collective-permute-start.26 = (bf16[2,288,256]{2,1,0:T(8,128)(2,1)S(1)}, bf16[2,288,256]{2,1,0:T(8,128)(2,1)S(1)}, u32[]{:S(2)}, u32[]{:S(2)}) collective-permute-start(bf16[2,288,256]{2,1,0:T(8,128)(2,1)S(1)} %constant_dynamic-update-slice_fusion.8.rest_4_), channel_id=1, source_target_pairs={{0,2},{1,3},{2,0},{3,1},{4,6},{5,7},{6,4},{7,5},{8,10},{9,11},{10,... | collective-permute-start | bytes 884744 | tf_op jit(solution)/shard_map/ppermute | solution.py:31
  77.0 1.6 %collective-permute-start.29 = (bf16[2,288,256]{2,1,0:T(8,128)(2,1)S(1)}, bf16[2,288,256]{2,1,0:T(8,128)(2,1)S(1)}, u32[]{:S(2)}, u32[]{:S(2)}) collective-permute-start(bf16[2,288,256]{2,1,0:T(8,128)(2,1)S(1)} %collective-permute-done.27.rest_1_), channel_id=1, source_target_pairs={{0,1},{1,0},{2,3},{3,2},{4,5},{5,4},{6,7},{7,6},{8,9},{9,8},{10,11... | collective-permute-start | bytes 884744 | tf_op jit(solution)/shard_map/ppermute | solution.py:31
  77.0 2.0 %collective-permute-start.33 = (bf16[2,288,256]{2,1,0:T(8,128)(2,1)S(1)}, bf16[2,288,256]{2,1,0:T(8,128)(2,1)S(1)}, u32[]{:S(2)}, u32[]{:S(2)}) collective-permute-start(bf16[2,288,256]{2,1,0:T(8,128)(2,1)S(1)} %collective-permute-done.31.rest_5_), channel_id=1, source_target_pairs={{0,1},{1,0},{2,3},{3,2},{4,5},{5,4},{6,7},{7,6},{8,9},{9,8},{10,11... | collective-permute-start | bytes 884744 | tf_op jit(solution)/shard_map/ppermute | solution.py:31
  77.5 9.0 %collective-permute-start.24 = (bf16[2,288,256]{2,1,0:T(8,128)(2,1)S(1)}, bf16[2,288,256]{2,1,0:T(8,128)(2,1)S(1)}, u32[]{:S(2)}, u32[]{:S(2)}) collective-permute-start(bf16[2,288,256]{2,1,0:T(8,128)(2,1)S(1)} %constant_dynamic-update-slice_fusion.6.rest_0_), channel_id=1, source_target_pairs={{0,4},{1,5},{2,6},{3,7},{4,0},{5,1},{6,2},{7,3},{8,12},{9,13},{10,... | collective-permute-start | bytes 884744 | tf_op jit(solution)/shard_map/ppermute | solution.py:31
  78.2 8.9 %collective-permute-start.36 = (bf16[2,288,256]{2,1,0:T(8,128)(2,1)S(1)}, bf16[2,288,256]{2,1,0:T(8,128)(2,1)S(1)}, u32[]{:S(2)}, u32[]{:S(2)}) collective-permute-start(bf16[2,288,256]{2,1,0:T(8,128)(2,1)S(1)} %constant_dynamic-update-slice_fusion.8.rest_4_), channel_id=1, source_target_pairs={{0,1},{1,0},{2,3},{3,2},{4,5},{5,4},{6,7},{7,6},{8,9},{9,8},{10,11... | collective-permute-start | bytes 884744 | tf_op jit(solution)/shard_map/ppermute | solution.py:31
  78.6 8.5 %collective-permute-start.34 = (bf16[2,288,256]{2,1,0:T(8,128)(2,1)S(1)}, bf16[2,288,256]{2,1,0:T(8,128)(2,1)S(1)}, u32[]{:S(2)}, u32[]{:S(2)}) collective-permute-start(bf16[2,288,256]{2,1,0:T(8,128)(2,1)S(1)} %constant_dynamic-update-slice_fusion.6.rest_0_), channel_id=1, source_target_pairs={{0,1},{1,0},{2,3},{3,2},{4,5},{5,4},{6,7},{7,6},{8,9},{9,8},{10,11... | collective-permute-start | bytes 884744 | tf_op jit(solution)/shard_map/ppermute | solution.py:31
  86.5 1.6 %collective-permute-start.35 = (bf16[2,288,256]{2,1,0:T(8,128)(2,1)S(1)}, bf16[2,288,256]{2,1,0:T(8,128)(2,1)S(1)}, u32[]{:S(2)}, u32[]{:S(2)}) collective-permute-start(bf16[2,288,256]{2,1,0:T(8,128)(2,1)S(1)} %collective-permute-done.24.rest_1_), channel_id=1, source_target_pairs={{0,1},{1,0},{2,3},{3,2},{4,5},{5,4},{6,7},{7,6},{8,9},{9,8},{10,11... | collective-permute-start | bytes 884744 | tf_op jit(solution)/shard_map/ppermute | solution.py:31
  86.5 2.0 %collective-permute-start.37 = (bf16[2,288,256]{2,1,0:T(8,128)(2,1)S(1)}, bf16[2,288,256]{2,1,0:T(8,128)(2,1)S(1)}, u32[]{:S(2)}, u32[]{:S(2)}) collective-permute-start(bf16[2,288,256]{2,1,0:T(8,128)(2,1)S(1)} %collective-permute-done.26.rest_5_), channel_id=1, source_target_pairs={{0,1},{1,0},{2,3},{3,2},{4,5},{5,4},{6,7},{7,6},{8,9},{9,8},{10,11... | collective-permute-start | bytes 884744 | tf_op jit(solution)/shard_map/ppermute | solution.py:31

commit v3 on v2

--- a/solution.py
+++ b/solution.py
@@ -22,67 +22,64 @@
 NT = (((1,), (1,)), ((), ()))
 
 
-def gather_chunks(block, n, early, middle, late):
+def gather_blocks(block, n, early, middle, third, late):
     if n != 32:
         whole = lax.all_gather(block, "train", axis=0, tiled=True)
-        return None, [[(whole, list(range(n)))]], early, middle(early)
+        middle = middle(early)
+        return None, [], [(whole, 0, list(range(n)))], early, middle, third(middle)
 
     def permute(held, mask):
         return lax.ppermute(held, "train", [(i, i ^ mask) for i in range(n)])
+
+    def join(chunk):
+        return jnp.concatenate([rows[chunk], first[chunk]], axis=0)
+
+    def near(chunk):
+        one, two = orders[chunk]
+        return [(held[chunk], chunk, [0, one]), (swapped[chunk], chunk, [1, one ^ 1])]
+
+    def far(chunk):
+        one, two = orders[chunk]
+        got = second[chunk]
+        return [(got, chunk, [two, one ^ two]), (permute(got, 1), chunk, [two ^ 1, one ^ two ^ 1])]
 
     orders = [(2, 4), (4, 2), (2, 4), (4, 2)]
     rows = [block] + [permute(block, mask) for mask in (8, 16, 24)]
     first, held, second, swapped = [permute(block, 2)], [], [], []
     first[0], rows[1], early = lax.optimization_barrier((first[0], rows[1], early))
-
-    def join(chunk):
-        held.append(jnp.concatenate([rows[chunk], first[chunk]], axis=0))
-
-    def spread(chunk):
+    held.append(join(0))
+    held[0], early = lax.optimization_barrier((held[0], early))
+    first.append(permute(rows[1], orders[1][0]))
+    second.append(permute(held[0], orders[0][1]))
+    swapped.append(permute(held[0], 1))
+    middle = middle(early)
+    rows[2], rows[3], first[1], middle = lax.optimization_barrier((rows[2], rows[3], first[1], middle))
+    first.append(permute(rows[2], orders[2][0]))
+    first.append(permute(rows[3], orders[3][0]))
+    held.append(join(1))
+    second.append(permute(held[1], orders[1][1]))
+    swapped.append(permute(held[1], 1))
+    third = third(middle)
+    first[2], first[3], second[0], third = lax.optimization_barrier((first[2], first[3], second[0], third))
+    for chunk in (2, 3):
+        held.append(join(chunk))
         second.append(permute(held[chunk], orders[chunk][1]))
         swapped.append(permute(held[chunk], 1))
-
-    def finish(chunk):
-        one, two = orders[chunk]
-        return [
-            (held[chunk], [0, one]),
-            (second[chunk], [two, one ^ two]),
-            (swapped[chunk], [1, one ^ 1]),
-            (permute(second[chunk], 1), [two ^ 1, one ^ two ^ 1]),
-        ]
-
-    first.append(permute(rows[1], orders[1][0]))
-    join(0)
-    held[0], early = lax.optimization_barrier((held[0], early))
-    spread(0)
-    middle = middle(early)
-    join(1)
-    spread(1)
-    rows[2], rows[3], middle = lax.optimization_barrier((rows[2], rows[3], middle))
-    first.append(permute(rows[2], orders[2][0]))
-    first.append(permute(rows[3], orders[3][0]))
-    join(2)
-    join(3)
-    spread(2)
-    spread(3)
-    front = [finish(0), finish(1)]
-    done = late(front, middle)
+    front = near(0) + far(0) + near(1) + far(1) + near(2) + near(3)
+    done = late(front, third)
     second[2], second[3], done = lax.optimization_barrier((second[2], second[3], done))
-    return (done, front), [finish(2), finish(3)], early, middle
+    return done, front, far(2) + far(3), early, middle, third
 
 
 def placed(n):
     mine = lax.axis_index("train").astype(jnp.int32)
     if n != 32:
-        return jnp.zeros((2,), jnp.int32), n
-    return jnp.stack([mine // 8, mine % 8]), 8
-
-
-def plan(chunks, start):
-    return (
-        [(start + c, lows) for c, chunk in enumerate(chunks) for _, lows in chunk],
-        [array for chunk in chunks for array, _ in chunk],
-    )
+        return jnp.stack([mine * 0, mine * 0, mine]), n
+    return jnp.stack([mine // 8, mine % 8, mine]), 8
+
+
+def plan(entries):
+    return [(chunk, lows) for _, chunk, lows in entries], [array for array, _, _ in entries]
 
 
 def split(value):
@@ -112,19 +109,29 @@
     return jnp.sum(each.reshape(RANK, items, 1), axis=0)
 
 
+def pairs_of(steps):
+    pairs = {}
+    for k, (chunk, lows) in enumerate(steps):
+        for s, low in enumerate(lows):
+            pairs.setdefault((chunk, low // 2), []).append((k, s, low))
+    return pairs
+
+
 def project(steps, size, place_ref, x_ref, g_ref, refs, held, grad, inp):
     hi, lo = place_ref[0], place_ref[1]
     part = refs[0].shape[1] // 2
-    start, width = steps[0][0], size * part
-    for ref, (chunk, lows) in zip(refs, steps):
-        for s, low in enumerate(lows):
-            held[chunk - start, 0, lo ^ low] = ref[s, 0:part, :]
-            held[chunk - start, 1, lo ^ low] = ref[s, part : 2 * part, :]
-    for chunk in sorted({c for c, _ in steps}):
-        columns = pl.ds(pl.multiple_of((hi ^ chunk) * width, width), width)
-        more = jnp.dot(g_ref[:, columns], held[chunk - start, 0].reshape(width, PW), preferred_element_type=F32)
+    pairs = pairs_of(steps)
+    for p, places in enumerate(pairs.values()):
+        for k, s, low in places:
+            held[p, 0, (lo ^ low) & 1] = refs[k][s, 0:part, :]
+            held[p, 1, (lo ^ low) & 1] = refs[k][s, part : 2 * part, :]
+    width = 2 * part
+    for p, ((chunk, _), places) in enumerate(pairs.items()):
+        device = (hi ^ chunk) * size + ((lo ^ places[0][2]) & -2)
+        columns = pl.ds(pl.multiple_of(device * part, width), width)
+        more = jnp.dot(g_ref[:, columns], held[p, 0].reshape(width, PW), preferred_element_type=F32)
         grad = more if grad is None else grad + more
-        more = jnp.dot(x_ref[:, columns], held[chunk - start, 1].reshape(width, PW), preferred_element_type=F32)
+        more = jnp.dot(x_ref[:, columns], held[p, 1].reshape(width, PW), preferred_element_type=F32)
         inp = more if inp is None else inp + more
     return grad, inp
 
@@ -158,7 +165,7 @@
     pack_ref[0, base + RANK : base + 2 * RANK, tokens:base] = index
 
 
-def train_kernel(steps, size, side, place_ref, act_ref, factor_ref, index_ref, *rest):
+def train_kernel(steps, size, side, place_ref, act_ref, adapter_ref, *rest):
     refs, rest = rest[: len(steps)], rest[len(steps) :]
     hi, lo = place_ref[0], place_ref[1]
     part = refs[0].shape[1] // 2
@@ -167,19 +174,29 @@
         for s, low in enumerate(lows):
             held[(hi ^ chunk) * size + (lo ^ low)] = ref[s, side * part : (side + 1) * part, :]
     width = held.shape[0] * part
+    factor = lax.dot_general(adapter_ref[...], act_ref[...], NT, preferred_element_type=F32)
     values = jnp.dot(act_ref[...], held[...].reshape(width, PW), preferred_element_type=F32)
+    if side == 0:
+        values_ref, factor_ref = rest[:2]
+        values_ref[...] = values
+        factor_ref[...] = factor
+        return
+    back_ref, index_ref, raw_ref, total_ref, factor_ref = rest[:5]
     picked = one_hot(index_ref[...], TRAIN_EXAMPLES)
-    raw = dot3(weighted(factor_ref[...], picked), values)
-    total = squares(raw, TRAIN_EXAMPLES)
-    if side == 0:
-        rest[0][...] = raw
-        rest[1][...] = total
-        return
-    raw_ref, total_ref, feats_ref = rest[:3]
-    scale = lax.rsqrt((total_ref[...] + total) * (1.0 / K) + EPS)[None]
+    raw = dot3(weighted(back_ref[...], picked), values)
+    raw_ref[...] = raw
+    total_ref[...] = squares(raw, TRAIN_EXAMPLES)
+    factor_ref[...] = factor
+
+
+def feats_kernel(hidden_ref, values_ref, raw_ref, total_ref, index_ref, feats_ref):
+    picked = one_hot(index_ref[...], TRAIN_EXAMPLES)
+    raw = dot3(weighted(hidden_ref[...], picked), values_ref[...])
+    total = total_ref[...] + squares(raw, TRAIN_EXAMPLES)
+    scale = lax.rsqrt(total * (1.0 / K) + EPS)[None]
     shape = (RANK, TRAIN_EXAMPLES, PW)
-    feats_ref[0] = (raw_ref[...].reshape(shape) * scale).reshape(RANK * TRAIN_EXAMPLES, PW).astype(BF16)
-    feats_ref[1] = (raw.reshape(shape) * scale).reshape(RANK * TRAIN_EXAMPLES, PW).astype(BF16)
+    feats_ref[0] = (raw.reshape(shape) * scale).reshape(RANK * TRAIN_EXAMPLES, PW).astype(BF16)
+    feats_ref[1] = (raw_ref[...].reshape(shape) * scale).reshape(RANK * TRAIN_EXAMPLES, PW).astype(BF16)
 
 
 def make_tiles(steps, size, place_ref, feats_ref, refs, tiles_ref):
@@ -211,17 +228,18 @@
     make_tiles(steps, size, place_ref, feats_ref, rest[: len(steps)], rest[len(steps)])
 
 
-def score_kernel(steps, size, front, place_ref, chosen_ref, live_ref, feats_ref, *rest):
+def score_kernel(steps, front, size, place_ref, pairing_ref, live_ref, feats_ref, *rest):
     refs, rest = rest[: len(steps)], rest[len(steps) :]
     out_ref, tiles = rest[-2:]
+    hi, lo, mine = place_ref[0], place_ref[1], place_ref[2]
     make_tiles(steps, size, place_ref, feats_ref, refs, tiles)
-    for chunk in range(front):
-        for low in range(size):
-            device = (place_ref[0] ^ chunk) * size + low
+    for chunk, lows in front:
+        for low in lows:
+            device = (hi ^ chunk) * size + (lo ^ low)
             tiles[device] = rest[0][device]
     for slot in range(SLOTS):
-        factor = jnp.where(slot < live_ref[0], 1.0 / K**0.5, 0.0)
-        out_ref[0, slot] = tiles[chosen_ref[slot]] * factor
+        factor = jnp.where(slot < live_ref[mine], 1.0 / K**0.5, 0.0)
+        out_ref[0, slot] = tiles[pairing_ref[slot, mine]] * factor
 
 
 def call(kernel, out_shape, scratch, flops, name, scalars, *arrays):
@@ -253,7 +271,6 @@
     live_slot_count,
 ):
     place, size = placed(n)
-    mine = lax.axis_index("train")
     tokens = eval_layer_input.shape[0]
     part = gradient_projector.shape[0]
     acts = (eval_layer_input, eval_output_gradient)
@@ -266,28 +283,25 @@
     def up(g):
         return lax.dot_general(adapter_up, g, NT, preferred_element_type=F32)
 
-    chosen = lax.dynamic_index_in_dim(paired_eval_index, mine, 0, keepdims=False)
-    live = lax.dynamic_index_in_dim(live_slot_count, mine, 0, keepdims=True)
-    early = (down(eval_layer_input), up(eval_output_gradient), chosen, live, train_layer_input, train_output_gradient)
-
-    def middle(early):
-        return down(early[4]), up(early[5])
-
-    held = [pltpu.VMEM((2, 2, size, part, PW), BF16)]
-
-    def begin(front, _):
-        steps, arrays = plan(front, 0)
+    def room(steps):
+        return [pltpu.VMEM((len(pairs_of(steps)), 2, 2, part, PW), BF16)]
+
+    def begin(front, early):
+        steps, arrays = plan(front)
+        place = early[2]
         kernel = functools.partial(begin_kernel, steps, size)
-        return call(kernel, sums, held, 5 * 10**8, "eval_begin", [place], *acts, *arrays)
-
+        return call(kernel, sums, room(steps), 8 * 10**8, "eval_begin", [place], *acts, *arrays)
+
+    early = (down(eval_layer_input), up(eval_output_gradient), place)
     block = jnp.concatenate([gradient_projector, input_projector], axis=0)[None]
-    begun, back, early, middle = gather_chunks(block, n, early, middle, begin)
-    front, extra = ([], []) if begun is None else (begun[1], [begun[0]])
-    steps, arrays = plan(back, len(front))
+    begun, front, back, early, _, _ = gather_blocks(block, n, early, tuple, tuple, begin)
+    place = early[2]
+    steps, arrays = plan(back)
+    extra = [] if begun is None else [begun]
     pack = call(
         functools.partial(eval_kernel, steps, size, len(extra)),
         jax.ShapeDtypeStruct((1, 2 * (tokens + RANK), PW), BF16),
-        held,
+        room(steps),
         10**9,
         "eval_factors",
         [place],
@@ -298,56 +312,61 @@
         *arrays,
         *extra,
     )
-    steps, arrays = plan(front + back, 0)
+    every, everything = plan(front + back)
     held = [pltpu.VMEM((n, part, PW), BF16)]
     rows = RANK * TRAIN_EXAMPLES
-    raw = call(
-        functools.partial(train_kernel, steps, size, 0),
-        [jax.ShapeDtypeStruct((rows, PW), F32), jax.ShapeDtypeStruct((TRAIN_EXAMPLES, 1), F32)],
+    values_shape = jax.ShapeDtypeStruct((train_layer_input.shape[0], PW), F32)
+    factor_shape = jax.ShapeDtypeStruct((RANK, train_layer_input.shape[0]), F32)
+    gradient_side = call(
+        functools.partial(train_kernel, every, size, 0),
+        [values_shape, factor_shape],
         held,
         2 * 10**9,
         "train_gradient_side",
         [place],
         train_output_gradient,
-        middle[0],
-        train_example_index,
-        *arrays,
-    )
-
-    def finish_train(raw):
-        return call(
-            functools.partial(train_kernel, steps, size, 1),
-            jax.ShapeDtypeStruct((2, rows, PW), BF16),
+        adapter_up,
+        *everything,
+    )
+
+    def input_side(gradient_side):
+        values, back = gradient_side
+        raw, total, hidden = call(
+            functools.partial(train_kernel, every, size, 1),
+            [jax.ShapeDtypeStruct((rows, PW), F32), jax.ShapeDtypeStruct((TRAIN_EXAMPLES, 1), F32), factor_shape],
             held,
             2 * 10**9,
             "train_input_side",
             [place],
             train_layer_input,
-            middle[1],
+            adapter_down.T,
+            *everything,
+            back,
             train_example_index,
-            *arrays,
-            *raw,
         )
+        return hidden, values, raw, total
+
+    def features(sides):
+        shape = jax.ShapeDtypeStruct((2, rows, PW), BF16)
+        return call(feats_kernel, shape, [], 10**9, "train_features", [], *sides, train_example_index)
 
     def tile(front, feats):
-        steps, arrays = plan(front, 0)
+        steps, arrays = plan(front)
         kernel = functools.partial(tile_kernel, steps, size)
-        shape = jax.ShapeDtypeStruct(tiles_shape, F32)
-        return call(kernel, shape, [], 10**9, "front_tiles", [place], feats, *arrays)
-
-    tiles, back, _, feats = gather_chunks(pack, n, raw, finish_train, tile)
-    front, extra = ([], []) if tiles is None else (tiles[1], [tiles[0]])
-    steps, arrays = plan(back, len(front))
+        return call(kernel, jax.ShapeDtypeStruct(tiles_shape, F32), [], 10**9, "front_tiles", [place], feats, *arrays)
+
+    tiles, front, back, _, _, feats = gather_blocks(pack, n, gradient_side, input_side, features, tile)
+    steps, arrays = plan(back)
     scores = call(
-        functools.partial(score_kernel, steps, size, len(front)),
+        functools.partial(score_kernel, steps, plan(front)[0], size),
         jax.ShapeDtypeStruct((1, SLOTS, EVAL_ROLLOUTS, TRAIN_EXAMPLES), F32),
         [pltpu.VMEM(tiles_shape, F32)],
         10**9,
         "score_tiles",
-        [place, early[2], early[3]],
+        [place, paired_eval_index.T, live_slot_count],
         feats,
         *arrays,
-        *extra,
+        *([] if tiles is None else [tiles]),
     )
     return jnp.swapaxes(scores, 2, 3)
 

time: 93.7 us -> 87.8 us (0.937)
  local copies, waits for them, and re-layouts: 6.82 us -> 0.18 us
  matrix products: 9.23 us -> 3.38 us
  waiting for transfers between devices: 26.6 us -> 31.6 us
  starting transfers between devices: 28.7 us -> 32 us
  Pallas kernels: 20.7 us -> 19 us
    ppermute x38, waiting for transfers between devices: 26.6 us -> 31.6 us  [permute(): return lax.ppermute(held, 'train', [(i, i ^ mask) for i in range(n)])]
    dot_general x2 -> x1, matrix products: 5.73 us -> 1.67 us  [down(): lax.dot_general(adapter_down, x, (((0,), (1,)), ((), ())), preferred_elem...]
    unnamed x36 -> x26, local copies, waits for them, and re-layouts: 3.84 us -> 0.12 us
    ppermute x38, starting transfers between devices: 28.7 us -> 32 us  [permute(): return lax.ppermute(held, 'train', [(i, i ^ mask) for i in range(n)])]
    dynamic_slice x2 -> x0, local copies, waits for them, and re-layouts: 2.92 us -> none  [the longest x1 1.47 us: per_device(): lax.dynamic_index_in_dim(paired_eval_index, mine, 0, keepdims=False)]
    dot_general x2 -> x1, matrix products: 3.5 us -> 1.7 us  [up(): return lax.dot_general(adapter_up, g, NT, preferred_element_type=F32)]
    pallas_call x6 -> x7, Pallas kernels: 20.7 us -> 19 us  [call(): pl.pallas_call(kernel, out_shape=out_shape, in_specs=[SMEM] * len(scalars...]
  transfers between devices with their start and end apart: 38 -> 38, of which waited for: 15 -> 18; matrix products, arithmetic and copies ran while one was open for 15% -> 4% of each run, Pallas kernels for 15% -> 17%
where the time goes in v3:
time: 87.8 us; the launch traced here: 87.6 us
  starting transfers between devices  32 us (36%)
  waiting for transfers between devices  31.6 us (36%)
  Pallas kernels  19 us (22%)
  matrix products  3.38 us (4%)
  other arithmetic  1.17 us (1%)
    ppermute x38, starting transfers between devices, permute(): return lax.ppermute(held, 'train', [(i, i ^ mask) for i in range(n)])  32 us
    ppermute x38, waiting for transfers between devices, permute(): return lax.ppermute(held, 'train', [(i, i ^ mask) for i in range(n)])  31.6 us
    pallas_call x7, Pallas kernels, call(): pl.pallas_call(kernel, out_shape=out_shape, in_specs=[SMEM] * len(scalars...  19 us
  transfers between devices with their start and end apart: 38, of which 18 were waited for; matrix products, arithmetic and copies ran while one was open for 4% of the time, Pallas kernels for 17%

profile of v3, /device:TPU:0, one launch (start us, length us, event | category | flops | bytes accessed | tf_op | source)
XLA Modules:
  0.0 87.6 jit_solution(206787732954379977)
XLA Ops:
  0.0 1.0 %maximum_bitcast_fusion = bf16[1,256,256]{2,1,0:T(8,128)(2,1)S(1)} fusion(bf16[128,256]{1,0:T(8,128)(2,1)} %param.21, bf16[128,256]{1,0:T(8,128)(2,1)} %param.20), kind=kLoop, calls=%fused_computation.2 | loop fusion | flops 262144 | bytes 262144 | tf_op jit(solution)/shard_map/broadcast_in_dim | solution.py:296
  1.0 3.0 %collective-permute-start = (bf16[1,256,256]{2,1,0:T(8,128)(2,1)S(1)}, bf16[1,256,256]{2,1,0:T(8,128)(2,1)S(1)}, u32[]{:S(2)}, u32[]{:S(2)}) collective-permute-start(bf16[1,256,256]{2,1,0:T(8,128)(2,1)S(1)} %maximum_bitcast_fusion), channel_id=1, source_target_pairs={{0,2},{1,3},{2,0},{3,1},{4,6},{5,7},{6,4},{7,5},{8,10},{9,11},{10,... | collective-permute-start | bytes 393224 | tf_op jit(solution)/shard_map/ppermute | solution.py:32
  4.0 1.6 %collective-permute-start.1 = (bf16[1,256,256]{2,1,0:T(8,128)(2,1)S(1)}, bf16[1,256,256]{2,1,0:T(8,128)(2,1)S(1)}, u32[]{:S(2)}, u32[]{:S(2)}) collective-permute-start(bf16[1,256,256]{2,1,0:T(8,128)(2,1)S(1)} %maximum_bitcast_fusion), channel_id=1, source_target_pairs={{0,8},{1,9},{2,10},{3,11},{4,12},{5,13},{6,14},{7,15},{8,0},{9,1},... | collective-permute-start | bytes 393224 | tf_op jit(solution)/shard_map/ppermute | solution.py:32
  5.6 2.6 %collective-permute-start.2 = (bf16[1,256,256]{2,1,0:T(8,128)(2,1)S(1)}, bf16[1,256,256]{2,1,0:T(8,128)(2,1)S(1)}, u32[]{:S(2)}, u32[]{:S(2)}) collective-permute-start(bf16[1,256,256]{2,1,0:T(8,128)(2,1)S(1)} %maximum_bitcast_fusion), channel_id=1, source_target_pairs={{0,16},{1,17},{2,18},{3,19},{4,20},{5,21},{6,22},{7,23},{8,24},{9,... | collective-permute-start | bytes 393224 | tf_op jit(solution)/shard_map/ppermute | solution.py:32
  8.2 0.2 collective-permute-start.3
  8.4 1.7 %fusion.hidden_ref = f32[16,128]{1,0:T(8,128)S(1)} fusion(bf16[4096,16]{0,1:T(8,128)(2,1)} %param.18, bf16[128,4096]{1,0:T(8,128)(2,1)} %x_ref.3), kind=kOutput, calls=%fused_computation.16 | convolution fusion | flops 16777216 | bytes 1187840 | tf_op jit(solution)/shard_map/dot_general | solution.py:281
  10.1 1.7 %fusion.1.back_ref = f32[16,128]{1,0:T(8,128)S(1)} fusion(bf16[16,4096]{1,0:T(8,128)(2,1)} %adapter_ref.1, bf16[128,4096]{1,0:T(8,128)(2,1)} %g_ref.3), kind=kOutput, calls=%fused_computation.17 | convolution fusion | flops 16777216 | bytes 1187840 | tf_op jit(solution)/shard_map/dot_general | solution.py:284
  11.8 0.1 pad_add_fusion.place_ref
  11.9 1.6 %collective-permute-start.4 = (bf16[1,256,256]{2,1,0:T(8,128)(2,1)S(1)}, bf16[1,256,256]{2,1,0:T(8,128)(2,1)S(1)}, u32[]{:S(2)}, u32[]{:S(2)}) collective-permute-start(bf16[1,256,256]{2,1,0:T(8,128)(2,1)S(1)} %collective-permute-done.1), channel_id=1, source_target_pairs={{0,4},{1,5},{2,6},{3,7},{4,0},{5,1},{6,2},{7,3},{8,12},{9,13},{10,... | collective-permute-start | bytes 393224 | tf_op jit(solution)/shard_map/ppermute | solution.py:32
  13.5 0.6 collective-permute-start.7
  14.1 0.1 collective-permute-start.10
  14.2 4.1 %collective-permute-done.2 = bf16[1,256,256]{2,1,0:T(8,128)(2,1)S(1)} collective-permute-done((bf16[1,256,256]{2,1,0:T(8,128)(2,1)S(1)}, bf16[1,256,256]{2,1,0:T(8,128)(2,1)S(1)}, u32[]{:S(2)}, u32[]{:S(2)}) %collective-permute-start.2) | collective-permute-done | bytes 131104 | tf_op jit(solution)/shard_map/ppermute | solution.py:32
  18.3 0.1 collective-permute-done.4
  18.4 0.4 collective-permute-start.5
  18.8 1.6 %collective-permute-start.6 = (bf16[1,256,256]{2,1,0:T(8,128)(2,1)S(1)}, bf16[1,256,256]{2,1,0:T(8,128)(2,1)S(1)}, u32[]{:S(2)}, u32[]{:S(2)}) collective-permute-start(bf16[1,256,256]{2,1,0:T(8,128)(2,1)S(1)} %collective-permute-done.3), channel_id=1, source_target_pairs={{0,4},{1,5},{2,6},{3,7},{4,0},{5,1},{6,2},{7,3},{8,12},{9,13},{10,... | collective-permute-start | bytes 393224 | tf_op jit(solution)/shard_map/ppermute | solution.py:32
  20.5 1.6 %collective-permute-start.13 = (bf16[2,256,256]{2,1,0:T(8,128)(2,1)S(1)}, bf16[2,256,256]{2,1,0:T(8,128)(2,1)S(1)}, u32[]{:S(2)}, u32[]{:S(2)}) collective-permute-start(bf16[2,256,256]{2,1,0:T(8,128)(2,1)S(1)} %constant_dynamic-update-slice_fusion.4.rest_4_), channel_id=1, source_target_pairs={{0,2},{1,3},{2,0},{3,1},{4,6},{5,7},{6,4},{7,5},{8,10},{9,11},{10,... | collective-permute-start | bytes 786440 | tf_op jit(solution)/shard_map/ppermute | solution.py:32
  22.0 1.4 %collective-permute-done.5 = bf16[1,256,256]{2,1,0:T(8,128)(2,1)S(1)} collective-permute-done((bf16[1,256,256]{2,1,0:T(8,128)(2,1)S(1)}, bf16[1,256,256]{2,1,0:T(8,128)(2,1)S(1)}, u32[]{:S(2)}, u32[]{:S(2)}) %collective-permute-start.5) | collective-permute-done | bytes 131104 | tf_op jit(solution)/shard_map/ppermute | solution.py:32
  23.4 1.2 %collective-permute-done.6 = bf16[1,256,256]{2,1,0:T(8,128)(2,1)S(1)} collective-permute-done((bf16[1,256,256]{2,1,0:T(8,128)(2,1)S(1)}, bf16[1,256,256]{2,1,0:T(8,128)(2,1)S(1)}, u32[]{:S(2)}, u32[]{:S(2)}) %collective-permute-start.6) | collective-permute-done | bytes 131104 | tf_op jit(solution)/shard_map/ppermute | solution.py:32
  24.6 0.1 collective-permute-start.16
  24.7 0.0 copy-start.1
  24.7 0.0 copy-start.4
  24.7 0.6 collective-permute-start.15
  25.3 0.1 collective-permute-start.11
  25.4 1.5 %collective-permute-done.13.rest_6_ = bf16[2,256,256]{2,1,0:T(8,128)(2,1)S(1)} collective-permute-done((bf16[2,256,256]{2,1,0:T(8,128)(2,1)S(1)}, bf16[2,256,256]{2,1,0:T(8,128)(2,1)S(1)}, u32[]{:S(2)}, u32[]{:S(2)}) %collective-permute-start.13) | collective-permute-done | bytes 262176 | tf_op jit(solution)/shard_map/ppermute | solution.py:32
  26.9 1.5 %collective-permute-start.9 = (bf16[2,256,256]{2,1,0:T(8,128)(2,1)S(1)}, bf16[2,256,256]{2,1,0:T(8,128)(2,1)S(1)}, u32[]{:S(2)}, u32[]{:S(2)}) collective-permute-start(bf16[2,256,256]{2,1,0:T(8,128)(2,1)S(1)} %constant_dynamic-update-slice_fusion.2.rest_10_), channel_id=1, source_target_pairs={{0,2},{1,3},{2,0},{3,1},{4,6},{5,7},{6,4},{7,5},{8,10},{9,11},{10,... | collective-permute-start | bytes 786440 | tf_op jit(solution)/shard_map/ppermute | solution.py:32
  28.4 0.5 collective-permute-start.8
  28.9 1.7 %eval_begin.1.rest_4_ = f32[2,128,256]{2,1,0:T(8,128)S(1)} custom-call(s32[3]{0:T(128)S(1)} %pad_add_fusion.place_ref, bf16[128,4096]{1,0:T(8,128)(2,1)S(1)} %copy-done.2, bf16[128,4096]{1,0:T(8,128)(2,1)S(1)} %copy-done.3, bf16[2,256,256]{2,1,0:T(8,128)(2,1)S(1)} %pad_maximum_fusion.1.rest_0_, bf16[2,256,256]{2,1,0:T(8,128)(2,1)S(1)} %collective-permute-done.10.rest_1_, ...), custom_call_target="tpu_custom_call" | custom-call | flops 800000000 | bytes 4194304 | tf_op jit(solution)/shard_map/eval_begin/pallas_call | solution.py:246
  30.6 5.0 %collective-permute-done.9.rest_2_.rest_14_ = bf16[2,256,256]{2,1,0:T(8,128)(2,1)S(1)} collective-permute-done((bf16[2,256,256]{2,1,0:T(8,128)(2,1)S(1)}, bf16[2,256,256]{2,1,0:T(8,128)(2,1)S(1)}, u32[]{:S(2)}, u32[]{:S(2)}) %collective-permute-start.9) | collective-permute-done | bytes 262176 | tf_op jit(solution)/shard_map/ppermute | solution.py:32
  35.6 1.2 %collective-permute-done.8.rest_0_.rest_12_ = bf16[2,256,256]{2,1,0:T(8,128)(2,1)S(1)} collective-permute-done((bf16[2,256,256]{2,1,0:T(8,128)(2,1)S(1)}, bf16[2,256,256]{2,1,0:T(8,128)(2,1)S(1)}, u32[]{:S(2)}, u32[]{:S(2)}) %collective-permute-start.8) | collective-permute-done | bytes 262176 | tf_op jit(solution)/shard_map/ppermute | solution.py:32
  36.8 0.5 collective-permute-start.18
  37.3 1.0 %collective-permute-done.17.rest_1_.rest_13_ = bf16[2,256,256]{2,1,0:T(8,128)(2,1)S(1)} collective-permute-done((bf16[2,256,256]{2,1,0:T(8,128)(2,1)S(1)}, bf16[2,256,256]{2,1,0:T(8,128)(2,1)S(1)}, u32[]{:S(2)}, u32[]{:S(2)}) %collective-permute-start.17) | collective-permute-done | bytes 262176 | tf_op jit(solution)/shard_map/ppermute | solution.py:32
  38.4 0.4 collective-permute-done.18.rest_3_.rest_15_
  38.8 1.4 %eval_factors.1 = bf16[1,288,256]{2,1,0:T(8,128)(2,1)S(1)} custom-call(s32[3]{0:T(128)S(1)} %pad_add_fusion.place_ref, bf16[128,4096]{1,0:T(8,128)(2,1)S(1)} %copy-done.2, bf16[128,4096]{1,0:T(8,128)(2,1)S(1)} %copy-done.3, f32[16,128]{1,0:T(8,128)S(1)} %fusion.hidden_ref, f32[16,128]{1,0:T(8,128)S(1)} %fusion.1.back_ref, s32[1,128]{1,0:T(1,128)S(1)} %copy-done.8, ...), custom_call_target="tpu_custom_call" | custom-call | flops 1000000000 | bytes 4194304 | tf_op jit(solution)/shard_map/eval_factors/pallas_call | solution.py:246
  40.2 0.0 copy-start
  40.2 0.6 collective-permute-start.21
  40.8 3.2 %collective-permute-start.22 = (bf16[1,288,256]{2,1,0:T(8,128)(2,1)S(1)}, bf16[1,288,256]{2,1,0:T(8,128)(2,1)S(1)}, u32[]{:S(2)}, u32[]{:S(2)}) collective-permute-start(bf16[1,288,256]{2,1,0:T(8,128)(2,1)S(1)} %eval_factors.1), channel_id=1, source_target_pairs={{0,8},{1,9},{2,10},{3,11},{4,12},{5,13},{6,14},{7,15},{8,0},{9,1},... | collective-permute-start | bytes 442376 | tf_op jit(solution)/shard_map/ppermute | solution.py:32
  44.0 1.1 %collective-permute-start.19 = (bf16[1,288,256]{2,1,0:T(8,128)(2,1)S(1)}, bf16[1,288,256]{2,1,0:T(8,128)(2,1)S(1)}, u32[]{:S(2)}, u32[]{:S(2)}) collective-permute-start(bf16[1,288,256]{2,1,0:T(8,128)(2,1)S(1)} %eval_factors.1), channel_id=1, source_target_pairs={{0,16},{1,17},{2,18},{3,19},{4,20},{5,21},{6,22},{7,23},{8,24},{9,... | collective-permute-start | bytes 442376 | tf_op jit(solution)/shard_map/ppermute | solution.py:32
  45.1 1.5 %collective-permute-start.20 = (bf16[1,288,256]{2,1,0:T(8,128)(2,1)S(1)}, bf16[1,288,256]{2,1,0:T(8,128)(2,1)S(1)}, u32[]{:S(2)}, u32[]{:S(2)}) collective-permute-start(bf16[1,288,256]{2,1,0:T(8,128)(2,1)S(1)} %eval_factors.1), channel_id=1, source_target_pairs={{0,24},{1,25},{2,26},{3,27},{4,28},{5,29},{6,30},{7,31},{8,16},{9,... | collective-permute-start | bytes 442376 | tf_op jit(solution)/shard_map/ppermute | solution.py:32
  46.6 2.9 %train_gradient_side.1 = (f32[512,256]{1,0:T(8,128)S(1)}, f32[16,512]{1,0:T(8,128)S(1)}) custom-call(s32[3]{0:T(128)S(1)} %pad_add_fusion.place_ref, bf16[512,4096]{1,0:T(8,128)(2,1)S(1)} %copy-done.1, bf16[16,4096]{1,0:T(8,128)(2,1)S(1)} %copy-done.4, bf16[2,256,256]{2,1,0:T(8,128)(2,1)S(1)} %pad_maximum_fusion.1.rest_0_, ...), custom_call_target="tpu_custom_call" | custom-call | flops 2000000000 | bytes 4194304 | tf_op jit(solution)/shard_map/train_gradient_side/pallas_call | solution.py:246
  49.5 0.4 collective-permute-done.22
  50.0 1.4 %collective-permute-start.26 = (bf16[2,288,256]{2,1,0:T(8,128)(2,1)S(1)}, bf16[2,288,256]{2,1,0:T(8,128)(2,1)S(1)}, u32[]{:S(2)}, u32[]{:S(2)}) collective-permute-start(bf16[2,288,256]{2,1,0:T(8,128)(2,1)S(1)} %pad_maximum_fusion.rest_0_), channel_id=1, source_target_pairs={{0,4},{1,5},{2,6},{3,7},{4,0},{5,1},{6,2},{7,3},{8,12},{9,13},{10,... | collective-permute-start | bytes 884744 | tf_op jit(solution)/shard_map/ppermute | solution.py:32
  51.4 0.7 collective-permute-start.23
  52.1 4.3 %train_input_side.1 = (f32[512,256]{1,0:T(8,128)S(1)}, f32[32,1]{1,0:T(8,128)S(1)}, f32[16,512]{1,0:T(8,128)S(1)}) custom-call(s32[3]{0:T(128)S(1)} %pad_add_fusion.place_ref, bf16[512,4096]{1,0:T(8,128)(2,1)S(1)} %copy-done, bf16[16,4096]{1,0:T(8,128)(2,1)S(1)} %bitcast.12, bf16[2,256,256]{2,1,0:T(8,128)(2,1)S(1)} %pad_maximum_fusion.1.rest_0_, ...), custom_call_target="tpu_custom_call" | custom-call | flops 2000000000 | bytes 4194304 | tf_op jit(solution)/shard_map/train_input_side/pallas_call | solution.py:246
  56.4 1.6 %collective-permute-done.19 = bf16[1,288,256]{2,1,0:T(8,128)(2,1)S(1)} collective-permute-done((bf16[1,288,256]{2,1,0:T(8,128)(2,1)S(1)}, bf16[1,288,256]{2,1,0:T(8,128)(2,1)S(1)}, u32[]{:S(2)}, u32[]{:S(2)}) %collective-permute-start.19) | collective-permute-done | bytes 147488 | tf_op jit(solution)/shard_map/ppermute | solution.py:32
  58.0 3.0 %collective-permute-done.23 = bf16[1,288,256]{2,1,0:T(8,128)(2,1)S(1)} collective-permute-done((bf16[1,288,256]{2,1,0:T(8,128)(2,1)S(1)}, bf16[1,288,256]{2,1,0:T(8,128)(2,1)S(1)}, u32[]{:S(2)}, u32[]{:S(2)}) %collective-permute-start.23) | collective-permute-done | bytes 147488 | tf_op jit(solution)/shard_map/ppermute | solution.py:32
  61.1 1.3 %collective-permute-start.32 = (bf16[2,288,256]{2,1,0:T(8,128)(2,1)S(1)}, bf16[2,288,256]{2,1,0:T(8,128)(2,1)S(1)}, u32[]{:S(2)}, u32[]{:S(2)}) collective-permute-start(bf16[2,288,256]{2,1,0:T(8,128)(2,1)S(1)} %constant_dynamic-update-slice_fusion.10.rest_4_), channel_id=1, source_target_pairs={{0,2},{1,3},{2,0},{3,1},{4,6},{5,7},{6,4},{7,5},{8,10},{9,11},{10,... | collective-permute-start | bytes 884744 | tf_op jit(solution)/shard_map/ppermute | solution.py:32
  62.3 0.8 collective-permute-start.24
  63.2 1.4 %collective-permute-start.25 = (bf16[1,288,256]{2,1,0:T(8,128)(2,1)S(1)}, bf16[1,288,256]{2,1,0:T(8,128)(2,1)S(1)}, u32[]{:S(2)}, u32[]{:S(2)}) collective-permute-start(bf16[1,288,256]{2,1,0:T(8,128)(2,1)S(1)} %collective-permute-done.20), channel_id=1, source_target_pairs={{0,4},{1,5},{2,6},{3,7},{4,0},{5,1},{6,2},{7,3},{8,12},{9,13},{10,... | collective-permute-start | bytes 442376 | tf_op jit(solution)/shard_map/ppermute | solution.py:32
  64.5 0.8 train_features.1.feats_ref
  65.4 5.8 %collective-permute-done.24 = bf16[1,288,256]{2,1,0:T(8,128)(2,1)S(1)} collective-permute-done((bf16[1,288,256]{2,1,0:T(8,128)(2,1)S(1)}, bf16[1,288,256]{2,1,0:T(8,128)(2,1)S(1)}, u32[]{:S(2)}, u32[]{:S(2)}) %collective-permute-start.24) | collective-permute-done | bytes 147488 | tf_op jit(solution)/shard_map/ppermute | solution.py:32
  71.2 0.6 collective-permute-start.35
  71.8 0.1 collective-permute-start.34
  71.9 0.5 collective-permute-start.30
  72.4 0.1 collective-permute-start.33
  72.5 0.3 collective-permute-done.31.rest_5_
  72.8 1.1 %collective-permute-start.28 = (bf16[2,288,256]{2,1,0:T(8,128)(2,1)S(1)}, bf16[2,288,256]{2,1,0:T(8,128)(2,1)S(1)}, u32[]{:S(2)}, u32[]{:S(2)}) collective-permute-start(bf16[2,288,256]{2,1,0:T(8,128)(2,1)S(1)} %constant_dynamic-update-slice_fusion.8.rest_10_), channel_id=1, source_target_pairs={{0,2},{1,3},{2,0},{3,1},{4,6},{5,7},{6,4},{7,5},{8,10},{9,11},{10,... | collective-permute-start | bytes 884744 | tf_op jit(solution)/shard_map/ppermute | solution.py:32
  73.9 0.8 collective-permute-start.27
  74.8 4.9 %front_tiles.1.rest_4_ = f32[32,16,32]{2,1,0:T(8,128)S(1)} custom-call(s32[3]{0:T(128)S(1)} %pad_add_fusion.place_ref, bf16[2,512,256]{2,1,0:T(8,128)(2,1)S(1)} %train_features.1.feats_ref, bf16[2,288,256]{2,1,0:T(8,128)(2,1)S(1)} %pad_maximum_fusion.rest_0_, bf16[2,288,256]{2,1,0:T(8,128)(2,1)S(1)} %collective-permute-done.29.rest_1_, ...), custom_call_target="tpu_custom_call" | custom-call | flops 1000000000 | bytes 4194304 | tf_op jit(solution)/shard_map/front_tiles/pallas_call | solution.py:246
  79.7 2.2 %collective-permute-done.28.rest_2_ = bf16[2,288,256]{2,1,0:T(8,128)(2,1)S(1)} collective-permute-done((bf16[2,288,256]{2,1,0:T(8,128)(2,1)S(1)}, bf16[2,288,256]{2,1,0:T(8,128)(2,1)S(1)}, u32[]{:S(2)}, u32[]{:S(2)}) %collective-permute-start.28) | collective-permute-done | bytes 294944 | tf_op jit(solution)/shard_map/ppermute | solution.py:32
  81.8 0.9 collective-permute-done.27.rest_0_
  82.7 0.5 collective-permute-start.37
  83.2 1.1 %collective-permute-done.36.rest_1_ = bf16[2,288,256]{2,1,0:T(8,128)(2,1)S(1)} collective-permute-done((bf16[2,288,256]{2,1,0:T(8,128)(2,1)S(1)}, bf16[2,288,256]{2,1,0:T(8,128)(2,1)S(1)}, u32[]{:S(2)}, u32[]{:S(2)}) %collective-permute-start.36) | collective-permute-done | bytes 294944 | tf_op jit(solution)/shard_map/ppermute | solution.py:32
  84.3 0.4 collective-permute-done.37.rest_3_
  84.7 2.9 %score_tiles.1 = f32[1,16,16,32]{3,2,1,0:T(8,128)} custom-call(s32[3]{0:T(128)S(1)} %pad_add_fusion.place_ref, s32[16,32]{1,0:T(8,128)S(1)} %bitcast.13, s32[32]{0:T(128)S(1)} %copy-done.9, bf16[2,512,256]{2,1,0:T(8,128)(2,1)S(1)} %train_features.1.feats_ref, bf16[2,288,256]{2,1,0:T(8,128)(2,1)S(1)} %collective-permute-done.27.rest_0_, ...), custom_call_target="tpu_custom_call" | custom-call | flops 1000000000 | bytes 4194304 | tf_op jit(solution)/shard_map/score_tiles/pallas_call | solution.py:246
  (57 shorter events, 0.3 us)
Async XLA Ops:
  0.0 28.9 %copy-start.2 = (bf16[128,4096]{1,0:T(8,128)(2,1)S(1)}, bf16[128,4096]{1,0:T(8,128)(2,1)}, u32[]{:S(2)}) copy-start(bf16[128,4096]{1,0:T(8,128)(2,1)} %x_ref.3) | copy-start | bytes 3145732
  0.0 28.9 %copy-start.3 = (bf16[128,4096]{1,0:T(8,128)(2,1)S(1)}, bf16[128,4096]{1,0:T(8,128)(2,1)}, u32[]{:S(2)}) copy-start(bf16[128,4096]{1,0:T(8,128)(2,1)} %g_ref.3) | copy-start | bytes 3145732
  1.0 10.9 %collective-permute-start = (bf16[1,256,256]{2,1,0:T(8,128)(2,1)S(1)}, bf16[1,256,256]{2,1,0:T(8,128)(2,1)S(1)}, u32[]{:S(2)}, u32[]{:S(2)}) collective-permute-start(bf16[1,256,256]{2,1,0:T(8,128)(2,1)S(1)} %maximum_bitcast_fusion), channel_id=1, source_target_pairs={{0,2},{1,3},{2,0},{3,1},{4,6},{5,7},{6,4},{7,5},{8,10},{9,11},{10,... | collective-permute-start | bytes 393224 | tf_op jit(solution)/shard_map/ppermute | solution.py:32
  4.0 7.9 %collective-permute-start.1 = (bf16[1,256,256]{2,1,0:T(8,128)(2,1)S(1)}, bf16[1,256,256]{2,1,0:T(8,128)(2,1)S(1)}, u32[]{:S(2)}, u32[]{:S(2)}) collective-permute-start(bf16[1,256,256]{2,1,0:T(8,128)(2,1)S(1)} %maximum_bitcast_fusion), channel_id=1, source_target_pairs={{0,8},{1,9},{2,10},{3,11},{4,12},{5,13},{6,14},{7,15},{8,0},{9,1},... | collective-permute-start | bytes 393224 | tf_op jit(solution)/shard_map/ppermute | solution.py:32
  5.6 12.6 %collective-permute-start.2 = (bf16[1,256,256]{2,1,0:T(8,128)(2,1)S(1)}, bf16[1,256,256]{2,1,0:T(8,128)(2,1)S(1)}, u32[]{:S(2)}, u32[]{:S(2)}) collective-permute-start(bf16[1,256,256]{2,1,0:T(8,128)(2,1)S(1)} %maximum_bitcast_fusion), channel_id=1, source_target_pairs={{0,16},{1,17},{2,18},{3,19},{4,20},{5,21},{6,22},{7,23},{8,24},{9,... | collective-permute-start | bytes 393224 | tf_op jit(solution)/shard_map/ppermute | solution.py:32
  8.2 10.1 %collective-permute-start.3 = (bf16[1,256,256]{2,1,0:T(8,128)(2,1)S(1)}, bf16[1,256,256]{2,1,0:T(8,128)(2,1)S(1)}, u32[]{:S(2)}, u32[]{:S(2)}) collective-permute-start(bf16[1,256,256]{2,1,0:T(8,128)(2,1)S(1)} %maximum_bitcast_fusion), channel_id=1, source_target_pairs={{0,24},{1,25},{2,26},{3,27},{4,28},{5,29},{6,30},{7,31},{8,16},{9,... | collective-permute-start | bytes 393224 | tf_op jit(solution)/shard_map/ppermute | solution.py:32
  10.1 28.6 %copy-start.8 = (s32[1,128]{1,0:T(1,128)S(1)}, s32[1,128]{1,0:T(1,128)}, u32[]{:S(2)}) copy-start(s32[1,128]{1,0:T(1,128)} %index_ref.2) | copy-start | bytes 1540
  11.9 6.5 %collective-permute-start.4 = (bf16[1,256,256]{2,1,0:T(8,128)(2,1)S(1)}, bf16[1,256,256]{2,1,0:T(8,128)(2,1)S(1)}, u32[]{:S(2)}, u32[]{:S(2)}) collective-permute-start(bf16[1,256,256]{2,1,0:T(8,128)(2,1)S(1)} %collective-permute-done.1), channel_id=1, source_target_pairs={{0,4},{1,5},{2,6},{3,7},{4,0},{5,1},{6,2},{7,3},{8,12},{9,13},{10,... | collective-permute-start | bytes 393224 | tf_op jit(solution)/shard_map/ppermute | solution.py:32
  13.5 11.1 %collective-permute-start.7 = (bf16[2,256,256]{2,1,0:T(8,128)(2,1)S(1)}, bf16[2,256,256]{2,1,0:T(8,128)(2,1)S(1)}, u32[]{:S(2)}, u32[]{:S(2)}) collective-permute-start(bf16[2,256,256]{2,1,0:T(8,128)(2,1)S(1)} %pad_maximum_fusion.1.rest_0_), channel_id=1, source_target_pairs={{0,4},{1,5},{2,6},{3,7},{4,0},{5,1},{6,2},{7,3},{8,12},{9,13},{10,... | collective-permute-start | bytes 786440 | tf_op jit(solution)/shard_map/ppermute | solution.py:32
  14.1 11.2 %collective-permute-start.10 = (bf16[2,256,256]{2,1,0:T(8,128)(2,1)S(1)}, bf16[2,256,256]{2,1,0:T(8,128)(2,1)S(1)}, u32[]{:S(2)}, u32[]{:S(2)}) collective-permute-start(bf16[2,256,256]{2,1,0:T(8,128)(2,1)S(1)} %pad_maximum_fusion.1.rest_0_), channel_id=1, source_target_pairs={{0,1},{1,0},{2,3},{3,2},{4,5},{5,4},{6,7},{7,6},{8,9},{9,8},{10,11... | collective-permute-start | bytes 786440 | tf_op jit(solution)/shard_map/ppermute | solution.py:32
  18.4 5.0 %collective-permute-start.5 = (bf16[1,256,256]{2,1,0:T(8,128)(2,1)S(1)}, bf16[1,256,256]{2,1,0:T(8,128)(2,1)S(1)}, u32[]{:S(2)}, u32[]{:S(2)}) collective-permute-start(bf16[1,256,256]{2,1,0:T(8,128)(2,1)S(1)} %collective-permute-done.2), channel_id=1, source_target_pairs={{0,2},{1,3},{2,0},{3,1},{4,6},{5,7},{6,4},{7,5},{8,10},{9,11},{10,... | collective-permute-start | bytes 393224 | tf_op jit(solution)/shard_map/ppermute | solution.py:32
  18.8 5.8 %collective-permute-start.6 = (bf16[1,256,256]{2,1,0:T(8,128)(2,1)S(1)}, bf16[1,256,256]{2,1,0:T(8,128)(2,1)S(1)}, u32[]{:S(2)}, u32[]{:S(2)}) collective-permute-start(bf16[1,256,256]{2,1,0:T(8,128)(2,1)S(1)} %collective-permute-done.3), channel_id=1, source_target_pairs={{0,4},{1,5},{2,6},{3,7},{4,0},{5,1},{6,2},{7,3},{8,12},{9,13},{10,... | collective-permute-start | bytes 393224 | tf_op jit(solution)/shard_map/ppermute | solution.py:32
  20.5 6.4 %collective-permute-start.13 = (bf16[2,256,256]{2,1,0:T(8,128)(2,1)S(1)}, bf16[2,256,256]{2,1,0:T(8,128)(2,1)S(1)}, u32[]{:S(2)}, u32[]{:S(2)}) collective-permute-start(bf16[2,256,256]{2,1,0:T(8,128)(2,1)S(1)} %constant_dynamic-update-slice_fusion.4.rest_4_), channel_id=1, source_target_pairs={{0,2},{1,3},{2,0},{3,1},{4,6},{5,7},{6,4},{7,5},{8,10},{9,11},{10,... | collective-permute-start | bytes 786440 | tf_op jit(solution)/shard_map/ppermute | solution.py:32
  23.4 3.5 %collective-permute-start.12 = (bf16[2,256,256]{2,1,0:T(8,128)(2,1)S(1)}, bf16[2,256,256]{2,1,0:T(8,128)(2,1)S(1)}, u32[]{:S(2)}, u32[]{:S(2)}) collective-permute-start(bf16[2,256,256]{2,1,0:T(8,128)(2,1)S(1)} %constant_dynamic-update-slice_fusion.4.rest_4_), channel_id=1, source_target_pairs={{0,1},{1,0},{2,3},{3,2},{4,5},{5,4},{6,7},{7,6},{8,9},{9,8},{10,11... | collective-permute-start | bytes 786440 | tf_op jit(solution)/shard_map/ppermute | solution.py:32
  24.6 3.8 %collective-permute-start.16 = (bf16[2,256,256]{2,1,0:T(8,128)(2,1)S(1)}, bf16[2,256,256]{2,1,0:T(8,128)(2,1)S(1)}, u32[]{:S(2)}, u32[]{:S(2)}) collective-permute-start(bf16[2,256,256]{2,1,0:T(8,128)(2,1)S(1)} %constant_dynamic-update-slice_fusion.2.rest_10_), channel_id=1, source_target_pairs={{0,1},{1,0},{2,3},{3,2},{4,5},{5,4},{6,7},{7,6},{8,9},{9,8},{10,11... | collective-permute-start | bytes 786440 | tf_op jit(solution)/shard_map/ppermute | solution.py:32
  24.7 21.9 %copy-start.1 = (bf16[512,4096]{1,0:T(8,128)(2,1)S(1)}, bf16[512,4096]{1,0:T(8,128)(2,1)}, u32[]{:S(2)}) copy-start(bf16[512,4096]{1,0:T(8,128)(2,1)} %act_ref.2) | copy-start | bytes 12582916
  24.7 21.9 %copy-start.4 = (bf16[16,4096]{1,0:T(8,128)(2,1)S(1)}, bf16[16,4096]{1,0:T(8,128)(2,1)}, u32[]{:S(2)}) copy-start(bf16[16,4096]{1,0:T(8,128)(2,1)} %adapter_ref.1) | copy-start | bytes 393220
  24.7 4.2 %collective-permute-start.15 = (bf16[2,256,256]{2,1,0:T(8,128)(2,1)S(1)}, bf16[2,256,256]{2,1,0:T(8,128)(2,1)S(1)}, u32[]{:S(2)}, u32[]{:S(2)}) collective-permute-start(bf16[2,256,256]{2,1,0:T(8,128)(2,1)S(1)} %constant_dynamic-update-slice_fusion.rest_8_), channel_id=1, source_target_pairs={{0,1},{1,0},{2,3},{3,2},{4,5},{5,4},{6,7},{7,6},{8,9},{9,8},{10,11... | collective-permute-start | bytes 786440 | tf_op jit(solution)/shard_map/ppermute | solution.py:32
  25.3 3.6 %collective-permute-start.11 = (bf16[2,256,256]{2,1,0:T(8,128)(2,1)S(1)}, bf16[2,256,256]{2,1,0:T(8,128)(2,1)S(1)}, u32[]{:S(2)}, u32[]{:S(2)}) collective-permute-start(bf16[2,256,256]{2,1,0:T(8,128)(2,1)S(1)} %collective-permute-done.7.rest_2_), channel_id=1, source_target_pairs={{0,1},{1,0},{2,3},{3,2},{4,5},{5,4},{6,7},{7,6},{8,9},{9,8},{10,11... | collective-permute-start | bytes 786440 | tf_op jit(solution)/shard_map/ppermute | solution.py:32
  26.9 2.0 %collective-permute-start.14 = (bf16[2,256,256]{2,1,0:T(8,128)(2,1)S(1)}, bf16[2,256,256]{2,1,0:T(8,128)(2,1)S(1)}, u32[]{:S(2)}, u32[]{:S(2)}) collective-permute-start(bf16[2,256,256]{2,1,0:T(8,128)(2,1)S(1)} %collective-permute-done.13.rest_6_), channel_id=1, source_target_pairs={{0,1},{1,0},{2,3},{3,2},{4,5},{5,4},{6,7},{7,6},{8,9},{9,8},{10,11... | collective-permute-start | bytes 786440 | tf_op jit(solution)/shard_map/ppermute | solution.py:32
  26.9 8.7 %collective-permute-start.9 = (bf16[2,256,256]{2,1,0:T(8,128)(2,1)S(1)}, bf16[2,256,256]{2,1,0:T(8,128)(2,1)S(1)}, u32[]{:S(2)}, u32[]{:S(2)}) collective-permute-start(bf16[2,256,256]{2,1,0:T(8,128)(2,1)S(1)} %constant_dynamic-update-slice_fusion.2.rest_10_), channel_id=1, source_target_pairs={{0,2},{1,3},{2,0},{3,1},{4,6},{5,7},{6,4},{7,5},{8,10},{9,11},{10,... | collective-permute-start | bytes 786440 | tf_op jit(solution)/shard_map/ppermute | solution.py:32
  28.4 8.4 %collective-permute-start.8 = (bf16[2,256,256]{2,1,0:T(8,128)(2,1)S(1)}, bf16[2,256,256]{2,1,0:T(8,128)(2,1)S(1)}, u32[]{:S(2)}, u32[]{:S(2)}) collective-permute-start(bf16[2,256,256]{2,1,0:T(8,128)(2,1)S(1)} %constant_dynamic-update-slice_fusion.rest_8_), channel_id=1, source_target_pairs={{0,4},{1,5},{2,6},{3,7},{4,0},{5,1},{6,2},{7,3},{8,12},{9,13},{10,... | collective-permute-start | bytes 786440 | tf_op jit(solution)/shard_map/ppermute | solution.py:32
  36.8 1.5 %collective-permute-start.17 = (bf16[2,256,256]{2,1,0:T(8,128)(2,1)S(1)}, bf16[2,256,256]{2,1,0:T(8,128)(2,1)S(1)}, u32[]{:S(2)}, u32[]{:S(2)}) collective-permute-start(bf16[2,256,256]{2,1,0:T(8,128)(2,1)S(1)} %collective-permute-done.8.rest_0_.rest_12_), channel_id=1, source_target_pairs={{0,1},{1,0},{2,3},{3,2},{4,5},{5,4},{6,7},{7,6},{8,9},{9,8},{10,11... | collective-permute-start | bytes 786440 | tf_op jit(solution)/shard_map/ppermute | solution.py:32
  36.8 1.9 %collective-permute-start.18 = (bf16[2,256,256]{2,1,0:T(8,128)(2,1)S(1)}, bf16[2,256,256]{2,1,0:T(8,128)(2,1)S(1)}, u32[]{:S(2)}, u32[]{:S(2)}) collective-permute-start(bf16[2,256,256]{2,1,0:T(8,128)(2,1)S(1)} %collective-permute-done.9.rest_2_.rest_14_), channel_id=1, source_target_pairs={{0,1},{1,0},{2,3},{3,2},{4,5},{5,4},{6,7},{7,6},{8,9},{9,8},{10,11... | collective-permute-start | bytes 786440 | tf_op jit(solution)/shard_map/ppermute | solution.py:32
  40.2 11.9 %copy-start = (bf16[512,4096]{1,0:T(8,128)(2,1)S(1)}, bf16[512,4096]{1,0:T(8,128)(2,1)}, u32[]{:S(2)}) copy-start(bf16[512,4096]{1,0:T(8,128)(2,1)} %act_ref.3) | copy-start | bytes 12582916
  40.2 11.9 %copy-start.5 = (bf16[4096,16]{0,1:T(8,128)(2,1)S(1)}, bf16[4096,16]{0,1:T(8,128)(2,1)}, u32[]{:S(2)}) copy-start(bf16[4096,16]{0,1:T(8,128)(2,1)} %param.18) | copy-start | bytes 393220
  40.2 11.9 %copy-start.6 = (s32[1,512]{1,0:T(1,128)S(1)}, s32[1,512]{1,0:T(1,128)}, u32[]{:S(2)}) copy-start(s32[1,512]{1,0:T(1,128)} %index_ref.3) | copy-start | bytes 6148
  40.2 9.3 %collective-permute-start.21 = (bf16[1,288,256]{2,1,0:T(8,128)(2,1)S(1)}, bf16[1,288,256]{2,1,0:T(8,128)(2,1)S(1)}, u32[]{:S(2)}, u32[]{:S(2)}) collective-permute-start(bf16[1,288,256]{2,1,0:T(8,128)(2,1)S(1)} %eval_factors.1), channel_id=1, source_target_pairs={{0,2},{1,3},{2,0},{3,1},{4,6},{5,7},{6,4},{7,5},{8,10},{9,11},{10,... | collective-permute-start | bytes 442376 | tf_op jit(solution)/shard_map/ppermute | solution.py:32
  40.8 9.1 %collective-permute-start.22 = (bf16[1,288,256]{2,1,0:T(8,128)(2,1)S(1)}, bf16[1,288,256]{2,1,0:T(8,128)(2,1)S(1)}, u32[]{:S(2)}, u32[]{:S(2)}) collective-permute-start(bf16[1,288,256]{2,1,0:T(8,128)(2,1)S(1)} %eval_factors.1), channel_id=1, source_target_pairs={{0,8},{1,9},{2,10},{3,11},{4,12},{5,13},{6,14},{7,15},{8,0},{9,1},... | collective-permute-start | bytes 442376 | tf_op jit(solution)/shard_map/ppermute | solution.py:32
  44.0 14.0 %collective-permute-start.19 = (bf16[1,288,256]{2,1,0:T(8,128)(2,1)S(1)}, bf16[1,288,256]{2,1,0:T(8,128)(2,1)S(1)}, u32[]{:S(2)}, u32[]{:S(2)}) collective-permute-start(bf16[1,288,256]{2,1,0:T(8,128)(2,1)S(1)} %eval_factors.1), channel_id=1, source_target_pairs={{0,16},{1,17},{2,18},{3,19},{4,20},{5,21},{6,22},{7,23},{8,24},{9,... | collective-permute-start | bytes 442376 | tf_op jit(solution)/shard_map/ppermute | solution.py:32
  45.1 12.9 %collective-permute-start.20 = (bf16[1,288,256]{2,1,0:T(8,128)(2,1)S(1)}, bf16[1,288,256]{2,1,0:T(8,128)(2,1)S(1)}, u32[]{:S(2)}, u32[]{:S(2)}) collective-permute-start(bf16[1,288,256]{2,1,0:T(8,128)(2,1)S(1)} %eval_factors.1), channel_id=1, source_target_pairs={{0,24},{1,25},{2,26},{3,27},{4,28},{5,29},{6,30},{7,31},{8,16},{9,... | collective-permute-start | bytes 442376 | tf_op jit(solution)/shard_map/ppermute | solution.py:32
  50.0 21.2 %collective-permute-start.26 = (bf16[2,288,256]{2,1,0:T(8,128)(2,1)S(1)}, bf16[2,288,256]{2,1,0:T(8,128)(2,1)S(1)}, u32[]{:S(2)}, u32[]{:S(2)}) collective-permute-start(bf16[2,288,256]{2,1,0:T(8,128)(2,1)S(1)} %pad_maximum_fusion.rest_0_), channel_id=1, source_target_pairs={{0,4},{1,5},{2,6},{3,7},{4,0},{5,1},{6,2},{7,3},{8,12},{9,13},{10,... | collective-permute-start | bytes 884744 | tf_op jit(solution)/shard_map/ppermute | solution.py:32
  51.4 20.5 %collective-permute-start.29 = (bf16[2,288,256]{2,1,0:T(8,128)(2,1)S(1)}, bf16[2,288,256]{2,1,0:T(8,128)(2,1)S(1)}, u32[]{:S(2)}, u32[]{:S(2)}) collective-permute-start(bf16[2,288,256]{2,1,0:T(8,128)(2,1)S(1)} %pad_maximum_fusion.rest_0_), channel_id=1, source_target_pairs={{0,1},{1,0},{2,3},{3,2},{4,5},{5,4},{6,7},{7,6},{8,9},{9,8},{10,11... | collective-permute-start | bytes 884744 | tf_op jit(solution)/shard_map/ppermute | solution.py:32
  51.4 9.6 %collective-permute-start.23 = (bf16[1,288,256]{2,1,0:T(8,128)(2,1)S(1)}, bf16[1,288,256]{2,1,0:T(8,128)(2,1)S(1)}, u32[]{:S(2)}, u32[]{:S(2)}) collective-permute-start(bf16[1,288,256]{2,1,0:T(8,128)(2,1)S(1)} %collective-permute-done.22), channel_id=1, source_target_pairs={{0,4},{1,5},{2,6},{3,7},{4,0},{5,1},{6,2},{7,3},{8,12},{9,13},{10,... | collective-permute-start | bytes 442376 | tf_op jit(solution)/shard_map/ppermute | solution.py:32
  61.0 23.7 %copy-start.7 = (s32[32,16]{0,1:T(8,128)S(1)}, s32[32,16]{0,1:T(8,128)}, u32[]{:S(2)}) copy-start(s32[32,16]{0,1:T(8,128)} %param.22) | copy-start | bytes 6148
  61.1 23.6 %copy-start.9 = (s32[32]{0:T(128)S(1)}, s32[32]{0:T(128)}, u32[]{:S(2)}) copy-start(s32[32]{0:T(128)} %live_ref.1) | copy-start | bytes 388
  61.1 11.3 %collective-permute-start.32 = (bf16[2,288,256]{2,1,0:T(8,128)(2,1)S(1)}, bf16[2,288,256]{2,1,0:T(8,128)(2,1)S(1)}, u32[]{:S(2)}, u32[]{:S(2)}) collective-permute-start(bf16[2,288,256]{2,1,0:T(8,128)(2,1)S(1)} %constant_dynamic-update-slice_fusion.10.rest_4_), channel_id=1, source_target_pairs={{0,2},{1,3},{2,0},{3,1},{4,6},{5,7},{6,4},{7,5},{8,10},{9,11},{10,... | collective-permute-start | bytes 884744 | tf_op jit(solution)/shard_map/ppermute | solution.py:32
  62.3 8.9 %collective-permute-start.24 = (bf16[1,288,256]{2,1,0:T(8,128)(2,1)S(1)}, bf16[1,288,256]{2,1,0:T(8,128)(2,1)S(1)}, u32[]{:S(2)}, u32[]{:S(2)}) collective-permute-start(bf16[1,288,256]{2,1,0:T(8,128)(2,1)S(1)} %collective-permute-done.19), channel_id=1, source_target_pairs={{0,2},{1,3},{2,0},{3,1},{4,6},{5,7},{6,4},{7,5},{8,10},{9,11},{10,... | collective-permute-start | bytes 442376 | tf_op jit(solution)/shard_map/ppermute | solution.py:32
  63.2 8.0 %collective-permute-start.25 = (bf16[1,288,256]{2,1,0:T(8,128)(2,1)S(1)}, bf16[1,288,256]{2,1,0:T(8,128)(2,1)S(1)}, u32[]{:S(2)}, u32[]{:S(2)}) collective-permute-start(bf16[1,288,256]{2,1,0:T(8,128)(2,1)S(1)} %collective-permute-done.20), channel_id=1, source_target_pairs={{0,4},{1,5},{2,6},{3,7},{4,0},{5,1},{6,2},{7,3},{8,12},{9,13},{10,... | collective-permute-start | bytes 442376 | tf_op jit(solution)/shard_map/ppermute | solution.py:32
  71.2 1.6 %collective-permute-start.31 = (bf16[2,288,256]{2,1,0:T(8,128)(2,1)S(1)}, bf16[2,288,256]{2,1,0:T(8,128)(2,1)S(1)}, u32[]{:S(2)}, u32[]{:S(2)}) collective-permute-start(bf16[2,288,256]{2,1,0:T(8,128)(2,1)S(1)} %constant_dynamic-update-slice_fusion.10.rest_4_), channel_id=1, source_target_pairs={{0,1},{1,0},{2,3},{3,2},{4,5},{5,4},{6,7},{7,6},{8,9},{9,8},{10,11... | collective-permute-start | bytes 884744 | tf_op jit(solution)/shard_map/ppermute | solution.py:32
  71.2 2.7 %collective-permute-start.35 = (bf16[2,288,256]{2,1,0:T(8,128)(2,1)S(1)}, bf16[2,288,256]{2,1,0:T(8,128)(2,1)S(1)}, u32[]{:S(2)}, u32[]{:S(2)}) collective-permute-start(bf16[2,288,256]{2,1,0:T(8,128)(2,1)S(1)} %constant_dynamic-update-slice_fusion.8.rest_10_), channel_id=1, source_target_pairs={{0,1},{1,0},{2,3},{3,2},{4,5},{5,4},{6,7},{7,6},{8,9},{9,8},{10,11... | collective-permute-start | bytes 884744 | tf_op jit(solution)/shard_map/ppermute | solution.py:32
  71.8 2.9 %collective-permute-start.34 = (bf16[2,288,256]{2,1,0:T(8,128)(2,1)S(1)}, bf16[2,288,256]{2,1,0:T(8,128)(2,1)S(1)}, u32[]{:S(2)}, u32[]{:S(2)}) collective-permute-start(bf16[2,288,256]{2,1,0:T(8,128)(2,1)S(1)} %constant_dynamic-update-slice_fusion.6.rest_8_), channel_id=1, source_target_pairs={{0,1},{1,0},{2,3},{3,2},{4,5},{5,4},{6,7},{7,6},{8,9},{9,8},{10,11... | collective-permute-start | bytes 884744 | tf_op jit(solution)/shard_map/ppermute | solution.py:32
  71.9 2.9 %collective-permute-start.30 = (bf16[2,288,256]{2,1,0:T(8,128)(2,1)S(1)}, bf16[2,288,256]{2,1,0:T(8,128)(2,1)S(1)}, u32[]{:S(2)}, u32[]{:S(2)}) collective-permute-start(bf16[2,288,256]{2,1,0:T(8,128)(2,1)S(1)} %collective-permute-done.26.rest_2_), channel_id=1, source_target_pairs={{0,1},{1,0},{2,3},{3,2},{4,5},{5,4},{6,7},{7,6},{8,9},{9,8},{10,11... | collective-permute-start | bytes 884744 | tf_op jit(solution)/shard_map/ppermute | solution.py:32
  72.4 2.4 %collective-permute-start.33 = (bf16[2,288,256]{2,1,0:T(8,128)(2,1)S(1)}, bf16[2,288,256]{2,1,0:T(8,128)(2,1)S(1)}, u32[]{:S(2)}, u32[]{:S(2)}) collective-permute-start(bf16[2,288,256]{2,1,0:T(8,128)(2,1)S(1)} %collective-permute-done.32.rest_6_), channel_id=1, source_target_pairs={{0,1},{1,0},{2,3},{3,2},{4,5},{5,4},{6,7},{7,6},{8,9},{9,8},{10,11... | collective-permute-start | bytes 884744 | tf_op jit(solution)/shard_map/ppermute | solution.py:32
  72.8 9.1 %collective-permute-start.28 = (bf16[2,288,256]{2,1,0:T(8,128)(2,1)S(1)}, bf16[2,288,256]{2,1,0:T(8,128)(2,1)S(1)}, u32[]{:S(2)}, u32[]{:S(2)}) collective-permute-start(bf16[2,288,256]{2,1,0:T(8,128)(2,1)S(1)} %constant_dynamic-update-slice_fusion.8.rest_10_), channel_id=1, source_target_pairs={{0,2},{1,3},{2,0},{3,1},{4,6},{5,7},{6,4},{7,5},{8,10},{9,11},{10,... | collective-permute-start | bytes 884744 | tf_op jit(solution)/shard_map/ppermute | solution.py:32
  73.9 8.8 %collective-permute-start.27 = (bf16[2,288,256]{2,1,0:T(8,128)(2,1)S(1)}, bf16[2,288,256]{2,1,0:T(8,128)(2,1)S(1)}, u32[]{:S(2)}, u32[]{:S(2)}) collective-permute-start(bf16[2,288,256]{2,1,0:T(8,128)(2,1)S(1)} %constant_dynamic-update-slice_fusion.6.rest_8_), channel_id=1, source_target_pairs={{0,4},{1,5},{2,6},{3,7},{4,0},{5,1},{6,2},{7,3},{8,12},{9,13},{10,... | collective-permute-start | bytes 884744 | tf_op jit(solution)/shard_map/ppermute | solution.py:32
  82.7 1.6 %collective-permute-start.36 = (bf16[2,288,256]{2,1,0:T(8,128)(2,1)S(1)}, bf16[2,288,256]{2,1,0:T(8,128)(2,1)S(1)}, u32[]{:S(2)}, u32[]{:S(2)}) collective-permute-start(bf16[2,288,256]{2,1,0:T(8,128)(2,1)S(1)} %collective-permute-done.27.rest_0_), channel_id=1, source_target_pairs={{0,1},{1,0},{2,3},{3,2},{4,5},{5,4},{6,7},{7,6},{8,9},{9,8},{10,11... | collective-permute-start | bytes 884744 | tf_op jit(solution)/shard_map/ppermute | solution.py:32
  82.7 2.0 %collective-permute-start.37 = (bf16[2,288,256]{2,1,0:T(8,128)(2,1)S(1)}, bf16[2,288,256]{2,1,0:T(8,128)(2,1)S(1)}, u32[]{:S(2)}, u32[]{:S(2)}) collective-permute-start(bf16[2,288,256]{2,1,0:T(8,128)(2,1)S(1)} %collective-permute-done.28.rest_2_), channel_id=1, source_target_pairs={{0,1},{1,0},{2,3},{3,2},{4,5},{5,4},{6,7},{7,6},{8,9},{9,8},{10,11... | collective-permute-start | bytes 884744 | tf_op jit(solution)/shard_map/ppermute | solution.py:32

commit v4 on v3

--- a/solution.py
+++ b/solution.py
@@ -65,6 +65,7 @@
         held.append(join(chunk))
         second.append(permute(held[chunk], orders[chunk][1]))
         swapped.append(permute(held[chunk], 1))
+    second[1] = lax.optimization_barrier((second[1], held[2], held[3]))[0]
     front = near(0) + far(0) + near(1) + far(1) + near(2) + near(3)
     done = late(front, third)
     second[2], second[3], done = lax.optimization_barrier((second[2], second[3], done))
@@ -250,7 +251,7 @@
         out_specs=jax.tree.map(lambda _: VMEM, out_shape),
         scratch_shapes=scratch,
         compiler_params=pltpu.CompilerParams(vmem_limit_bytes=28 * 1024 * 1024),
-        cost_estimate=pl.CostEstimate(flops=flops, bytes_accessed=4 * 2**20, transcendentals=0),
+        cost_estimate=pl.CostEstimate(flops=flops // 1000, bytes_accessed=4096, transcendentals=0),
         name=name,
     )(*scalars, *arrays)
 
@@ -317,17 +318,19 @@
     rows = RANK * TRAIN_EXAMPLES
     values_shape = jax.ShapeDtypeStruct((train_layer_input.shape[0], PW), F32)
     factor_shape = jax.ShapeDtypeStruct((RANK, train_layer_input.shape[0]), F32)
-    gradient_side = call(
-        functools.partial(train_kernel, every, size, 0),
-        [values_shape, factor_shape],
-        held,
-        2 * 10**9,
-        "train_gradient_side",
-        [place],
-        train_output_gradient,
-        adapter_up,
-        *everything,
-    )
+
+    def gradient_side(early):
+        return call(
+            functools.partial(train_kernel, every, size, 0),
+            [values_shape, factor_shape],
+            held,
+            2 * 10**9,
+            "train_gradient_side",
+            [early[0]],
+            train_output_gradient,
+            adapter_up,
+            *everything,
+        )
 
     def input_side(gradient_side):
         values, back = gradient_side
@@ -346,8 +349,9 @@
         )
         return hidden, values, raw, total
 
-    def features(sides):
+    def features(gradient_side):
         shape = jax.ShapeDtypeStruct((2, rows, PW), BF16)
+        sides = input_side(gradient_side)
         return call(feats_kernel, shape, [], 10**9, "train_features", [], *sides, train_example_index)
 
     def tile(front, feats):
@@ -355,7 +359,7 @@
         kernel = functools.partial(tile_kernel, steps, size)
         return call(kernel, jax.ShapeDtypeStruct(tiles_shape, F32), [], 10**9, "front_tiles", [place], feats, *arrays)
 
-    tiles, front, back, _, _, feats = gather_blocks(pack, n, gradient_side, input_side, features, tile)
+    tiles, front, back, _, _, feats = gather_blocks(pack, n, (place,), gradient_side, features, tile)
     steps, arrays = plan(back)
     scores = call(
         functools.partial(score_kernel, steps, plan(front)[0], size),

time: 87.8 us -> 84.4 us (0.961); the launches traced: 87.6 us -> 83.3 us
  waiting for transfers between devices: 31.6 us -> 26.8 us
    ppermute x38, waiting for transfers between devices: 31.6 us -> 26.8 us  [permute(): return lax.ppermute(held, 'train', [(i, i ^ mask) for i in range(n)])]
  transfers between devices with their start and end apart: 38 -> 38, of which waited for: 18 -> 17; matrix products, arithmetic and copies ran while one was open for 4% -> 4% of each run, Pallas kernels for 17% -> 18%
where the time goes in v4:
time: 84.4 us; the launch traced here: 83.3 us
  starting transfers between devices  32.4 us (38%)
  waiting for transfers between devices  26.8 us (32%)
  Pallas kernels  19 us (23%)
  matrix products  3.38 us (4%)
  other arithmetic  1.17 us (1%)
    ppermute x38, starting transfers between devices, permute(): return lax.ppermute(held, 'train', [(i, i ^ mask) for i in range(n)])  32.4 us
    ppermute x38, waiting for transfers between devices, permute(): return lax.ppermute(held, 'train', [(i, i ^ mask) for i in range(n)])  26.8 us
    pallas_call x7, Pallas kernels, call(): pl.pallas_call(kernel, out_shape=out_shape, in_specs=[SMEM] * len(scalars...  19 us
    dot_general x1, matrix products, up(): return lax.dot_general(adapter_up, g, NT, preferred_element_type=F32)  1.7 us
  transfers between devices with their start and end apart: 38, of which 17 were waited for; matrix products, arithmetic and copies ran while one was open for 4% of the time, Pallas kernels for 18%

profile of v4, /device:TPU:0, one launch (start us, length us, event | category | flops | bytes accessed | tf_op | source)
XLA Modules:
  0.0 83.3 jit_solution(16407307199090041867)
XLA Ops:
  0.0 1.0 %maximum_bitcast_fusion = bf16[1,256,256]{2,1,0:T(8,128)(2,1)S(1)} fusion(bf16[128,256]{1,0:T(8,128)(2,1)} %param.21, bf16[128,256]{1,0:T(8,128)(2,1)} %param.20), kind=kLoop, calls=%fused_computation.2 | loop fusion | flops 262144 | bytes 262144 | tf_op jit(solution)/shard_map/broadcast_in_dim | solution.py:297
  1.0 3.0 %collective-permute-start = (bf16[1,256,256]{2,1,0:T(8,128)(2,1)S(1)}, bf16[1,256,256]{2,1,0:T(8,128)(2,1)S(1)}, u32[]{:S(2)}, u32[]{:S(2)}) collective-permute-start(bf16[1,256,256]{2,1,0:T(8,128)(2,1)S(1)} %maximum_bitcast_fusion), channel_id=1, source_target_pairs={{0,2},{1,3},{2,0},{3,1},{4,6},{5,7},{6,4},{7,5},{8,10},{9,11},{10,... | collective-permute-start | bytes 393224 | tf_op jit(solution)/shard_map/ppermute | solution.py:32
  4.0 1.6 %collective-permute-start.1 = (bf16[1,256,256]{2,1,0:T(8,128)(2,1)S(1)}, bf16[1,256,256]{2,1,0:T(8,128)(2,1)S(1)}, u32[]{:S(2)}, u32[]{:S(2)}) collective-permute-start(bf16[1,256,256]{2,1,0:T(8,128)(2,1)S(1)} %maximum_bitcast_fusion), channel_id=1, source_target_pairs={{0,8},{1,9},{2,10},{3,11},{4,12},{5,13},{6,14},{7,15},{8,0},{9,1},... | collective-permute-start | bytes 393224 | tf_op jit(solution)/shard_map/ppermute | solution.py:32
  5.6 2.6 %collective-permute-start.2 = (bf16[1,256,256]{2,1,0:T(8,128)(2,1)S(1)}, bf16[1,256,256]{2,1,0:T(8,128)(2,1)S(1)}, u32[]{:S(2)}, u32[]{:S(2)}) collective-permute-start(bf16[1,256,256]{2,1,0:T(8,128)(2,1)S(1)} %maximum_bitcast_fusion), channel_id=1, source_target_pairs={{0,16},{1,17},{2,18},{3,19},{4,20},{5,21},{6,22},{7,23},{8,24},{9,... | collective-permute-start | bytes 393224 | tf_op jit(solution)/shard_map/ppermute | solution.py:32
  8.2 0.2 collective-permute-start.3
  8.4 1.7 %fusion.hidden_ref = f32[16,128]{1,0:T(8,128)S(1)} fusion(bf16[4096,16]{0,1:T(8,128)(2,1)} %param.18, bf16[128,4096]{1,0:T(8,128)(2,1)} %x_ref.3), kind=kOutput, calls=%fused_computation.16 | convolution fusion | flops 16777216 | bytes 1187840 | tf_op jit(solution)/shard_map/dot_general | solution.py:282
  10.1 1.7 %fusion.1.back_ref = f32[16,128]{1,0:T(8,128)S(1)} fusion(bf16[16,4096]{1,0:T(8,128)(2,1)} %adapter_ref.1, bf16[128,4096]{1,0:T(8,128)(2,1)} %g_ref.3), kind=kOutput, calls=%fused_computation.17 | convolution fusion | flops 16777216 | bytes 1187840 | tf_op jit(solution)/shard_map/dot_general | solution.py:285
  11.8 0.1 pad_add_fusion.place_ref
  11.9 1.6 %collective-permute-start.4 = (bf16[1,256,256]{2,1,0:T(8,128)(2,1)S(1)}, bf16[1,256,256]{2,1,0:T(8,128)(2,1)S(1)}, u32[]{:S(2)}, u32[]{:S(2)}) collective-permute-start(bf16[1,256,256]{2,1,0:T(8,128)(2,1)S(1)} %collective-permute-done.1), channel_id=1, source_target_pairs={{0,4},{1,5},{2,6},{3,7},{4,0},{5,1},{6,2},{7,3},{8,12},{9,13},{10,... | collective-permute-start | bytes 393224 | tf_op jit(solution)/shard_map/ppermute | solution.py:32
  13.5 0.6 collective-permute-start.7
  14.1 0.1 collective-permute-start.10
  14.2 4.1 %collective-permute-done.2 = bf16[1,256,256]{2,1,0:T(8,128)(2,1)S(1)} collective-permute-done((bf16[1,256,256]{2,1,0:T(8,128)(2,1)S(1)}, bf16[1,256,256]{2,1,0:T(8,128)(2,1)S(1)}, u32[]{:S(2)}, u32[]{:S(2)}) %collective-permute-start.2) | collective-permute-done | bytes 131104 | tf_op jit(solution)/shard_map/ppermute | solution.py:32
  18.3 0.1 collective-permute-done.4
  18.4 0.4 collective-permute-start.5
  18.8 1.6 %collective-permute-start.6 = (bf16[1,256,256]{2,1,0:T(8,128)(2,1)S(1)}, bf16[1,256,256]{2,1,0:T(8,128)(2,1)S(1)}, u32[]{:S(2)}, u32[]{:S(2)}) collective-permute-start(bf16[1,256,256]{2,1,0:T(8,128)(2,1)S(1)} %collective-permute-done.3), channel_id=1, source_target_pairs={{0,4},{1,5},{2,6},{3,7},{4,0},{5,1},{6,2},{7,3},{8,12},{9,13},{10,... | collective-permute-start | bytes 393224 | tf_op jit(solution)/shard_map/ppermute | solution.py:32
  20.5 1.6 %collective-permute-start.13 = (bf16[2,256,256]{2,1,0:T(8,128)(2,1)S(1)}, bf16[2,256,256]{2,1,0:T(8,128)(2,1)S(1)}, u32[]{:S(2)}, u32[]{:S(2)}) collective-permute-start(bf16[2,256,256]{2,1,0:T(8,128)(2,1)S(1)} %constant_dynamic-update-slice_fusion.4.rest_4_), channel_id=1, source_target_pairs={{0,2},{1,3},{2,0},{3,1},{4,6},{5,7},{6,4},{7,5},{8,10},{9,11},{10,... | collective-permute-start | bytes 786440 | tf_op jit(solution)/shard_map/ppermute | solution.py:32
  22.0 1.4 %collective-permute-done.5 = bf16[1,256,256]{2,1,0:T(8,128)(2,1)S(1)} collective-permute-done((bf16[1,256,256]{2,1,0:T(8,128)(2,1)S(1)}, bf16[1,256,256]{2,1,0:T(8,128)(2,1)S(1)}, u32[]{:S(2)}, u32[]{:S(2)}) %collective-permute-start.5) | collective-permute-done | bytes 131104 | tf_op jit(solution)/shard_map/ppermute | solution.py:32
  23.4 1.2 %collective-permute-done.6 = bf16[1,256,256]{2,1,0:T(8,128)(2,1)S(1)} collective-permute-done((bf16[1,256,256]{2,1,0:T(8,128)(2,1)S(1)}, bf16[1,256,256]{2,1,0:T(8,128)(2,1)S(1)}, u32[]{:S(2)}, u32[]{:S(2)}) %collective-permute-start.6) | collective-permute-done | bytes 131104 | tf_op jit(solution)/shard_map/ppermute | solution.py:32
  24.6 0.1 collective-permute-start.16
  24.7 0.0 copy-start.3
  24.7 0.6 collective-permute-start.15
  25.3 1.6 %collective-permute-done.13.rest_6_ = bf16[2,256,256]{2,1,0:T(8,128)(2,1)S(1)} collective-permute-done((bf16[2,256,256]{2,1,0:T(8,128)(2,1)S(1)}, bf16[2,256,256]{2,1,0:T(8,128)(2,1)S(1)}, u32[]{:S(2)}, u32[]{:S(2)}) %collective-permute-start.13) | collective-permute-done | bytes 262176 | tf_op jit(solution)/shard_map/ppermute | solution.py:32
  26.9 0.5 collective-permute-start.14
  27.4 1.5 %collective-permute-start.9 = (bf16[2,256,256]{2,1,0:T(8,128)(2,1)S(1)}, bf16[2,256,256]{2,1,0:T(8,128)(2,1)S(1)}, u32[]{:S(2)}, u32[]{:S(2)}) collective-permute-start(bf16[2,256,256]{2,1,0:T(8,128)(2,1)S(1)} %constant_dynamic-update-slice_fusion.2.rest_10_), channel_id=1, source_target_pairs={{0,2},{1,3},{2,0},{3,1},{4,6},{5,7},{6,4},{7,5},{8,10},{9,11},{10,... | collective-permute-start | bytes 786440 | tf_op jit(solution)/shard_map/ppermute | solution.py:32
  28.9 0.5 collective-permute-start.8
  29.4 1.7 %eval_begin.1.rest_4_ = f32[2,128,256]{2,1,0:T(8,128)S(1)} custom-call(s32[3]{0:T(128)S(1)} %pad_add_fusion.place_ref, bf16[128,4096]{1,0:T(8,128)(2,1)S(1)} %copy-done, bf16[128,4096]{1,0:T(8,128)(2,1)S(1)} %copy-done.1, bf16[2,256,256]{2,1,0:T(8,128)(2,1)S(1)} %pad_maximum_fusion.1.rest_0_, bf16[2,256,256]{2,1,0:T(8,128)(2,1)S(1)} %collective-permute-done.10.rest_1_, ...), custom_call_target="tpu_custom_call" | custom-call | flops 800000 | bytes 4096 | tf_op jit(solution)/shard_map/eval_begin/pallas_call | solution.py:247
  31.1 4.6 %collective-permute-done.9.rest_2_.rest_14_ = bf16[2,256,256]{2,1,0:T(8,128)(2,1)S(1)} collective-permute-done((bf16[2,256,256]{2,1,0:T(8,128)(2,1)S(1)}, bf16[2,256,256]{2,1,0:T(8,128)(2,1)S(1)}, u32[]{:S(2)}, u32[]{:S(2)}) %collective-permute-start.9) | collective-permute-done | bytes 262176 | tf_op jit(solution)/shard_map/ppermute | solution.py:32
  35.7 1.2 %collective-permute-done.8.rest_0_.rest_12_ = bf16[2,256,256]{2,1,0:T(8,128)(2,1)S(1)} collective-permute-done((bf16[2,256,256]{2,1,0:T(8,128)(2,1)S(1)}, bf16[2,256,256]{2,1,0:T(8,128)(2,1)S(1)}, u32[]{:S(2)}, u32[]{:S(2)}) %collective-permute-start.8) | collective-permute-done | bytes 262176 | tf_op jit(solution)/shard_map/ppermute | solution.py:32
  36.9 0.5 collective-permute-start.18
  37.4 1.0 %collective-permute-done.17.rest_1_.rest_13_ = bf16[2,256,256]{2,1,0:T(8,128)(2,1)S(1)} collective-permute-done((bf16[2,256,256]{2,1,0:T(8,128)(2,1)S(1)}, bf16[2,256,256]{2,1,0:T(8,128)(2,1)S(1)}, u32[]{:S(2)}, u32[]{:S(2)}) %collective-permute-start.17) | collective-permute-done | bytes 262176 | tf_op jit(solution)/shard_map/ppermute | solution.py:32
  38.4 0.4 collective-permute-done.18.rest_3_.rest_15_
  38.8 1.4 %eval_factors.1 = bf16[1,288,256]{2,1,0:T(8,128)(2,1)S(1)} custom-call(s32[3]{0:T(128)S(1)} %pad_add_fusion.place_ref, bf16[128,4096]{1,0:T(8,128)(2,1)S(1)} %copy-done, bf16[128,4096]{1,0:T(8,128)(2,1)S(1)} %copy-done.1, f32[16,128]{1,0:T(8,128)S(1)} %fusion.hidden_ref, f32[16,128]{1,0:T(8,128)S(1)} %fusion.1.back_ref, s32[1,128]{1,0:T(1,128)S(1)} %copy-done.8, ...), custom_call_target="tpu_custom_call" | custom-call | flops 1000000 | bytes 4096 | tf_op jit(solution)/shard_map/eval_factors/pallas_call | solution.py:247
  40.3 0.6 collective-permute-start.21
  40.9 3.2 %collective-permute-start.22 = (bf16[1,288,256]{2,1,0:T(8,128)(2,1)S(1)}, bf16[1,288,256]{2,1,0:T(8,128)(2,1)S(1)}, u32[]{:S(2)}, u32[]{:S(2)}) collective-permute-start(bf16[1,288,256]{2,1,0:T(8,128)(2,1)S(1)} %eval_factors.1), channel_id=1, source_target_pairs={{0,8},{1,9},{2,10},{3,11},{4,12},{5,13},{6,14},{7,15},{8,0},{9,1},... | collective-permute-start | bytes 442376 | tf_op jit(solution)/shard_map/ppermute | solution.py:32
  44.1 1.1 %collective-permute-start.19 = (bf16[1,288,256]{2,1,0:T(8,128)(2,1)S(1)}, bf16[1,288,256]{2,1,0:T(8,128)(2,1)S(1)}, u32[]{:S(2)}, u32[]{:S(2)}) collective-permute-start(bf16[1,288,256]{2,1,0:T(8,128)(2,1)S(1)} %eval_factors.1), channel_id=1, source_target_pairs={{0,16},{1,17},{2,18},{3,19},{4,20},{5,21},{6,22},{7,23},{8,24},{9,... | collective-permute-start | bytes 442376 | tf_op jit(solution)/shard_map/ppermute | solution.py:32
  45.2 1.5 %collective-permute-start.20 = (bf16[1,288,256]{2,1,0:T(8,128)(2,1)S(1)}, bf16[1,288,256]{2,1,0:T(8,128)(2,1)S(1)}, u32[]{:S(2)}, u32[]{:S(2)}) collective-permute-start(bf16[1,288,256]{2,1,0:T(8,128)(2,1)S(1)} %eval_factors.1), channel_id=1, source_target_pairs={{0,24},{1,25},{2,26},{3,27},{4,28},{5,29},{6,30},{7,31},{8,16},{9,... | collective-permute-start | bytes 442376 | tf_op jit(solution)/shard_map/ppermute | solution.py:32
  46.6 3.4 %collective-permute-done.22 = bf16[1,288,256]{2,1,0:T(8,128)(2,1)S(1)} collective-permute-done((bf16[1,288,256]{2,1,0:T(8,128)(2,1)S(1)}, bf16[1,288,256]{2,1,0:T(8,128)(2,1)S(1)}, u32[]{:S(2)}, u32[]{:S(2)}) %collective-permute-start.22) | collective-permute-done | bytes 147488 | tf_op jit(solution)/shard_map/ppermute | solution.py:32
  50.0 1.4 %collective-permute-start.23 = (bf16[1,288,256]{2,1,0:T(8,128)(2,1)S(1)}, bf16[1,288,256]{2,1,0:T(8,128)(2,1)S(1)}, u32[]{:S(2)}, u32[]{:S(2)}) collective-permute-start(bf16[1,288,256]{2,1,0:T(8,128)(2,1)S(1)} %collective-permute-done.22), channel_id=1, source_target_pairs={{0,4},{1,5},{2,6},{3,7},{4,0},{5,1},{6,2},{7,3},{8,12},{9,13},{10,... | collective-permute-start | bytes 442376 | tf_op jit(solution)/shard_map/ppermute | solution.py:32
  51.4 0.0 copy-start.5
  51.4 0.0 copy-start.7
  51.4 0.7 collective-permute-start.26
  52.2 3.0 %train_gradient_side.1 = (f32[512,256]{1,0:T(8,128)S(1)}, f32[16,512]{1,0:T(8,128)S(1)}) custom-call(s32[3]{0:T(128)S(1)} %pad_add_fusion.place_ref, bf16[512,4096]{1,0:T(8,128)(2,1)S(1)} %copy-done.3, bf16[16,4096]{1,0:T(8,128)(2,1)S(1)} %copy-done.4, bf16[2,256,256]{2,1,0:T(8,128)(2,1)S(1)} %pad_maximum_fusion.1.rest_0_, ...), custom_call_target="tpu_custom_call" | custom-call | flops 2000000 | bytes 4096 | tf_op jit(solution)/shard_map/train_gradient_side/pallas_call | solution.py:247
  55.1 2.9 %collective-permute-done.19 = bf16[1,288,256]{2,1,0:T(8,128)(2,1)S(1)} collective-permute-done((bf16[1,288,256]{2,1,0:T(8,128)(2,1)S(1)}, bf16[1,288,256]{2,1,0:T(8,128)(2,1)S(1)}, u32[]{:S(2)}, u32[]{:S(2)}) %collective-permute-start.19) | collective-permute-done | bytes 147488 | tf_op jit(solution)/shard_map/ppermute | solution.py:32
  58.1 1.3 %collective-permute-start.24 = (bf16[1,288,256]{2,1,0:T(8,128)(2,1)S(1)}, bf16[1,288,256]{2,1,0:T(8,128)(2,1)S(1)}, u32[]{:S(2)}, u32[]{:S(2)}) collective-permute-start(bf16[1,288,256]{2,1,0:T(8,128)(2,1)S(1)} %collective-permute-done.19), channel_id=1, source_target_pairs={{0,2},{1,3},{2,0},{3,1},{4,6},{5,7},{6,4},{7,5},{8,10},{9,11},{10,... | collective-permute-start | bytes 442376 | tf_op jit(solution)/shard_map/ppermute | solution.py:32
  59.3 0.7 collective-permute-start.25
  60.1 1.4 %collective-permute-start.32 = (bf16[2,288,256]{2,1,0:T(8,128)(2,1)S(1)}, bf16[2,288,256]{2,1,0:T(8,128)(2,1)S(1)}, u32[]{:S(2)}, u32[]{:S(2)}) collective-permute-start(bf16[2,288,256]{2,1,0:T(8,128)(2,1)S(1)} %constant_dynamic-update-slice_fusion.10.rest_4_), channel_id=1, source_target_pairs={{0,2},{1,3},{2,0},{3,1},{4,6},{5,7},{6,4},{7,5},{8,10},{9,11},{10,... | collective-permute-start | bytes 884744 | tf_op jit(solution)/shard_map/ppermute | solution.py:32
  61.5 4.3 %train_input_side.1 = (f32[512,256]{1,0:T(8,128)S(1)}, f32[32,1]{1,0:T(8,128)S(1)}, f32[16,512]{1,0:T(8,128)S(1)}) custom-call(s32[3]{0:T(128)S(1)} %pad_add_fusion.place_ref, bf16[512,4096]{1,0:T(8,128)(2,1)S(1)} %copy-done.2, bf16[16,4096]{1,0:T(8,128)(2,1)S(1)} %bitcast.12, bf16[2,256,256]{2,1,0:T(8,128)(2,1)S(1)} %pad_maximum_fusion.1.rest_0_, ...), custom_call_target="tpu_custom_call" | custom-call | flops 2000000 | bytes 4096 | tf_op jit(solution)/shard_map/train_input_side/pallas_call | solution.py:247
  65.8 0.9 %train_features.1.feats_ref = bf16[2,512,256]{2,1,0:T(8,128)(2,1)S(1)} custom-call(f32[16,512]{1,0:T(8,128)S(1)} %get-tuple-element.80.hidden_ref, f32[512,256]{1,0:T(8,128)S(1)} %get-tuple-element.81.values_ref, f32[512,256]{1,0:T(8,128)S(1)} %get-tuple-element.82.raw_ref, f32[32,1]{1,0:T(8,128)S(1)} %get-tuple-element.83.total_ref, s32[1,512]{1,0:T(1,128)S(1)} %copy-done.7), custom_call_target="tpu_custom_call" | custom-call | flops 1000000 | bytes 4096 | tf_op jit(solution)/shard_map/train_features/pallas_call | solution.py:247
  66.7 0.1 collective-permute-start.31
  66.8 0.5 collective-permute-start.35
  67.4 0.1 collective-permute-start.34
  67.5 0.3 collective-permute-done.32.rest_6_
  67.8 0.2 collective-permute-start.30
  68.0 0.3 collective-permute-start.33
  68.3 0.1 collective-permute-done.31.rest_5_
  68.4 1.3 %collective-permute-start.28 = (bf16[2,288,256]{2,1,0:T(8,128)(2,1)S(1)}, bf16[2,288,256]{2,1,0:T(8,128)(2,1)S(1)}, u32[]{:S(2)}, u32[]{:S(2)}) collective-permute-start(bf16[2,288,256]{2,1,0:T(8,128)(2,1)S(1)} %constant_dynamic-update-slice_fusion.8.rest_10_), channel_id=1, source_target_pairs={{0,2},{1,3},{2,0},{3,1},{4,6},{5,7},{6,4},{7,5},{8,10},{9,11},{10,... | collective-permute-start | bytes 884744 | tf_op jit(solution)/shard_map/ppermute | solution.py:32
  69.6 0.7 collective-permute-start.27
  70.3 4.9 %front_tiles.1.rest_4_ = f32[32,16,32]{2,1,0:T(8,128)S(1)} custom-call(s32[3]{0:T(128)S(1)} %pad_add_fusion.place_ref, bf16[2,512,256]{2,1,0:T(8,128)(2,1)S(1)} %train_features.1.feats_ref, bf16[2,288,256]{2,1,0:T(8,128)(2,1)S(1)} %pad_maximum_fusion.rest_0_, bf16[2,288,256]{2,1,0:T(8,128)(2,1)S(1)} %collective-permute-done.29.rest_1_, ...), custom_call_target="tpu_custom_call" | custom-call | flops 1000000 | bytes 4096 | tf_op jit(solution)/shard_map/front_tiles/pallas_call | solution.py:247
  75.3 2.2 %collective-permute-done.28.rest_2_ = bf16[2,288,256]{2,1,0:T(8,128)(2,1)S(1)} collective-permute-done((bf16[2,288,256]{2,1,0:T(8,128)(2,1)S(1)}, bf16[2,288,256]{2,1,0:T(8,128)(2,1)S(1)}, u32[]{:S(2)}, u32[]{:S(2)}) %collective-permute-start.28) | collective-permute-done | bytes 294944 | tf_op jit(solution)/shard_map/ppermute | solution.py:32
  77.4 0.9 %collective-permute-done.27.rest_0_ = bf16[2,288,256]{2,1,0:T(8,128)(2,1)S(1)} collective-permute-done((bf16[2,288,256]{2,1,0:T(8,128)(2,1)S(1)}, bf16[2,288,256]{2,1,0:T(8,128)(2,1)S(1)}, u32[]{:S(2)}, u32[]{:S(2)}) %collective-permute-start.27) | collective-permute-done | bytes 294944 | tf_op jit(solution)/shard_map/ppermute | solution.py:32
  78.4 0.5 collective-permute-start.37
  78.9 1.1 %collective-permute-done.36.rest_1_ = bf16[2,288,256]{2,1,0:T(8,128)(2,1)S(1)} collective-permute-done((bf16[2,288,256]{2,1,0:T(8,128)(2,1)S(1)}, bf16[2,288,256]{2,1,0:T(8,128)(2,1)S(1)}, u32[]{:S(2)}, u32[]{:S(2)}) %collective-permute-start.36) | collective-permute-done | bytes 294944 | tf_op jit(solution)/shard_map/ppermute | solution.py:32
  79.9 0.4 collective-permute-done.37.rest_3_
  80.4 2.9 %score_tiles.1 = f32[1,16,16,32]{3,2,1,0:T(8,128)} custom-call(s32[3]{0:T(128)S(1)} %pad_add_fusion.place_ref, s32[16,32]{1,0:T(8,128)S(1)} %bitcast.13, s32[32]{0:T(128)S(1)} %copy-done.9, bf16[2,512,256]{2,1,0:T(8,128)(2,1)S(1)} %train_features.1.feats_ref, bf16[2,288,256]{2,1,0:T(8,128)(2,1)S(1)} %collective-permute-done.27.rest_0_, ...), custom_call_target="tpu_custom_call" | custom-call | flops 1000000 | bytes 4096 | tf_op jit(solution)/shard_map/score_tiles/pallas_call | solution.py:247
  (57 shorter events, 0.3 us)
Async XLA Ops:
  0.0 29.4 %copy-start = (bf16[128,4096]{1,0:T(8,128)(2,1)S(1)}, bf16[128,4096]{1,0:T(8,128)(2,1)}, u32[]{:S(2)}) copy-start(bf16[128,4096]{1,0:T(8,128)(2,1)} %x_ref.3) | copy-start | bytes 3145732
  0.0 29.4 %copy-start.1 = (bf16[128,4096]{1,0:T(8,128)(2,1)S(1)}, bf16[128,4096]{1,0:T(8,128)(2,1)}, u32[]{:S(2)}) copy-start(bf16[128,4096]{1,0:T(8,128)(2,1)} %g_ref.3) | copy-start | bytes 3145732
  1.0 10.9 %collective-permute-start = (bf16[1,256,256]{2,1,0:T(8,128)(2,1)S(1)}, bf16[1,256,256]{2,1,0:T(8,128)(2,1)S(1)}, u32[]{:S(2)}, u32[]{:S(2)}) collective-permute-start(bf16[1,256,256]{2,1,0:T(8,128)(2,1)S(1)} %maximum_bitcast_fusion), channel_id=1, source_target_pairs={{0,2},{1,3},{2,0},{3,1},{4,6},{5,7},{6,4},{7,5},{8,10},{9,11},{10,... | collective-permute-start | bytes 393224 | tf_op jit(solution)/shard_map/ppermute | solution.py:32
  4.0 7.9 %collective-permute-start.1 = (bf16[1,256,256]{2,1,0:T(8,128)(2,1)S(1)}, bf16[1,256,256]{2,1,0:T(8,128)(2,1)S(1)}, u32[]{:S(2)}, u32[]{:S(2)}) collective-permute-start(bf16[1,256,256]{2,1,0:T(8,128)(2,1)S(1)} %maximum_bitcast_fusion), channel_id=1, source_target_pairs={{0,8},{1,9},{2,10},{3,11},{4,12},{5,13},{6,14},{7,15},{8,0},{9,1},... | collective-permute-start | bytes 393224 | tf_op jit(solution)/shard_map/ppermute | solution.py:32
  5.6 12.6 %collective-permute-start.2 = (bf16[1,256,256]{2,1,0:T(8,128)(2,1)S(1)}, bf16[1,256,256]{2,1,0:T(8,128)(2,1)S(1)}, u32[]{:S(2)}, u32[]{:S(2)}) collective-permute-start(bf16[1,256,256]{2,1,0:T(8,128)(2,1)S(1)} %maximum_bitcast_fusion), channel_id=1, source_target_pairs={{0,16},{1,17},{2,18},{3,19},{4,20},{5,21},{6,22},{7,23},{8,24},{9,... | collective-permute-start | bytes 393224 | tf_op jit(solution)/shard_map/ppermute | solution.py:32
  8.2 10.1 %collective-permute-start.3 = (bf16[1,256,256]{2,1,0:T(8,128)(2,1)S(1)}, bf16[1,256,256]{2,1,0:T(8,128)(2,1)S(1)}, u32[]{:S(2)}, u32[]{:S(2)}) collective-permute-start(bf16[1,256,256]{2,1,0:T(8,128)(2,1)S(1)} %maximum_bitcast_fusion), channel_id=1, source_target_pairs={{0,24},{1,25},{2,26},{3,27},{4,28},{5,29},{6,30},{7,31},{8,16},{9,... | collective-permute-start | bytes 393224 | tf_op jit(solution)/shard_map/ppermute | solution.py:32
  10.1 28.7 %copy-start.8 = (s32[1,128]{1,0:T(1,128)S(1)}, s32[1,128]{1,0:T(1,128)}, u32[]{:S(2)}) copy-start(s32[1,128]{1,0:T(1,128)} %index_ref.2) | copy-start | bytes 1540
  11.9 6.5 %collective-permute-start.4 = (bf16[1,256,256]{2,1,0:T(8,128)(2,1)S(1)}, bf16[1,256,256]{2,1,0:T(8,128)(2,1)S(1)}, u32[]{:S(2)}, u32[]{:S(2)}) collective-permute-start(bf16[1,256,256]{2,1,0:T(8,128)(2,1)S(1)} %collective-permute-done.1), channel_id=1, source_target_pairs={{0,4},{1,5},{2,6},{3,7},{4,0},{5,1},{6,2},{7,3},{8,12},{9,13},{10,... | collective-permute-start | bytes 393224 | tf_op jit(solution)/shard_map/ppermute | solution.py:32
  13.5 11.1 %collective-permute-start.7 = (bf16[2,256,256]{2,1,0:T(8,128)(2,1)S(1)}, bf16[2,256,256]{2,1,0:T(8,128)(2,1)S(1)}, u32[]{:S(2)}, u32[]{:S(2)}) collective-permute-start(bf16[2,256,256]{2,1,0:T(8,128)(2,1)S(1)} %pad_maximum_fusion.1.rest_0_), channel_id=1, source_target_pairs={{0,4},{1,5},{2,6},{3,7},{4,0},{5,1},{6,2},{7,3},{8,12},{9,13},{10,... | collective-permute-start | bytes 786440 | tf_op jit(solution)/shard_map/ppermute | solution.py:32
  14.1 12.8 %collective-permute-start.10 = (bf16[2,256,256]{2,1,0:T(8,128)(2,1)S(1)}, bf16[2,256,256]{2,1,0:T(8,128)(2,1)S(1)}, u32[]{:S(2)}, u32[]{:S(2)}) collective-permute-start(bf16[2,256,256]{2,1,0:T(8,128)(2,1)S(1)} %pad_maximum_fusion.1.rest_0_), channel_id=1, source_target_pairs={{0,1},{1,0},{2,3},{3,2},{4,5},{5,4},{6,7},{7,6},{8,9},{9,8},{10,11... | collective-permute-start | bytes 786440 | tf_op jit(solution)/shard_map/ppermute | solution.py:32
  18.4 5.0 %collective-permute-start.5 = (bf16[1,256,256]{2,1,0:T(8,128)(2,1)S(1)}, bf16[1,256,256]{2,1,0:T(8,128)(2,1)S(1)}, u32[]{:S(2)}, u32[]{:S(2)}) collective-permute-start(bf16[1,256,256]{2,1,0:T(8,128)(2,1)S(1)} %collective-permute-done.2), channel_id=1, source_target_pairs={{0,2},{1,3},{2,0},{3,1},{4,6},{5,7},{6,4},{7,5},{8,10},{9,11},{10,... | collective-permute-start | bytes 393224 | tf_op jit(solution)/shard_map/ppermute | solution.py:32
  18.8 5.8 %collective-permute-start.6 = (bf16[1,256,256]{2,1,0:T(8,128)(2,1)S(1)}, bf16[1,256,256]{2,1,0:T(8,128)(2,1)S(1)}, u32[]{:S(2)}, u32[]{:S(2)}) collective-permute-start(bf16[1,256,256]{2,1,0:T(8,128)(2,1)S(1)} %collective-permute-done.3), channel_id=1, source_target_pairs={{0,4},{1,5},{2,6},{3,7},{4,0},{5,1},{6,2},{7,3},{8,12},{9,13},{10,... | collective-permute-start | bytes 393224 | tf_op jit(solution)/shard_map/ppermute | solution.py:32
  20.5 6.4 %collective-permute-start.13 = (bf16[2,256,256]{2,1,0:T(8,128)(2,1)S(1)}, bf16[2,256,256]{2,1,0:T(8,128)(2,1)S(1)}, u32[]{:S(2)}, u32[]{:S(2)}) collective-permute-start(bf16[2,256,256]{2,1,0:T(8,128)(2,1)S(1)} %constant_dynamic-update-slice_fusion.4.rest_4_), channel_id=1, source_target_pairs={{0,2},{1,3},{2,0},{3,1},{4,6},{5,7},{6,4},{7,5},{8,10},{9,11},{10,... | collective-permute-start | bytes 786440 | tf_op jit(solution)/shard_map/ppermute | solution.py:32
  23.4 4.0 %collective-permute-start.12 = (bf16[2,256,256]{2,1,0:T(8,128)(2,1)S(1)}, bf16[2,256,256]{2,1,0:T(8,128)(2,1)S(1)}, u32[]{:S(2)}, u32[]{:S(2)}) collective-permute-start(bf16[2,256,256]{2,1,0:T(8,128)(2,1)S(1)} %constant_dynamic-update-slice_fusion.4.rest_4_), channel_id=1, source_target_pairs={{0,1},{1,0},{2,3},{3,2},{4,5},{5,4},{6,7},{7,6},{8,9},{9,8},{10,11... | collective-permute-start | bytes 786440 | tf_op jit(solution)/shard_map/ppermute | solution.py:32
  24.6 4.3 %collective-permute-start.16 = (bf16[2,256,256]{2,1,0:T(8,128)(2,1)S(1)}, bf16[2,256,256]{2,1,0:T(8,128)(2,1)S(1)}, u32[]{:S(2)}, u32[]{:S(2)}) collective-permute-start(bf16[2,256,256]{2,1,0:T(8,128)(2,1)S(1)} %constant_dynamic-update-slice_fusion.2.rest_10_), channel_id=1, source_target_pairs={{0,1},{1,0},{2,3},{3,2},{4,5},{5,4},{6,7},{7,6},{8,9},{9,8},{10,11... | collective-permute-start | bytes 786440 | tf_op jit(solution)/shard_map/ppermute | solution.py:32
  24.7 27.5 %copy-start.3 = (bf16[512,4096]{1,0:T(8,128)(2,1)S(1)}, bf16[512,4096]{1,0:T(8,128)(2,1)}, u32[]{:S(2)}) copy-start(bf16[512,4096]{1,0:T(8,128)(2,1)} %act_ref.2) | copy-start | bytes 12582916
  24.7 27.5 %copy-start.4 = (bf16[16,4096]{1,0:T(8,128)(2,1)S(1)}, bf16[16,4096]{1,0:T(8,128)(2,1)}, u32[]{:S(2)}) copy-start(bf16[16,4096]{1,0:T(8,128)(2,1)} %adapter_ref.1) | copy-start | bytes 393220
  24.7 4.7 %collective-permute-start.15 = (bf16[2,256,256]{2,1,0:T(8,128)(2,1)S(1)}, bf16[2,256,256]{2,1,0:T(8,128)(2,1)S(1)}, u32[]{:S(2)}, u32[]{:S(2)}) collective-permute-start(bf16[2,256,256]{2,1,0:T(8,128)(2,1)S(1)} %constant_dynamic-update-slice_fusion.rest_8_), channel_id=1, source_target_pairs={{0,1},{1,0},{2,3},{3,2},{4,5},{5,4},{6,7},{7,6},{8,9},{9,8},{10,11... | collective-permute-start | bytes 786440 | tf_op jit(solution)/shard_map/ppermute | solution.py:32
  26.9 2.5 %collective-permute-start.11 = (bf16[2,256,256]{2,1,0:T(8,128)(2,1)S(1)}, bf16[2,256,256]{2,1,0:T(8,128)(2,1)S(1)}, u32[]{:S(2)}, u32[]{:S(2)}) collective-permute-start(bf16[2,256,256]{2,1,0:T(8,128)(2,1)S(1)} %collective-permute-done.7.rest_2_), channel_id=1, source_target_pairs={{0,1},{1,0},{2,3},{3,2},{4,5},{5,4},{6,7},{7,6},{8,9},{9,8},{10,11... | collective-permute-start | bytes 786440 | tf_op jit(solution)/shard_map/ppermute | solution.py:32
  26.9 2.5 %collective-permute-start.14 = (bf16[2,256,256]{2,1,0:T(8,128)(2,1)S(1)}, bf16[2,256,256]{2,1,0:T(8,128)(2,1)S(1)}, u32[]{:S(2)}, u32[]{:S(2)}) collective-permute-start(bf16[2,256,256]{2,1,0:T(8,128)(2,1)S(1)} %collective-permute-done.13.rest_6_), channel_id=1, source_target_pairs={{0,1},{1,0},{2,3},{3,2},{4,5},{5,4},{6,7},{7,6},{8,9},{9,8},{10,11... | collective-permute-start | bytes 786440 | tf_op jit(solution)/shard_map/ppermute | solution.py:32
  27.4 8.3 %collective-permute-start.9 = (bf16[2,256,256]{2,1,0:T(8,128)(2,1)S(1)}, bf16[2,256,256]{2,1,0:T(8,128)(2,1)S(1)}, u32[]{:S(2)}, u32[]{:S(2)}) collective-permute-start(bf16[2,256,256]{2,1,0:T(8,128)(2,1)S(1)} %constant_dynamic-update-slice_fusion.2.rest_10_), channel_id=1, source_target_pairs={{0,2},{1,3},{2,0},{3,1},{4,6},{5,7},{6,4},{7,5},{8,10},{9,11},{10,... | collective-permute-start | bytes 786440 | tf_op jit(solution)/shard_map/ppermute | solution.py:32
  28.9 8.0 %collective-permute-start.8 = (bf16[2,256,256]{2,1,0:T(8,128)(2,1)S(1)}, bf16[2,256,256]{2,1,0:T(8,128)(2,1)S(1)}, u32[]{:S(2)}, u32[]{:S(2)}) collective-permute-start(bf16[2,256,256]{2,1,0:T(8,128)(2,1)S(1)} %constant_dynamic-update-slice_fusion.rest_8_), channel_id=1, source_target_pairs={{0,4},{1,5},{2,6},{3,7},{4,0},{5,1},{6,2},{7,3},{8,12},{9,13},{10,... | collective-permute-start | bytes 786440 | tf_op jit(solution)/shard_map/ppermute | solution.py:32
  36.9 1.5 %collective-permute-start.17 = (bf16[2,256,256]{2,1,0:T(8,128)(2,1)S(1)}, bf16[2,256,256]{2,1,0:T(8,128)(2,1)S(1)}, u32[]{:S(2)}, u32[]{:S(2)}) collective-permute-start(bf16[2,256,256]{2,1,0:T(8,128)(2,1)S(1)} %collective-permute-done.8.rest_0_.rest_12_), channel_id=1, source_target_pairs={{0,1},{1,0},{2,3},{3,2},{4,5},{5,4},{6,7},{7,6},{8,9},{9,8},{10,11... | collective-permute-start | bytes 786440 | tf_op jit(solution)/shard_map/ppermute | solution.py:32
  36.9 1.9 %collective-permute-start.18 = (bf16[2,256,256]{2,1,0:T(8,128)(2,1)S(1)}, bf16[2,256,256]{2,1,0:T(8,128)(2,1)S(1)}, u32[]{:S(2)}, u32[]{:S(2)}) collective-permute-start(bf16[2,256,256]{2,1,0:T(8,128)(2,1)S(1)} %collective-permute-done.9.rest_2_.rest_14_), channel_id=1, source_target_pairs={{0,1},{1,0},{2,3},{3,2},{4,5},{5,4},{6,7},{7,6},{8,9},{9,8},{10,11... | collective-permute-start | bytes 786440 | tf_op jit(solution)/shard_map/ppermute | solution.py:32
  40.3 6.3 %collective-permute-start.21 = (bf16[1,288,256]{2,1,0:T(8,128)(2,1)S(1)}, bf16[1,288,256]{2,1,0:T(8,128)(2,1)S(1)}, u32[]{:S(2)}, u32[]{:S(2)}) collective-permute-start(bf16[1,288,256]{2,1,0:T(8,128)(2,1)S(1)} %eval_factors.1), channel_id=1, source_target_pairs={{0,2},{1,3},{2,0},{3,1},{4,6},{5,7},{6,4},{7,5},{8,10},{9,11},{10,... | collective-permute-start | bytes 442376 | tf_op jit(solution)/shard_map/ppermute | solution.py:32
  40.9 9.1 %collective-permute-start.22 = (bf16[1,288,256]{2,1,0:T(8,128)(2,1)S(1)}, bf16[1,288,256]{2,1,0:T(8,128)(2,1)S(1)}, u32[]{:S(2)}, u32[]{:S(2)}) collective-permute-start(bf16[1,288,256]{2,1,0:T(8,128)(2,1)S(1)} %eval_factors.1), channel_id=1, source_target_pairs={{0,8},{1,9},{2,10},{3,11},{4,12},{5,13},{6,14},{7,15},{8,0},{9,1},... | collective-permute-start | bytes 442376 | tf_op jit(solution)/shard_map/ppermute | solution.py:32
  44.1 14.0 %collective-permute-start.19 = (bf16[1,288,256]{2,1,0:T(8,128)(2,1)S(1)}, bf16[1,288,256]{2,1,0:T(8,128)(2,1)S(1)}, u32[]{:S(2)}, u32[]{:S(2)}) collective-permute-start(bf16[1,288,256]{2,1,0:T(8,128)(2,1)S(1)} %eval_factors.1), channel_id=1, source_target_pairs={{0,16},{1,17},{2,18},{3,19},{4,20},{5,21},{6,22},{7,23},{8,24},{9,... | collective-permute-start | bytes 442376 | tf_op jit(solution)/shard_map/ppermute | solution.py:32
  45.2 12.9 %collective-permute-start.20 = (bf16[1,288,256]{2,1,0:T(8,128)(2,1)S(1)}, bf16[1,288,256]{2,1,0:T(8,128)(2,1)S(1)}, u32[]{:S(2)}, u32[]{:S(2)}) collective-permute-start(bf16[1,288,256]{2,1,0:T(8,128)(2,1)S(1)} %eval_factors.1), channel_id=1, source_target_pairs={{0,24},{1,25},{2,26},{3,27},{4,28},{5,29},{6,30},{7,31},{8,16},{9,... | collective-permute-start | bytes 442376 | tf_op jit(solution)/shard_map/ppermute | solution.py:32
  50.0 8.1 %collective-permute-start.23 = (bf16[1,288,256]{2,1,0:T(8,128)(2,1)S(1)}, bf16[1,288,256]{2,1,0:T(8,128)(2,1)S(1)}, u32[]{:S(2)}, u32[]{:S(2)}) collective-permute-start(bf16[1,288,256]{2,1,0:T(8,128)(2,1)S(1)} %collective-permute-done.22), channel_id=1, source_target_pairs={{0,4},{1,5},{2,6},{3,7},{4,0},{5,1},{6,2},{7,3},{8,12},{9,13},{10,... | collective-permute-start | bytes 442376 | tf_op jit(solution)/shard_map/ppermute | solution.py:32
  51.4 10.1 %copy-start.2 = (bf16[512,4096]{1,0:T(8,128)(2,1)S(1)}, bf16[512,4096]{1,0:T(8,128)(2,1)}, u32[]{:S(2)}) copy-start(bf16[512,4096]{1,0:T(8,128)(2,1)} %act_ref.3) | copy-start | bytes 12582916
  51.4 10.1 %copy-start.5 = (bf16[4096,16]{0,1:T(8,128)(2,1)S(1)}, bf16[4096,16]{0,1:T(8,128)(2,1)}, u32[]{:S(2)}) copy-start(bf16[4096,16]{0,1:T(8,128)(2,1)} %param.18) | copy-start | bytes 393220
  51.4 10.1 %copy-start.7 = (s32[1,512]{1,0:T(1,128)S(1)}, s32[1,512]{1,0:T(1,128)}, u32[]{:S(2)}) copy-start(s32[1,512]{1,0:T(1,128)} %index_ref.3) | copy-start | bytes 6148
  51.4 15.4 %collective-permute-start.26 = (bf16[2,288,256]{2,1,0:T(8,128)(2,1)S(1)}, bf16[2,288,256]{2,1,0:T(8,128)(2,1)S(1)}, u32[]{:S(2)}, u32[]{:S(2)}) collective-permute-start(bf16[2,288,256]{2,1,0:T(8,128)(2,1)S(1)} %pad_maximum_fusion.rest_0_), channel_id=1, source_target_pairs={{0,4},{1,5},{2,6},{3,7},{4,0},{5,1},{6,2},{7,3},{8,12},{9,13},{10,... | collective-permute-start | bytes 884744 | tf_op jit(solution)/shard_map/ppermute | solution.py:32
  52.2 15.9 %collective-permute-start.29 = (bf16[2,288,256]{2,1,0:T(8,128)(2,1)S(1)}, bf16[2,288,256]{2,1,0:T(8,128)(2,1)S(1)}, u32[]{:S(2)}, u32[]{:S(2)}) collective-permute-start(bf16[2,288,256]{2,1,0:T(8,128)(2,1)S(1)} %pad_maximum_fusion.rest_0_), channel_id=1, source_target_pairs={{0,1},{1,0},{2,3},{3,2},{4,5},{5,4},{6,7},{7,6},{8,9},{9,8},{10,11... | collective-permute-start | bytes 884744 | tf_op jit(solution)/shard_map/ppermute | solution.py:32
  58.1 8.6 %collective-permute-start.24 = (bf16[1,288,256]{2,1,0:T(8,128)(2,1)S(1)}, bf16[1,288,256]{2,1,0:T(8,128)(2,1)S(1)}, u32[]{:S(2)}, u32[]{:S(2)}) collective-permute-start(bf16[1,288,256]{2,1,0:T(8,128)(2,1)S(1)} %collective-permute-done.19), channel_id=1, source_target_pairs={{0,2},{1,3},{2,0},{3,1},{4,6},{5,7},{6,4},{7,5},{8,10},{9,11},{10,... | collective-permute-start | bytes 442376 | tf_op jit(solution)/shard_map/ppermute | solution.py:32
  59.3 7.5 %collective-permute-start.25 = (bf16[1,288,256]{2,1,0:T(8,128)(2,1)S(1)}, bf16[1,288,256]{2,1,0:T(8,128)(2,1)S(1)}, u32[]{:S(2)}, u32[]{:S(2)}) collective-permute-start(bf16[1,288,256]{2,1,0:T(8,128)(2,1)S(1)} %collective-permute-done.20), channel_id=1, source_target_pairs={{0,4},{1,5},{2,6},{3,7},{4,0},{5,1},{6,2},{7,3},{8,12},{9,13},{10,... | collective-permute-start | bytes 442376 | tf_op jit(solution)/shard_map/ppermute | solution.py:32
  60.1 7.7 %collective-permute-start.32 = (bf16[2,288,256]{2,1,0:T(8,128)(2,1)S(1)}, bf16[2,288,256]{2,1,0:T(8,128)(2,1)S(1)}, u32[]{:S(2)}, u32[]{:S(2)}) collective-permute-start(bf16[2,288,256]{2,1,0:T(8,128)(2,1)S(1)} %constant_dynamic-update-slice_fusion.10.rest_4_), channel_id=1, source_target_pairs={{0,2},{1,3},{2,0},{3,1},{4,6},{5,7},{6,4},{7,5},{8,10},{9,11},{10,... | collective-permute-start | bytes 884744 | tf_op jit(solution)/shard_map/ppermute | solution.py:32
  65.8 14.6 %copy-start.6 = (s32[32,16]{0,1:T(8,128)S(1)}, s32[32,16]{0,1:T(8,128)}, u32[]{:S(2)}) copy-start(s32[32,16]{0,1:T(8,128)} %param.22) | copy-start | bytes 6148
  65.8 14.5 %copy-start.9 = (s32[32]{0:T(128)S(1)}, s32[32]{0:T(128)}, u32[]{:S(2)}) copy-start(s32[32]{0:T(128)} %live_ref.1) | copy-start | bytes 388
  66.7 1.6 %collective-permute-start.31 = (bf16[2,288,256]{2,1,0:T(8,128)(2,1)S(1)}, bf16[2,288,256]{2,1,0:T(8,128)(2,1)S(1)}, u32[]{:S(2)}, u32[]{:S(2)}) collective-permute-start(bf16[2,288,256]{2,1,0:T(8,128)(2,1)S(1)} %constant_dynamic-update-slice_fusion.10.rest_4_), channel_id=1, source_target_pairs={{0,1},{1,0},{2,3},{3,2},{4,5},{5,4},{6,7},{7,6},{8,9},{9,8},{10,11... | collective-permute-start | bytes 884744 | tf_op jit(solution)/shard_map/ppermute | solution.py:32
  66.8 2.8 %collective-permute-start.35 = (bf16[2,288,256]{2,1,0:T(8,128)(2,1)S(1)}, bf16[2,288,256]{2,1,0:T(8,128)(2,1)S(1)}, u32[]{:S(2)}, u32[]{:S(2)}) collective-permute-start(bf16[2,288,256]{2,1,0:T(8,128)(2,1)S(1)} %constant_dynamic-update-slice_fusion.8.rest_10_), channel_id=1, source_target_pairs={{0,1},{1,0},{2,3},{3,2},{4,5},{5,4},{6,7},{7,6},{8,9},{9,8},{10,11... | collective-permute-start | bytes 884744 | tf_op jit(solution)/shard_map/ppermute | solution.py:32
  67.4 2.9 %collective-permute-start.34 = (bf16[2,288,256]{2,1,0:T(8,128)(2,1)S(1)}, bf16[2,288,256]{2,1,0:T(8,128)(2,1)S(1)}, u32[]{:S(2)}, u32[]{:S(2)}) collective-permute-start(bf16[2,288,256]{2,1,0:T(8,128)(2,1)S(1)} %constant_dynamic-update-slice_fusion.6.rest_8_), channel_id=1, source_target_pairs={{0,1},{1,0},{2,3},{3,2},{4,5},{5,4},{6,7},{7,6},{8,9},{9,8},{10,11... | collective-permute-start | bytes 884744 | tf_op jit(solution)/shard_map/ppermute | solution.py:32
  67.8 2.5 %collective-permute-start.30 = (bf16[2,288,256]{2,1,0:T(8,128)(2,1)S(1)}, bf16[2,288,256]{2,1,0:T(8,128)(2,1)S(1)}, u32[]{:S(2)}, u32[]{:S(2)}) collective-permute-start(bf16[2,288,256]{2,1,0:T(8,128)(2,1)S(1)} %collective-permute-done.26.rest_2_), channel_id=1, source_target_pairs={{0,1},{1,0},{2,3},{3,2},{4,5},{5,4},{6,7},{7,6},{8,9},{9,8},{10,11... | collective-permute-start | bytes 884744 | tf_op jit(solution)/shard_map/ppermute | solution.py:32
  68.0 2.3 %collective-permute-start.33 = (bf16[2,288,256]{2,1,0:T(8,128)(2,1)S(1)}, bf16[2,288,256]{2,1,0:T(8,128)(2,1)S(1)}, u32[]{:S(2)}, u32[]{:S(2)}) collective-permute-start(bf16[2,288,256]{2,1,0:T(8,128)(2,1)S(1)} %collective-permute-done.32.rest_6_), channel_id=1, source_target_pairs={{0,1},{1,0},{2,3},{3,2},{4,5},{5,4},{6,7},{7,6},{8,9},{9,8},{10,11... | collective-permute-start | bytes 884744 | tf_op jit(solution)/shard_map/ppermute | solution.py:32
  68.4 9.1 %collective-permute-start.28 = (bf16[2,288,256]{2,1,0:T(8,128)(2,1)S(1)}, bf16[2,288,256]{2,1,0:T(8,128)(2,1)S(1)}, u32[]{:S(2)}, u32[]{:S(2)}) collective-permute-start(bf16[2,288,256]{2,1,0:T(8,128)(2,1)S(1)} %constant_dynamic-update-slice_fusion.8.rest_10_), channel_id=1, source_target_pairs={{0,2},{1,3},{2,0},{3,1},{4,6},{5,7},{6,4},{7,5},{8,10},{9,11},{10,... | collective-permute-start | bytes 884744 | tf_op jit(solution)/shard_map/ppermute | solution.py:32
  69.6 8.7 %collective-permute-start.27 = (bf16[2,288,256]{2,1,0:T(8,128)(2,1)S(1)}, bf16[2,288,256]{2,1,0:T(8,128)(2,1)S(1)}, u32[]{:S(2)}, u32[]{:S(2)}) collective-permute-start(bf16[2,288,256]{2,1,0:T(8,128)(2,1)S(1)} %constant_dynamic-update-slice_fusion.6.rest_8_), channel_id=1, source_target_pairs={{0,4},{1,5},{2,6},{3,7},{4,0},{5,1},{6,2},{7,3},{8,12},{9,13},{10,... | collective-permute-start | bytes 884744 | tf_op jit(solution)/shard_map/ppermute | solution.py:32
  78.4 1.6 %collective-permute-start.36 = (bf16[2,288,256]{2,1,0:T(8,128)(2,1)S(1)}, bf16[2,288,256]{2,1,0:T(8,128)(2,1)S(1)}, u32[]{:S(2)}, u32[]{:S(2)}) collective-permute-start(bf16[2,288,256]{2,1,0:T(8,128)(2,1)S(1)} %collective-permute-done.27.rest_0_), channel_id=1, source_target_pairs={{0,1},{1,0},{2,3},{3,2},{4,5},{5,4},{6,7},{7,6},{8,9},{9,8},{10,11... | collective-permute-start | bytes 884744 | tf_op jit(solution)/shard_map/ppermute | solution.py:32
  78.4 2.0 %collective-permute-start.37 = (bf16[2,288,256]{2,1,0:T(8,128)(2,1)S(1)}, bf16[2,288,256]{2,1,0:T(8,128)(2,1)S(1)}, u32[]{:S(2)}, u32[]{:S(2)}) collective-permute-start(bf16[2,288,256]{2,1,0:T(8,128)(2,1)S(1)} %collective-permute-done.28.rest_2_), channel_id=1, source_target_pairs={{0,1},{1,0},{2,3},{3,2},{4,5},{5,4},{6,7},{7,6},{8,9},{9,8},{10,11... | collective-permute-start | bytes 884744 | tf_op jit(solution)/shard_map/ppermute | solution.py:32

commit v5 on v4

--- a/solution.py
+++ b/solution.py
@@ -177,27 +177,20 @@
     width = held.shape[0] * part
     factor = lax.dot_general(adapter_ref[...], act_ref[...], NT, preferred_element_type=F32)
     values = jnp.dot(act_ref[...], held[...].reshape(width, PW), preferred_element_type=F32)
-    if side == 0:
-        values_ref, factor_ref = rest[:2]
-        values_ref[...] = values
-        factor_ref[...] = factor
-        return
-    back_ref, index_ref, raw_ref, total_ref, factor_ref = rest[:5]
+    values_ref, factor_ref = rest[:2]
+    values_ref[...] = values
+    factor_ref[...] = factor
+
+
+def feats_kernel(values_ref, back_ref, inputs_ref, hidden_ref, index_ref, feats_ref):
     picked = one_hot(index_ref[...], TRAIN_EXAMPLES)
-    raw = dot3(weighted(back_ref[...], picked), values)
-    raw_ref[...] = raw
-    total_ref[...] = squares(raw, TRAIN_EXAMPLES)
-    factor_ref[...] = factor
-
-
-def feats_kernel(hidden_ref, values_ref, raw_ref, total_ref, index_ref, feats_ref):
-    picked = one_hot(index_ref[...], TRAIN_EXAMPLES)
-    raw = dot3(weighted(hidden_ref[...], picked), values_ref[...])
-    total = total_ref[...] + squares(raw, TRAIN_EXAMPLES)
+    raw_a = dot3(weighted(hidden_ref[...], picked), values_ref[...])
+    raw_b = dot3(weighted(back_ref[...], picked), inputs_ref[...])
+    total = squares(raw_a, TRAIN_EXAMPLES) + squares(raw_b, TRAIN_EXAMPLES)
     scale = lax.rsqrt(total * (1.0 / K) + EPS)[None]
     shape = (RANK, TRAIN_EXAMPLES, PW)
-    feats_ref[0] = (raw.reshape(shape) * scale).reshape(RANK * TRAIN_EXAMPLES, PW).astype(BF16)
-    feats_ref[1] = (raw_ref[...].reshape(shape) * scale).reshape(RANK * TRAIN_EXAMPLES, PW).astype(BF16)
+    feats_ref[0] = (raw_a.reshape(shape) * scale).reshape(RANK * TRAIN_EXAMPLES, PW).astype(BF16)
+    feats_ref[1] = (raw_b.reshape(shape) * scale).reshape(RANK * TRAIN_EXAMPLES, PW).astype(BF16)
 
 
 def make_tiles(steps, size, place_ref, feats_ref, refs, tiles_ref):
@@ -229,15 +222,16 @@
     make_tiles(steps, size, place_ref, feats_ref, rest[: len(steps)], rest[len(steps)])
 
 
-def score_kernel(steps, front, size, place_ref, pairing_ref, live_ref, feats_ref, *rest):
+def score_kernel(steps, earlier, size, place_ref, pairing_ref, live_ref, feats_ref, *rest):
     refs, rest = rest[: len(steps)], rest[len(steps) :]
     out_ref, tiles = rest[-2:]
     hi, lo, mine = place_ref[0], place_ref[1], place_ref[2]
     make_tiles(steps, size, place_ref, feats_ref, refs, tiles)
-    for chunk, lows in front:
-        for low in lows:
-            device = (hi ^ chunk) * size + (lo ^ low)
-            tiles[device] = rest[0][device]
+    for ref, known in zip(rest, earlier):
+        for chunk, lows in known:
+            for low in lows:
+                device = (hi ^ chunk) * size + (lo ^ low)
+                tiles[device] = ref[device]
     for slot in range(SLOTS):
         factor = jnp.where(slot < live_ref[mine], 1.0 / K**0.5, 0.0)
         out_ref[0, slot] = tiles[pairing_ref[slot, mine]] * factor
@@ -319,39 +313,20 @@
     values_shape = jax.ShapeDtypeStruct((train_layer_input.shape[0], PW), F32)
     factor_shape = jax.ShapeDtypeStruct((RANK, train_layer_input.shape[0]), F32)
 
+    def train_side(side, place, acts, adapter):
+        name = ("train_gradient_side", "train_input_side")[side]
+        kernel = functools.partial(train_kernel, every, size, side)
+        shapes = [values_shape, factor_shape]
+        return call(kernel, shapes, held, 2 * 10**9, name, [place], acts, adapter, *everything)
+
     def gradient_side(early):
-        return call(
-            functools.partial(train_kernel, every, size, 0),
-            [values_shape, factor_shape],
-            held,
-            2 * 10**9,
-            "train_gradient_side",
-            [early[0]],
-            train_output_gradient,
-            adapter_up,
-            *everything,
-        )
-
-    def input_side(gradient_side):
-        values, back = gradient_side
-        raw, total, hidden = call(
-            functools.partial(train_kernel, every, size, 1),
-            [jax.ShapeDtypeStruct((rows, PW), F32), jax.ShapeDtypeStruct((TRAIN_EXAMPLES, 1), F32), factor_shape],
-            held,
-            2 * 10**9,
-            "train_input_side",
-            [place],
-            train_layer_input,
-            adapter_down.T,
-            *everything,
-            back,
-            train_example_index,
-        )
-        return hidden, values, raw, total
-
-    def features(gradient_side):
+        return early[0], *train_side(0, early[0], train_output_gradient, adapter_up)
+
+    def input_side(middle):
+        return *middle[1:], *train_side(1, middle[0], train_layer_input, adapter_down.T)
+
+    def features(sides):
         shape = jax.ShapeDtypeStruct((2, rows, PW), BF16)
-        sides = input_side(gradient_side)
         return call(feats_kernel, shape, [], 10**9, "train_features", [], *sides, train_example_index)
 
     def tile(front, feats):
@@ -359,10 +334,21 @@
         kernel = functools.partial(tile_kernel, steps, size)
         return call(kernel, jax.ShapeDtypeStruct(tiles_shape, F32), [], 10**9, "front_tiles", [place], feats, *arrays)
 
-    tiles, front, back, _, _, feats = gather_blocks(pack, n, (place,), gradient_side, features, tile)
+    def late(front, sides):
+        feats = features(sides)
+        return tile(front, feats), feats
+
+    done, front, back, _, _, sides = gather_blocks(pack, n, (place,), gradient_side, input_side, late)
+    extra, earlier = [], []
+    if done is None:
+        feats = features(sides)
+    else:
+        tiles, feats = done
+        own, back = back[0::2], back[1::2]
+        extra, earlier = [tiles, tile(own, feats)], [plan(front)[0], plan(own)[0]]
     steps, arrays = plan(back)
     scores = call(
-        functools.partial(score_kernel, steps, plan(front)[0], size),
+        functools.partial(score_kernel, steps, earlier, size),
         jax.ShapeDtypeStruct((1, SLOTS, EVAL_ROLLOUTS, TRAIN_EXAMPLES), F32),
         [pltpu.VMEM(tiles_shape, F32)],
         10**9,
@@ -370,7 +356,7 @@
         [place, paired_eval_index.T, live_slot_count],
         feats,
         *arrays,
-        *([] if tiles is None else [tiles]),
+        *extra,
     )
     return jnp.swapaxes(scores, 2, 3)
 

time: 84.4 us -> 83.7 us (level)
    pallas_call x7 -> x8, Pallas kernels: 19 us -> 18.7 us  [call(): pl.pallas_call(kernel, out_shape=out_shape, in_specs=[SMEM] * len(scalars...]
  transfers between devices with their start and end apart: 38 -> 38, of which waited for: 17 -> 16; matrix products, arithmetic and copies ran while one was open for 4% -> 4% of each run, Pallas kernels for 18% -> 18%
where the time goes in v5:
time: 83.7 us; the launch traced here: 82.5 us
  starting transfers between devices  32.4 us (39%)
  waiting for transfers between devices  26.4 us (32%)
  Pallas kernels  18.7 us (22%)
  matrix products  3.38 us (4%)
  other arithmetic  1.17 us (1%)
    ppermute x38, starting transfers between devices, permute(): return lax.ppermute(held, 'train', [(i, i ^ mask) for i in range(n)])  32.4 us
    ppermute x38, waiting for transfers between devices, permute(): return lax.ppermute(held, 'train', [(i, i ^ mask) for i in range(n)])  26.4 us
    pallas_call x8, Pallas kernels, call(): pl.pallas_call(kernel, out_shape=out_shape, in_specs=[SMEM] * len(scalars...  18.7 us
    dot_general x1, matrix products, up(): return lax.dot_general(adapter_up, g, NT, preferred_element_type=F32)  1.7 us
  transfers between devices with their start and end apart: 38, of which 16 were waited for; matrix products, arithmetic and copies ran while one was open for 4% of the time, Pallas kernels for 18%

profile of v5, /device:TPU:0, one launch (start us, length us, event | category | flops | bytes accessed | tf_op | source)
XLA Modules:
  0.0 82.5 jit_solution(17505769914188427915)
XLA Ops:
  0.0 1.0 %maximum_bitcast_fusion = bf16[1,256,256]{2,1,0:T(8,128)(2,1)S(1)} fusion(bf16[128,256]{1,0:T(8,128)(2,1)} %param.21, bf16[128,256]{1,0:T(8,128)(2,1)} %param.20), kind=kLoop, calls=%fused_computation.2 | loop fusion | flops 262144 | bytes 262144 | tf_op jit(solution)/shard_map/broadcast_in_dim | solution.py:291
  1.0 3.0 %collective-permute-start = (bf16[1,256,256]{2,1,0:T(8,128)(2,1)S(1)}, bf16[1,256,256]{2,1,0:T(8,128)(2,1)S(1)}, u32[]{:S(2)}, u32[]{:S(2)}) collective-permute-start(bf16[1,256,256]{2,1,0:T(8,128)(2,1)S(1)} %maximum_bitcast_fusion), channel_id=1, source_target_pairs={{0,2},{1,3},{2,0},{3,1},{4,6},{5,7},{6,4},{7,5},{8,10},{9,11},{10,... | collective-permute-start | bytes 393224 | tf_op jit(solution)/shard_map/ppermute | solution.py:32
  4.0 1.6 %collective-permute-start.1 = (bf16[1,256,256]{2,1,0:T(8,128)(2,1)S(1)}, bf16[1,256,256]{2,1,0:T(8,128)(2,1)S(1)}, u32[]{:S(2)}, u32[]{:S(2)}) collective-permute-start(bf16[1,256,256]{2,1,0:T(8,128)(2,1)S(1)} %maximum_bitcast_fusion), channel_id=1, source_target_pairs={{0,8},{1,9},{2,10},{3,11},{4,12},{5,13},{6,14},{7,15},{8,0},{9,1},... | collective-permute-start | bytes 393224 | tf_op jit(solution)/shard_map/ppermute | solution.py:32
  5.6 2.6 %collective-permute-start.2 = (bf16[1,256,256]{2,1,0:T(8,128)(2,1)S(1)}, bf16[1,256,256]{2,1,0:T(8,128)(2,1)S(1)}, u32[]{:S(2)}, u32[]{:S(2)}) collective-permute-start(bf16[1,256,256]{2,1,0:T(8,128)(2,1)S(1)} %maximum_bitcast_fusion), channel_id=1, source_target_pairs={{0,16},{1,17},{2,18},{3,19},{4,20},{5,21},{6,22},{7,23},{8,24},{9,... | collective-permute-start | bytes 393224 | tf_op jit(solution)/shard_map/ppermute | solution.py:32
  8.2 0.2 collective-permute-start.3
  8.4 1.7 %fusion.hidden_ref = f32[16,128]{1,0:T(8,128)S(1)} fusion(bf16[4096,16]{0,1:T(8,128)(2,1)} %param.18, bf16[128,4096]{1,0:T(8,128)(2,1)} %x_ref.3), kind=kOutput, calls=%fused_computation.16 | convolution fusion | flops 16777216 | bytes 1187840 | tf_op jit(solution)/shard_map/dot_general | solution.py:276
  10.1 1.7 %fusion.1.back_ref = f32[16,128]{1,0:T(8,128)S(1)} fusion(bf16[16,4096]{1,0:T(8,128)(2,1)} %adapter_ref.1, bf16[128,4096]{1,0:T(8,128)(2,1)} %g_ref.3), kind=kOutput, calls=%fused_computation.17 | convolution fusion | flops 16777216 | bytes 1187840 | tf_op jit(solution)/shard_map/dot_general | solution.py:279
  11.8 0.1 pad_add_fusion.place_ref
  11.9 1.6 %collective-permute-start.4 = (bf16[1,256,256]{2,1,0:T(8,128)(2,1)S(1)}, bf16[1,256,256]{2,1,0:T(8,128)(2,1)S(1)}, u32[]{:S(2)}, u32[]{:S(2)}) collective-permute-start(bf16[1,256,256]{2,1,0:T(8,128)(2,1)S(1)} %collective-permute-done.1), channel_id=1, source_target_pairs={{0,4},{1,5},{2,6},{3,7},{4,0},{5,1},{6,2},{7,3},{8,12},{9,13},{10,... | collective-permute-start | bytes 393224 | tf_op jit(solution)/shard_map/ppermute | solution.py:32
  13.5 0.6 collective-permute-start.7
  14.1 0.1 collective-permute-start.10
  14.2 4.1 %collective-permute-done.2 = bf16[1,256,256]{2,1,0:T(8,128)(2,1)S(1)} collective-permute-done((bf16[1,256,256]{2,1,0:T(8,128)(2,1)S(1)}, bf16[1,256,256]{2,1,0:T(8,128)(2,1)S(1)}, u32[]{:S(2)}, u32[]{:S(2)}) %collective-permute-start.2) | collective-permute-done | bytes 131104 | tf_op jit(solution)/shard_map/ppermute | solution.py:32
  18.3 0.1 collective-permute-done.4
  18.4 0.4 collective-permute-start.5
  18.8 1.6 %collective-permute-start.6 = (bf16[1,256,256]{2,1,0:T(8,128)(2,1)S(1)}, bf16[1,256,256]{2,1,0:T(8,128)(2,1)S(1)}, u32[]{:S(2)}, u32[]{:S(2)}) collective-permute-start(bf16[1,256,256]{2,1,0:T(8,128)(2,1)S(1)} %collective-permute-done.3), channel_id=1, source_target_pairs={{0,4},{1,5},{2,6},{3,7},{4,0},{5,1},{6,2},{7,3},{8,12},{9,13},{10,... | collective-permute-start | bytes 393224 | tf_op jit(solution)/shard_map/ppermute | solution.py:32
  20.5 1.6 %collective-permute-start.13 = (bf16[2,256,256]{2,1,0:T(8,128)(2,1)S(1)}, bf16[2,256,256]{2,1,0:T(8,128)(2,1)S(1)}, u32[]{:S(2)}, u32[]{:S(2)}) collective-permute-start(bf16[2,256,256]{2,1,0:T(8,128)(2,1)S(1)} %constant_dynamic-update-slice_fusion.4.rest_4_), channel_id=1, source_target_pairs={{0,2},{1,3},{2,0},{3,1},{4,6},{5,7},{6,4},{7,5},{8,10},{9,11},{10,... | collective-permute-start | bytes 786440 | tf_op jit(solution)/shard_map/ppermute | solution.py:32
  22.0 1.4 %collective-permute-done.5 = bf16[1,256,256]{2,1,0:T(8,128)(2,1)S(1)} collective-permute-done((bf16[1,256,256]{2,1,0:T(8,128)(2,1)S(1)}, bf16[1,256,256]{2,1,0:T(8,128)(2,1)S(1)}, u32[]{:S(2)}, u32[]{:S(2)}) %collective-permute-start.5) | collective-permute-done | bytes 131104 | tf_op jit(solution)/shard_map/ppermute | solution.py:32
  23.4 1.2 %collective-permute-done.6 = bf16[1,256,256]{2,1,0:T(8,128)(2,1)S(1)} collective-permute-done((bf16[1,256,256]{2,1,0:T(8,128)(2,1)S(1)}, bf16[1,256,256]{2,1,0:T(8,128)(2,1)S(1)}, u32[]{:S(2)}, u32[]{:S(2)}) %collective-permute-start.6) | collective-permute-done | bytes 131104 | tf_op jit(solution)/shard_map/ppermute | solution.py:32
  24.6 0.1 collective-permute-start.16
  24.7 0.0 copy-start.2
  24.7 0.0 copy-start.4
  24.7 0.6 collective-permute-start.15
  25.3 1.6 %collective-permute-done.13.rest_6_ = bf16[2,256,256]{2,1,0:T(8,128)(2,1)S(1)} collective-permute-done((bf16[2,256,256]{2,1,0:T(8,128)(2,1)S(1)}, bf16[2,256,256]{2,1,0:T(8,128)(2,1)S(1)}, u32[]{:S(2)}, u32[]{:S(2)}) %collective-permute-start.13) | collective-permute-done | bytes 262176 | tf_op jit(solution)/shard_map/ppermute | solution.py:32
  26.9 0.5 collective-permute-start.14
  27.4 1.5 %collective-permute-start.9 = (bf16[2,256,256]{2,1,0:T(8,128)(2,1)S(1)}, bf16[2,256,256]{2,1,0:T(8,128)(2,1)S(1)}, u32[]{:S(2)}, u32[]{:S(2)}) collective-permute-start(bf16[2,256,256]{2,1,0:T(8,128)(2,1)S(1)} %constant_dynamic-update-slice_fusion.2.rest_10_), channel_id=1, source_target_pairs={{0,2},{1,3},{2,0},{3,1},{4,6},{5,7},{6,4},{7,5},{8,10},{9,11},{10,... | collective-permute-start | bytes 786440 | tf_op jit(solution)/shard_map/ppermute | solution.py:32
  28.9 0.5 collective-permute-start.8
  29.4 1.7 %eval_begin.1.rest_4_ = f32[2,128,256]{2,1,0:T(8,128)S(1)} custom-call(s32[3]{0:T(128)S(1)} %pad_add_fusion.place_ref, bf16[128,4096]{1,0:T(8,128)(2,1)S(1)} %copy-done, bf16[128,4096]{1,0:T(8,128)(2,1)S(1)} %copy-done.1, bf16[2,256,256]{2,1,0:T(8,128)(2,1)S(1)} %pad_maximum_fusion.1.rest_0_, bf16[2,256,256]{2,1,0:T(8,128)(2,1)S(1)} %collective-permute-done.10.rest_1_, ...), custom_call_target="tpu_custom_call" | custom-call | flops 800000 | bytes 4096 | tf_op jit(solution)/shard_map/eval_begin/pallas_call | solution.py:241
  31.1 4.6 %collective-permute-done.9.rest_2_.rest_14_ = bf16[2,256,256]{2,1,0:T(8,128)(2,1)S(1)} collective-permute-done((bf16[2,256,256]{2,1,0:T(8,128)(2,1)S(1)}, bf16[2,256,256]{2,1,0:T(8,128)(2,1)S(1)}, u32[]{:S(2)}, u32[]{:S(2)}) %collective-permute-start.9) | collective-permute-done | bytes 262176 | tf_op jit(solution)/shard_map/ppermute | solution.py:32
  35.7 1.2 %collective-permute-done.8.rest_0_.rest_12_ = bf16[2,256,256]{2,1,0:T(8,128)(2,1)S(1)} collective-permute-done((bf16[2,256,256]{2,1,0:T(8,128)(2,1)S(1)}, bf16[2,256,256]{2,1,0:T(8,128)(2,1)S(1)}, u32[]{:S(2)}, u32[]{:S(2)}) %collective-permute-start.8) | collective-permute-done | bytes 262176 | tf_op jit(solution)/shard_map/ppermute | solution.py:32
  36.9 0.5 collective-permute-start.18
  37.4 1.0 %collective-permute-done.17.rest_1_.rest_13_ = bf16[2,256,256]{2,1,0:T(8,128)(2,1)S(1)} collective-permute-done((bf16[2,256,256]{2,1,0:T(8,128)(2,1)S(1)}, bf16[2,256,256]{2,1,0:T(8,128)(2,1)S(1)}, u32[]{:S(2)}, u32[]{:S(2)}) %collective-permute-start.17) | collective-permute-done | bytes 262176 | tf_op jit(solution)/shard_map/ppermute | solution.py:32
  38.4 0.4 collective-permute-done.18.rest_3_.rest_15_
  38.8 1.4 %eval_factors.1 = bf16[1,288,256]{2,1,0:T(8,128)(2,1)S(1)} custom-call(s32[3]{0:T(128)S(1)} %pad_add_fusion.place_ref, bf16[128,4096]{1,0:T(8,128)(2,1)S(1)} %copy-done, bf16[128,4096]{1,0:T(8,128)(2,1)S(1)} %copy-done.1, f32[16,128]{1,0:T(8,128)S(1)} %fusion.hidden_ref, f32[16,128]{1,0:T(8,128)S(1)} %fusion.1.back_ref, s32[1,128]{1,0:T(1,128)S(1)} %copy-done.8, ...), custom_call_target="tpu_custom_call" | custom-call | flops 1000000 | bytes 4096 | tf_op jit(solution)/shard_map/eval_factors/pallas_call | solution.py:241
  40.3 0.6 collective-permute-start.21
  40.9 3.2 %collective-permute-start.22 = (bf16[1,288,256]{2,1,0:T(8,128)(2,1)S(1)}, bf16[1,288,256]{2,1,0:T(8,128)(2,1)S(1)}, u32[]{:S(2)}, u32[]{:S(2)}) collective-permute-start(bf16[1,288,256]{2,1,0:T(8,128)(2,1)S(1)} %eval_factors.1), channel_id=1, source_target_pairs={{0,8},{1,9},{2,10},{3,11},{4,12},{5,13},{6,14},{7,15},{8,0},{9,1},... | collective-permute-start | bytes 442376 | tf_op jit(solution)/shard_map/ppermute | solution.py:32
  44.1 1.1 %collective-permute-start.19 = (bf16[1,288,256]{2,1,0:T(8,128)(2,1)S(1)}, bf16[1,288,256]{2,1,0:T(8,128)(2,1)S(1)}, u32[]{:S(2)}, u32[]{:S(2)}) collective-permute-start(bf16[1,288,256]{2,1,0:T(8,128)(2,1)S(1)} %eval_factors.1), channel_id=1, source_target_pairs={{0,16},{1,17},{2,18},{3,19},{4,20},{5,21},{6,22},{7,23},{8,24},{9,... | collective-permute-start | bytes 442376 | tf_op jit(solution)/shard_map/ppermute | solution.py:32
  45.2 1.5 %collective-permute-start.20 = (bf16[1,288,256]{2,1,0:T(8,128)(2,1)S(1)}, bf16[1,288,256]{2,1,0:T(8,128)(2,1)S(1)}, u32[]{:S(2)}, u32[]{:S(2)}) collective-permute-start(bf16[1,288,256]{2,1,0:T(8,128)(2,1)S(1)} %eval_factors.1), channel_id=1, source_target_pairs={{0,24},{1,25},{2,26},{3,27},{4,28},{5,29},{6,30},{7,31},{8,16},{9,... | collective-permute-start | bytes 442376 | tf_op jit(solution)/shard_map/ppermute | solution.py:32
  46.6 3.4 %collective-permute-done.22 = bf16[1,288,256]{2,1,0:T(8,128)(2,1)S(1)} collective-permute-done((bf16[1,288,256]{2,1,0:T(8,128)(2,1)S(1)}, bf16[1,288,256]{2,1,0:T(8,128)(2,1)S(1)}, u32[]{:S(2)}, u32[]{:S(2)}) %collective-permute-start.22) | collective-permute-done | bytes 147488 | tf_op jit(solution)/shard_map/ppermute | solution.py:32
  50.0 1.4 %collective-permute-start.23 = (bf16[1,288,256]{2,1,0:T(8,128)(2,1)S(1)}, bf16[1,288,256]{2,1,0:T(8,128)(2,1)S(1)}, u32[]{:S(2)}, u32[]{:S(2)}) collective-permute-start(bf16[1,288,256]{2,1,0:T(8,128)(2,1)S(1)} %collective-permute-done.22), channel_id=1, source_target_pairs={{0,4},{1,5},{2,6},{3,7},{4,0},{5,1},{6,2},{7,3},{8,12},{9,13},{10,... | collective-permute-start | bytes 442376 | tf_op jit(solution)/shard_map/ppermute | solution.py:32
  51.4 0.0 copy-start.3
  51.4 0.0 copy-start.5
  51.4 0.7 collective-permute-start.26
  52.2 2.9 %train_gradient_side.1 = (f32[512,256]{1,0:T(8,128)S(1)}, f32[16,512]{1,0:T(8,128)S(1)}) custom-call(s32[3]{0:T(128)S(1)} %pad_add_fusion.place_ref, bf16[512,4096]{1,0:T(8,128)(2,1)S(1)} %copy-done.2, bf16[16,4096]{1,0:T(8,128)(2,1)S(1)} %copy-done.4, bf16[2,256,256]{2,1,0:T(8,128)(2,1)S(1)} %pad_maximum_fusion.1.rest_0_, ...), custom_call_target="tpu_custom_call" | custom-call | flops 2000000 | bytes 4096 | tf_op jit(solution)/shard_map/train_gradient_side/pallas_call | solution.py:241
  55.1 2.9 %collective-permute-done.19 = bf16[1,288,256]{2,1,0:T(8,128)(2,1)S(1)} collective-permute-done((bf16[1,288,256]{2,1,0:T(8,128)(2,1)S(1)}, bf16[1,288,256]{2,1,0:T(8,128)(2,1)S(1)}, u32[]{:S(2)}, u32[]{:S(2)}) %collective-permute-start.19) | collective-permute-done | bytes 147488 | tf_op jit(solution)/shard_map/ppermute | solution.py:32
  58.1 1.3 %collective-permute-start.24 = (bf16[1,288,256]{2,1,0:T(8,128)(2,1)S(1)}, bf16[1,288,256]{2,1,0:T(8,128)(2,1)S(1)}, u32[]{:S(2)}, u32[]{:S(2)}) collective-permute-start(bf16[1,288,256]{2,1,0:T(8,128)(2,1)S(1)} %collective-permute-done.19), channel_id=1, source_target_pairs={{0,2},{1,3},{2,0},{3,1},{4,6},{5,7},{6,4},{7,5},{8,10},{9,11},{10,... | collective-permute-start | bytes 442376 | tf_op jit(solution)/shard_map/ppermute | solution.py:32
  59.3 0.7 collective-permute-start.25
  60.1 1.4 %collective-permute-start.32 = (bf16[2,288,256]{2,1,0:T(8,128)(2,1)S(1)}, bf16[2,288,256]{2,1,0:T(8,128)(2,1)S(1)}, u32[]{:S(2)}, u32[]{:S(2)}) collective-permute-start(bf16[2,288,256]{2,1,0:T(8,128)(2,1)S(1)} %constant_dynamic-update-slice_fusion.10.rest_4_), channel_id=1, source_target_pairs={{0,2},{1,3},{2,0},{3,1},{4,6},{5,7},{6,4},{7,5},{8,10},{9,11},{10,... | collective-permute-start | bytes 884744 | tf_op jit(solution)/shard_map/ppermute | solution.py:32
  61.5 2.9 %train_input_side.1 = (f32[512,256]{1,0:T(8,128)S(1)}, f32[16,512]{1,0:T(8,128)S(1)}) custom-call(s32[3]{0:T(128)S(1)} %pad_add_fusion.place_ref, bf16[512,4096]{1,0:T(8,128)(2,1)S(1)} %copy-done.3, bf16[16,4096]{1,0:T(8,128)(2,1)S(1)} %bitcast.12, bf16[2,256,256]{2,1,0:T(8,128)(2,1)S(1)} %pad_maximum_fusion.1.rest_0_, ...), custom_call_target="tpu_custom_call" | custom-call | flops 2000000 | bytes 4096 | tf_op jit(solution)/shard_map/train_input_side/pallas_call | solution.py:241
  64.5 0.0 copy-start.9
  64.5 0.1 collective-permute-done.24
  64.7 0.6 collective-permute-start.35
  65.3 0.1 collective-permute-start.34
  65.3 2.4 %collective-permute-done.32.rest_6_ = bf16[2,288,256]{2,1,0:T(8,128)(2,1)S(1)} collective-permute-done((bf16[2,288,256]{2,1,0:T(8,128)(2,1)S(1)}, bf16[2,288,256]{2,1,0:T(8,128)(2,1)S(1)}, u32[]{:S(2)}, u32[]{:S(2)}) %collective-permute-start.32) | collective-permute-done | bytes 294944 | tf_op jit(solution)/shard_map/ppermute | solution.py:32
  67.8 0.5 collective-permute-start.33
  68.3 1.3 %collective-permute-start.28 = (bf16[2,288,256]{2,1,0:T(8,128)(2,1)S(1)}, bf16[2,288,256]{2,1,0:T(8,128)(2,1)S(1)}, u32[]{:S(2)}, u32[]{:S(2)}) collective-permute-start(bf16[2,288,256]{2,1,0:T(8,128)(2,1)S(1)} %constant_dynamic-update-slice_fusion.8.rest_10_), channel_id=1, source_target_pairs={{0,2},{1,3},{2,0},{3,1},{4,6},{5,7},{6,4},{7,5},{8,10},{9,11},{10,... | collective-permute-start | bytes 884744 | tf_op jit(solution)/shard_map/ppermute | solution.py:32
  69.6 0.7 collective-permute-start.27
  70.3 1.2 %train_features.1.feats_ref = bf16[2,512,256]{2,1,0:T(8,128)(2,1)S(1)} custom-call(f32[512,256]{1,0:T(8,128)S(1)} %get-tuple-element.90.values_ref, f32[16,512]{1,0:T(8,128)S(1)} %get-tuple-element.91.back_ref, f32[512,256]{1,0:T(8,128)S(1)} %get-tuple-element.92.inputs_ref, f32[16,512]{1,0:T(8,128)S(1)} %get-tuple-element.93.hidden_ref, s32[1,512]{1,0:T(1,128)S(1)} %copy-done.7), custom_call_target="tpu_custom_call" | custom-call | flops 1000000 | bytes 4096 | tf_op jit(solution)/shard_map/train_features/pallas_call | solution.py:241
  71.6 4.9 %front_tiles.2.rest_2_ = f32[32,16,32]{2,1,0:T(8,128)S(1)} custom-call(s32[3]{0:T(128)S(1)} %pad_add_fusion.place_ref, bf16[2,512,256]{2,1,0:T(8,128)(2,1)S(1)} %train_features.1.feats_ref, bf16[2,288,256]{2,1,0:T(8,128)(2,1)S(1)} %pad_maximum_fusion.rest_0_, bf16[2,288,256]{2,1,0:T(8,128)(2,1)S(1)} %collective-permute-done.29.rest_1_, ...), custom_call_target="tpu_custom_call" | custom-call | flops 1000000 | bytes 4096 | tf_op jit(solution)/shard_map/front_tiles/pallas_call | solution.py:241
  76.5 0.8 collective-permute-done.28.rest_1_
  77.3 1.0 %collective-permute-done.27.rest_0_ = bf16[2,288,256]{2,1,0:T(8,128)(2,1)S(1)} collective-permute-done((bf16[2,288,256]{2,1,0:T(8,128)(2,1)S(1)}, bf16[2,288,256]{2,1,0:T(8,128)(2,1)S(1)}, u32[]{:S(2)}, u32[]{:S(2)}) %collective-permute-start.27) | collective-permute-done | bytes 294944 | tf_op jit(solution)/shard_map/ppermute | solution.py:32
  78.3 0.5 collective-permute-start.37
  78.8 1.3 %front_tiles.3.rest_3_ = f32[32,16,32]{2,1,0:T(8,128)S(1)} custom-call(s32[3]{0:T(128)S(1)} %pad_add_fusion.place_ref, bf16[2,512,256]{2,1,0:T(8,128)(2,1)S(1)} %train_features.1.feats_ref, bf16[2,288,256]{2,1,0:T(8,128)(2,1)S(1)} %collective-permute-done.27.rest_0_, bf16[2,288,256]{2,1,0:T(8,128)(2,1)S(1)} %collective-permute-done.28.rest_1_), custom_call_target="tpu_custom_call" | custom-call | flops 1000000 | bytes 4096 | tf_op jit(solution)/shard_map/front_tiles/pallas_call | solution.py:241
  80.2 0.1 collective-permute-done.37.rest_1_
  80.3 2.2 %score_tiles.1 = f32[1,16,16,32]{3,2,1,0:T(8,128)} custom-call(s32[3]{0:T(128)S(1)} %pad_add_fusion.place_ref, s32[16,32]{1,0:T(8,128)S(1)} %bitcast.13, s32[32]{0:T(128)S(1)} %copy-done.9, bf16[2,512,256]{2,1,0:T(8,128)(2,1)S(1)} %train_features.1.feats_ref, bf16[2,288,256]{2,1,0:T(8,128)(2,1)S(1)} %collective-permute-done.36.rest_0_, ...), custom_call_target="tpu_custom_call" | custom-call | flops 1000000 | bytes 4096 | tf_op jit(solution)/shard_map/score_tiles/pallas_call | solution.py:241
  (58 shorter events, 0.3 us)
Async XLA Ops:
  0.0 29.4 %copy-start = (bf16[128,4096]{1,0:T(8,128)(2,1)S(1)}, bf16[128,4096]{1,0:T(8,128)(2,1)}, u32[]{:S(2)}) copy-start(bf16[128,4096]{1,0:T(8,128)(2,1)} %x_ref.3) | copy-start | bytes 3145732
  0.0 29.4 %copy-start.1 = (bf16[128,4096]{1,0:T(8,128)(2,1)S(1)}, bf16[128,4096]{1,0:T(8,128)(2,1)}, u32[]{:S(2)}) copy-start(bf16[128,4096]{1,0:T(8,128)(2,1)} %g_ref.3) | copy-start | bytes 3145732
  1.0 10.9 %collective-permute-start = (bf16[1,256,256]{2,1,0:T(8,128)(2,1)S(1)}, bf16[1,256,256]{2,1,0:T(8,128)(2,1)S(1)}, u32[]{:S(2)}, u32[]{:S(2)}) collective-permute-start(bf16[1,256,256]{2,1,0:T(8,128)(2,1)S(1)} %maximum_bitcast_fusion), channel_id=1, source_target_pairs={{0,2},{1,3},{2,0},{3,1},{4,6},{5,7},{6,4},{7,5},{8,10},{9,11},{10,... | collective-permute-start | bytes 393224 | tf_op jit(solution)/shard_map/ppermute | solution.py:32
  4.0 7.9 %collective-permute-start.1 = (bf16[1,256,256]{2,1,0:T(8,128)(2,1)S(1)}, bf16[1,256,256]{2,1,0:T(8,128)(2,1)S(1)}, u32[]{:S(2)}, u32[]{:S(2)}) collective-permute-start(bf16[1,256,256]{2,1,0:T(8,128)(2,1)S(1)} %maximum_bitcast_fusion), channel_id=1, source_target_pairs={{0,8},{1,9},{2,10},{3,11},{4,12},{5,13},{6,14},{7,15},{8,0},{9,1},... | collective-permute-start | bytes 393224 | tf_op jit(solution)/shard_map/ppermute | solution.py:32
  5.6 12.6 %collective-permute-start.2 = (bf16[1,256,256]{2,1,0:T(8,128)(2,1)S(1)}, bf16[1,256,256]{2,1,0:T(8,128)(2,1)S(1)}, u32[]{:S(2)}, u32[]{:S(2)}) collective-permute-start(bf16[1,256,256]{2,1,0:T(8,128)(2,1)S(1)} %maximum_bitcast_fusion), channel_id=1, source_target_pairs={{0,16},{1,17},{2,18},{3,19},{4,20},{5,21},{6,22},{7,23},{8,24},{9,... | collective-permute-start | bytes 393224 | tf_op jit(solution)/shard_map/ppermute | solution.py:32
  8.2 10.1 %collective-permute-start.3 = (bf16[1,256,256]{2,1,0:T(8,128)(2,1)S(1)}, bf16[1,256,256]{2,1,0:T(8,128)(2,1)S(1)}, u32[]{:S(2)}, u32[]{:S(2)}) collective-permute-start(bf16[1,256,256]{2,1,0:T(8,128)(2,1)S(1)} %maximum_bitcast_fusion), channel_id=1, source_target_pairs={{0,24},{1,25},{2,26},{3,27},{4,28},{5,29},{6,30},{7,31},{8,16},{9,... | collective-permute-start | bytes 393224 | tf_op jit(solution)/shard_map/ppermute | solution.py:32
  10.1 28.7 %copy-start.8 = (s32[1,128]{1,0:T(1,128)S(1)}, s32[1,128]{1,0:T(1,128)}, u32[]{:S(2)}) copy-start(s32[1,128]{1,0:T(1,128)} %index_ref.2) | copy-start | bytes 1540
  11.9 6.5 %collective-permute-start.4 = (bf16[1,256,256]{2,1,0:T(8,128)(2,1)S(1)}, bf16[1,256,256]{2,1,0:T(8,128)(2,1)S(1)}, u32[]{:S(2)}, u32[]{:S(2)}) collective-permute-start(bf16[1,256,256]{2,1,0:T(8,128)(2,1)S(1)} %collective-permute-done.1), channel_id=1, source_target_pairs={{0,4},{1,5},{2,6},{3,7},{4,0},{5,1},{6,2},{7,3},{8,12},{9,13},{10,... | collective-permute-start | bytes 393224 | tf_op jit(solution)/shard_map/ppermute | solution.py:32
  13.5 11.1 %collective-permute-start.7 = (bf16[2,256,256]{2,1,0:T(8,128)(2,1)S(1)}, bf16[2,256,256]{2,1,0:T(8,128)(2,1)S(1)}, u32[]{:S(2)}, u32[]{:S(2)}) collective-permute-start(bf16[2,256,256]{2,1,0:T(8,128)(2,1)S(1)} %pad_maximum_fusion.1.rest_0_), channel_id=1, source_target_pairs={{0,4},{1,5},{2,6},{3,7},{4,0},{5,1},{6,2},{7,3},{8,12},{9,13},{10,... | collective-permute-start | bytes 786440 | tf_op jit(solution)/shard_map/ppermute | solution.py:32
  14.1 12.8 %collective-permute-start.10 = (bf16[2,256,256]{2,1,0:T(8,128)(2,1)S(1)}, bf16[2,256,256]{2,1,0:T(8,128)(2,1)S(1)}, u32[]{:S(2)}, u32[]{:S(2)}) collective-permute-start(bf16[2,256,256]{2,1,0:T(8,128)(2,1)S(1)} %pad_maximum_fusion.1.rest_0_), channel_id=1, source_target_pairs={{0,1},{1,0},{2,3},{3,2},{4,5},{5,4},{6,7},{7,6},{8,9},{9,8},{10,11... | collective-permute-start | bytes 786440 | tf_op jit(solution)/shard_map/ppermute | solution.py:32
  18.4 5.0 %collective-permute-start.5 = (bf16[1,256,256]{2,1,0:T(8,128)(2,1)S(1)}, bf16[1,256,256]{2,1,0:T(8,128)(2,1)S(1)}, u32[]{:S(2)}, u32[]{:S(2)}) collective-permute-start(bf16[1,256,256]{2,1,0:T(8,128)(2,1)S(1)} %collective-permute-done.2), channel_id=1, source_target_pairs={{0,2},{1,3},{2,0},{3,1},{4,6},{5,7},{6,4},{7,5},{8,10},{9,11},{10,... | collective-permute-start | bytes 393224 | tf_op jit(solution)/shard_map/ppermute | solution.py:32
  18.8 5.8 %collective-permute-start.6 = (bf16[1,256,256]{2,1,0:T(8,128)(2,1)S(1)}, bf16[1,256,256]{2,1,0:T(8,128)(2,1)S(1)}, u32[]{:S(2)}, u32[]{:S(2)}) collective-permute-start(bf16[1,256,256]{2,1,0:T(8,128)(2,1)S(1)} %collective-permute-done.3), channel_id=1, source_target_pairs={{0,4},{1,5},{2,6},{3,7},{4,0},{5,1},{6,2},{7,3},{8,12},{9,13},{10,... | collective-permute-start | bytes 393224 | tf_op jit(solution)/shard_map/ppermute | solution.py:32
  20.5 6.4 %collective-permute-start.13 = (bf16[2,256,256]{2,1,0:T(8,128)(2,1)S(1)}, bf16[2,256,256]{2,1,0:T(8,128)(2,1)S(1)}, u32[]{:S(2)}, u32[]{:S(2)}) collective-permute-start(bf16[2,256,256]{2,1,0:T(8,128)(2,1)S(1)} %constant_dynamic-update-slice_fusion.4.rest_4_), channel_id=1, source_target_pairs={{0,2},{1,3},{2,0},{3,1},{4,6},{5,7},{6,4},{7,5},{8,10},{9,11},{10,... | collective-permute-start | bytes 786440 | tf_op jit(solution)/shard_map/ppermute | solution.py:32
  23.4 4.0 %collective-permute-start.12 = (bf16[2,256,256]{2,1,0:T(8,128)(2,1)S(1)}, bf16[2,256,256]{2,1,0:T(8,128)(2,1)S(1)}, u32[]{:S(2)}, u32[]{:S(2)}) collective-permute-start(bf16[2,256,256]{2,1,0:T(8,128)(2,1)S(1)} %constant_dynamic-update-slice_fusion.4.rest_4_), channel_id=1, source_target_pairs={{0,1},{1,0},{2,3},{3,2},{4,5},{5,4},{6,7},{7,6},{8,9},{9,8},{10,11... | collective-permute-start | bytes 786440 | tf_op jit(solution)/shard_map/ppermute | solution.py:32
  24.6 4.3 %collective-permute-start.16 = (bf16[2,256,256]{2,1,0:T(8,128)(2,1)S(1)}, bf16[2,256,256]{2,1,0:T(8,128)(2,1)S(1)}, u32[]{:S(2)}, u32[]{:S(2)}) collective-permute-start(bf16[2,256,256]{2,1,0:T(8,128)(2,1)S(1)} %constant_dynamic-update-slice_fusion.2.rest_10_), channel_id=1, source_target_pairs={{0,1},{1,0},{2,3},{3,2},{4,5},{5,4},{6,7},{7,6},{8,9},{9,8},{10,11... | collective-permute-start | bytes 786440 | tf_op jit(solution)/shard_map/ppermute | solution.py:32
  24.7 27.4 %copy-start.2 = (bf16[512,4096]{1,0:T(8,128)(2,1)S(1)}, bf16[512,4096]{1,0:T(8,128)(2,1)}, u32[]{:S(2)}) copy-start(bf16[512,4096]{1,0:T(8,128)(2,1)} %act_ref.2) | copy-start | bytes 12582916
  24.7 27.4 %copy-start.4 = (bf16[16,4096]{1,0:T(8,128)(2,1)S(1)}, bf16[16,4096]{1,0:T(8,128)(2,1)}, u32[]{:S(2)}) copy-start(bf16[16,4096]{1,0:T(8,128)(2,1)} %adapter_ref.1) | copy-start | bytes 393220
  24.7 4.7 %collective-permute-start.15 = (bf16[2,256,256]{2,1,0:T(8,128)(2,1)S(1)}, bf16[2,256,256]{2,1,0:T(8,128)(2,1)S(1)}, u32[]{:S(2)}, u32[]{:S(2)}) collective-permute-start(bf16[2,256,256]{2,1,0:T(8,128)(2,1)S(1)} %constant_dynamic-update-slice_fusion.rest_8_), channel_id=1, source_target_pairs={{0,1},{1,0},{2,3},{3,2},{4,5},{5,4},{6,7},{7,6},{8,9},{9,8},{10,11... | collective-permute-start | bytes 786440 | tf_op jit(solution)/shard_map/ppermute | solution.py:32
  26.9 2.5 %collective-permute-start.11 = (bf16[2,256,256]{2,1,0:T(8,128)(2,1)S(1)}, bf16[2,256,256]{2,1,0:T(8,128)(2,1)S(1)}, u32[]{:S(2)}, u32[]{:S(2)}) collective-permute-start(bf16[2,256,256]{2,1,0:T(8,128)(2,1)S(1)} %collective-permute-done.7.rest_2_), channel_id=1, source_target_pairs={{0,1},{1,0},{2,3},{3,2},{4,5},{5,4},{6,7},{7,6},{8,9},{9,8},{10,11... | collective-permute-start | bytes 786440 | tf_op jit(solution)/shard_map/ppermute | solution.py:32
  26.9 2.5 %collective-permute-start.14 = (bf16[2,256,256]{2,1,0:T(8,128)(2,1)S(1)}, bf16[2,256,256]{2,1,0:T(8,128)(2,1)S(1)}, u32[]{:S(2)}, u32[]{:S(2)}) collective-permute-start(bf16[2,256,256]{2,1,0:T(8,128)(2,1)S(1)} %collective-permute-done.13.rest_6_), channel_id=1, source_target_pairs={{0,1},{1,0},{2,3},{3,2},{4,5},{5,4},{6,7},{7,6},{8,9},{9,8},{10,11... | collective-permute-start | bytes 786440 | tf_op jit(solution)/shard_map/ppermute | solution.py:32
  27.4 8.3 %collective-permute-start.9 = (bf16[2,256,256]{2,1,0:T(8,128)(2,1)S(1)}, bf16[2,256,256]{2,1,0:T(8,128)(2,1)S(1)}, u32[]{:S(2)}, u32[]{:S(2)}) collective-permute-start(bf16[2,256,256]{2,1,0:T(8,128)(2,1)S(1)} %constant_dynamic-update-slice_fusion.2.rest_10_), channel_id=1, source_target_pairs={{0,2},{1,3},{2,0},{3,1},{4,6},{5,7},{6,4},{7,5},{8,10},{9,11},{10,... | collective-permute-start | bytes 786440 | tf_op jit(solution)/shard_map/ppermute | solution.py:32
  28.9 8.0 %collective-permute-start.8 = (bf16[2,256,256]{2,1,0:T(8,128)(2,1)S(1)}, bf16[2,256,256]{2,1,0:T(8,128)(2,1)S(1)}, u32[]{:S(2)}, u32[]{:S(2)}) collective-permute-start(bf16[2,256,256]{2,1,0:T(8,128)(2,1)S(1)} %constant_dynamic-update-slice_fusion.rest_8_), channel_id=1, source_target_pairs={{0,4},{1,5},{2,6},{3,7},{4,0},{5,1},{6,2},{7,3},{8,12},{9,13},{10,... | collective-permute-start | bytes 786440 | tf_op jit(solution)/shard_map/ppermute | solution.py:32
  36.9 1.5 %collective-permute-start.17 = (bf16[2,256,256]{2,1,0:T(8,128)(2,1)S(1)}, bf16[2,256,256]{2,1,0:T(8,128)(2,1)S(1)}, u32[]{:S(2)}, u32[]{:S(2)}) collective-permute-start(bf16[2,256,256]{2,1,0:T(8,128)(2,1)S(1)} %collective-permute-done.8.rest_0_.rest_12_), channel_id=1, source_target_pairs={{0,1},{1,0},{2,3},{3,2},{4,5},{5,4},{6,7},{7,6},{8,9},{9,8},{10,11... | collective-permute-start | bytes 786440 | tf_op jit(solution)/shard_map/ppermute | solution.py:32
  36.9 1.9 %collective-permute-start.18 = (bf16[2,256,256]{2,1,0:T(8,128)(2,1)S(1)}, bf16[2,256,256]{2,1,0:T(8,128)(2,1)S(1)}, u32[]{:S(2)}, u32[]{:S(2)}) collective-permute-start(bf16[2,256,256]{2,1,0:T(8,128)(2,1)S(1)} %collective-permute-done.9.rest_2_.rest_14_), channel_id=1, source_target_pairs={{0,1},{1,0},{2,3},{3,2},{4,5},{5,4},{6,7},{7,6},{8,9},{9,8},{10,11... | collective-permute-start | bytes 786440 | tf_op jit(solution)/shard_map/ppermute | solution.py:32
  40.3 6.3 %collective-permute-start.21 = (bf16[1,288,256]{2,1,0:T(8,128)(2,1)S(1)}, bf16[1,288,256]{2,1,0:T(8,128)(2,1)S(1)}, u32[]{:S(2)}, u32[]{:S(2)}) collective-permute-start(bf16[1,288,256]{2,1,0:T(8,128)(2,1)S(1)} %eval_factors.1), channel_id=1, source_target_pairs={{0,2},{1,3},{2,0},{3,1},{4,6},{5,7},{6,4},{7,5},{8,10},{9,11},{10,... | collective-permute-start | bytes 442376 | tf_op jit(solution)/shard_map/ppermute | solution.py:32
  40.9 9.1 %collective-permute-start.22 = (bf16[1,288,256]{2,1,0:T(8,128)(2,1)S(1)}, bf16[1,288,256]{2,1,0:T(8,128)(2,1)S(1)}, u32[]{:S(2)}, u32[]{:S(2)}) collective-permute-start(bf16[1,288,256]{2,1,0:T(8,128)(2,1)S(1)} %eval_factors.1), channel_id=1, source_target_pairs={{0,8},{1,9},{2,10},{3,11},{4,12},{5,13},{6,14},{7,15},{8,0},{9,1},... | collective-permute-start | bytes 442376 | tf_op jit(solution)/shard_map/ppermute | solution.py:32
  44.1 14.0 %collective-permute-start.19 = (bf16[1,288,256]{2,1,0:T(8,128)(2,1)S(1)}, bf16[1,288,256]{2,1,0:T(8,128)(2,1)S(1)}, u32[]{:S(2)}, u32[]{:S(2)}) collective-permute-start(bf16[1,288,256]{2,1,0:T(8,128)(2,1)S(1)} %eval_factors.1), channel_id=1, source_target_pairs={{0,16},{1,17},{2,18},{3,19},{4,20},{5,21},{6,22},{7,23},{8,24},{9,... | collective-permute-start | bytes 442376 | tf_op jit(solution)/shard_map/ppermute | solution.py:32
  45.2 12.9 %collective-permute-start.20 = (bf16[1,288,256]{2,1,0:T(8,128)(2,1)S(1)}, bf16[1,288,256]{2,1,0:T(8,128)(2,1)S(1)}, u32[]{:S(2)}, u32[]{:S(2)}) collective-permute-start(bf16[1,288,256]{2,1,0:T(8,128)(2,1)S(1)} %eval_factors.1), channel_id=1, source_target_pairs={{0,24},{1,25},{2,26},{3,27},{4,28},{5,29},{6,30},{7,31},{8,16},{9,... | collective-permute-start | bytes 442376 | tf_op jit(solution)/shard_map/ppermute | solution.py:32
  50.0 8.1 %collective-permute-start.23 = (bf16[1,288,256]{2,1,0:T(8,128)(2,1)S(1)}, bf16[1,288,256]{2,1,0:T(8,128)(2,1)S(1)}, u32[]{:S(2)}, u32[]{:S(2)}) collective-permute-start(bf16[1,288,256]{2,1,0:T(8,128)(2,1)S(1)} %collective-permute-done.22), channel_id=1, source_target_pairs={{0,4},{1,5},{2,6},{3,7},{4,0},{5,1},{6,2},{7,3},{8,12},{9,13},{10,... | collective-permute-start | bytes 442376 | tf_op jit(solution)/shard_map/ppermute | solution.py:32
  51.4 10.1 %copy-start.3 = (bf16[512,4096]{1,0:T(8,128)(2,1)S(1)}, bf16[512,4096]{1,0:T(8,128)(2,1)}, u32[]{:S(2)}) copy-start(bf16[512,4096]{1,0:T(8,128)(2,1)} %act_ref.3) | copy-start | bytes 12582916
  51.4 10.1 %copy-start.5 = (bf16[4096,16]{0,1:T(8,128)(2,1)S(1)}, bf16[4096,16]{0,1:T(8,128)(2,1)}, u32[]{:S(2)}) copy-start(bf16[4096,16]{0,1:T(8,128)(2,1)} %param.18) | copy-start | bytes 393220
  51.4 13.2 %collective-permute-start.26 = (bf16[2,288,256]{2,1,0:T(8,128)(2,1)S(1)}, bf16[2,288,256]{2,1,0:T(8,128)(2,1)S(1)}, u32[]{:S(2)}, u32[]{:S(2)}) collective-permute-start(bf16[2,288,256]{2,1,0:T(8,128)(2,1)S(1)} %pad_maximum_fusion.rest_0_), channel_id=1, source_target_pairs={{0,4},{1,5},{2,6},{3,7},{4,0},{5,1},{6,2},{7,3},{8,12},{9,13},{10,... | collective-permute-start | bytes 884744 | tf_op jit(solution)/shard_map/ppermute | solution.py:32
  52.1 15.7 %collective-permute-start.29 = (bf16[2,288,256]{2,1,0:T(8,128)(2,1)S(1)}, bf16[2,288,256]{2,1,0:T(8,128)(2,1)S(1)}, u32[]{:S(2)}, u32[]{:S(2)}) collective-permute-start(bf16[2,288,256]{2,1,0:T(8,128)(2,1)S(1)} %pad_maximum_fusion.rest_0_), channel_id=1, source_target_pairs={{0,1},{1,0},{2,3},{3,2},{4,5},{5,4},{6,7},{7,6},{8,9},{9,8},{10,11... | collective-permute-start | bytes 884744 | tf_op jit(solution)/shard_map/ppermute | solution.py:32
  58.1 6.6 %collective-permute-start.24 = (bf16[1,288,256]{2,1,0:T(8,128)(2,1)S(1)}, bf16[1,288,256]{2,1,0:T(8,128)(2,1)S(1)}, u32[]{:S(2)}, u32[]{:S(2)}) collective-permute-start(bf16[1,288,256]{2,1,0:T(8,128)(2,1)S(1)} %collective-permute-done.19), channel_id=1, source_target_pairs={{0,2},{1,3},{2,0},{3,1},{4,6},{5,7},{6,4},{7,5},{8,10},{9,11},{10,... | collective-permute-start | bytes 442376 | tf_op jit(solution)/shard_map/ppermute | solution.py:32
  59.3 5.3 %collective-permute-start.25 = (bf16[1,288,256]{2,1,0:T(8,128)(2,1)S(1)}, bf16[1,288,256]{2,1,0:T(8,128)(2,1)S(1)}, u32[]{:S(2)}, u32[]{:S(2)}) collective-permute-start(bf16[1,288,256]{2,1,0:T(8,128)(2,1)S(1)} %collective-permute-done.20), channel_id=1, source_target_pairs={{0,4},{1,5},{2,6},{3,7},{4,0},{5,1},{6,2},{7,3},{8,12},{9,13},{10,... | collective-permute-start | bytes 442376 | tf_op jit(solution)/shard_map/ppermute | solution.py:32
  60.1 7.7 %collective-permute-start.32 = (bf16[2,288,256]{2,1,0:T(8,128)(2,1)S(1)}, bf16[2,288,256]{2,1,0:T(8,128)(2,1)S(1)}, u32[]{:S(2)}, u32[]{:S(2)}) collective-permute-start(bf16[2,288,256]{2,1,0:T(8,128)(2,1)S(1)} %constant_dynamic-update-slice_fusion.10.rest_4_), channel_id=1, source_target_pairs={{0,2},{1,3},{2,0},{3,1},{4,6},{5,7},{6,4},{7,5},{8,10},{9,11},{10,... | collective-permute-start | bytes 884744 | tf_op jit(solution)/shard_map/ppermute | solution.py:32
  61.5 8.8 %copy-start.7 = (s32[1,512]{1,0:T(1,128)S(1)}, s32[1,512]{1,0:T(1,128)}, u32[]{:S(2)}) copy-start(s32[1,512]{1,0:T(1,128)} %index_ref.3) | copy-start | bytes 6148
  64.5 15.9 %copy-start.6 = (s32[32,16]{0,1:T(8,128)S(1)}, s32[32,16]{0,1:T(8,128)}, u32[]{:S(2)}) copy-start(s32[32,16]{0,1:T(8,128)} %param.22) | copy-start | bytes 6148
  64.5 15.9 %copy-start.9 = (s32[32]{0:T(128)S(1)}, s32[32]{0:T(128)}, u32[]{:S(2)}) copy-start(s32[32]{0:T(128)} %live_ref.1) | copy-start | bytes 388
  64.6 3.7 %collective-permute-start.31 = (bf16[2,288,256]{2,1,0:T(8,128)(2,1)S(1)}, bf16[2,288,256]{2,1,0:T(8,128)(2,1)S(1)}, u32[]{:S(2)}, u32[]{:S(2)}) collective-permute-start(bf16[2,288,256]{2,1,0:T(8,128)(2,1)S(1)} %constant_dynamic-update-slice_fusion.10.rest_4_), channel_id=1, source_target_pairs={{0,1},{1,0},{2,3},{3,2},{4,5},{5,4},{6,7},{7,6},{8,9},{9,8},{10,11... | collective-permute-start | bytes 884744 | tf_op jit(solution)/shard_map/ppermute | solution.py:32
  64.7 5.0 %collective-permute-start.35 = (bf16[2,288,256]{2,1,0:T(8,128)(2,1)S(1)}, bf16[2,288,256]{2,1,0:T(8,128)(2,1)S(1)}, u32[]{:S(2)}, u32[]{:S(2)}) collective-permute-start(bf16[2,288,256]{2,1,0:T(8,128)(2,1)S(1)} %constant_dynamic-update-slice_fusion.8.rest_10_), channel_id=1, source_target_pairs={{0,1},{1,0},{2,3},{3,2},{4,5},{5,4},{6,7},{7,6},{8,9},{9,8},{10,11... | collective-permute-start | bytes 884744 | tf_op jit(solution)/shard_map/ppermute | solution.py:32
  65.3 6.3 %collective-permute-start.34 = (bf16[2,288,256]{2,1,0:T(8,128)(2,1)S(1)}, bf16[2,288,256]{2,1,0:T(8,128)(2,1)S(1)}, u32[]{:S(2)}, u32[]{:S(2)}) collective-permute-start(bf16[2,288,256]{2,1,0:T(8,128)(2,1)S(1)} %constant_dynamic-update-slice_fusion.6.rest_8_), channel_id=1, source_target_pairs={{0,1},{1,0},{2,3},{3,2},{4,5},{5,4},{6,7},{7,6},{8,9},{9,8},{10,11... | collective-permute-start | bytes 884744 | tf_op jit(solution)/shard_map/ppermute | solution.py:32
  67.8 3.8 %collective-permute-start.30 = (bf16[2,288,256]{2,1,0:T(8,128)(2,1)S(1)}, bf16[2,288,256]{2,1,0:T(8,128)(2,1)S(1)}, u32[]{:S(2)}, u32[]{:S(2)}) collective-permute-start(bf16[2,288,256]{2,1,0:T(8,128)(2,1)S(1)} %collective-permute-done.26.rest_2_), channel_id=1, source_target_pairs={{0,1},{1,0},{2,3},{3,2},{4,5},{5,4},{6,7},{7,6},{8,9},{9,8},{10,11... | collective-permute-start | bytes 884744 | tf_op jit(solution)/shard_map/ppermute | solution.py:32
  67.8 3.8 %collective-permute-start.33 = (bf16[2,288,256]{2,1,0:T(8,128)(2,1)S(1)}, bf16[2,288,256]{2,1,0:T(8,128)(2,1)S(1)}, u32[]{:S(2)}, u32[]{:S(2)}) collective-permute-start(bf16[2,288,256]{2,1,0:T(8,128)(2,1)S(1)} %collective-permute-done.32.rest_6_), channel_id=1, source_target_pairs={{0,1},{1,0},{2,3},{3,2},{4,5},{5,4},{6,7},{7,6},{8,9},{9,8},{10,11... | collective-permute-start | bytes 884744 | tf_op jit(solution)/shard_map/ppermute | solution.py:32
  68.3 9.0 %collective-permute-start.28 = (bf16[2,288,256]{2,1,0:T(8,128)(2,1)S(1)}, bf16[2,288,256]{2,1,0:T(8,128)(2,1)S(1)}, u32[]{:S(2)}, u32[]{:S(2)}) collective-permute-start(bf16[2,288,256]{2,1,0:T(8,128)(2,1)S(1)} %constant_dynamic-update-slice_fusion.8.rest_10_), channel_id=1, source_target_pairs={{0,2},{1,3},{2,0},{3,1},{4,6},{5,7},{6,4},{7,5},{8,10},{9,11},{10,... | collective-permute-start | bytes 884744 | tf_op jit(solution)/shard_map/ppermute | solution.py:32
  69.6 8.7 %collective-permute-start.27 = (bf16[2,288,256]{2,1,0:T(8,128)(2,1)S(1)}, bf16[2,288,256]{2,1,0:T(8,128)(2,1)S(1)}, u32[]{:S(2)}, u32[]{:S(2)}) collective-permute-start(bf16[2,288,256]{2,1,0:T(8,128)(2,1)S(1)} %constant_dynamic-update-slice_fusion.6.rest_8_), channel_id=1, source_target_pairs={{0,4},{1,5},{2,6},{3,7},{4,0},{5,1},{6,2},{7,3},{8,12},{9,13},{10,... | collective-permute-start | bytes 884744 | tf_op jit(solution)/shard_map/ppermute | solution.py:32
  78.3 1.9 %collective-permute-start.36 = (bf16[2,288,256]{2,1,0:T(8,128)(2,1)S(1)}, bf16[2,288,256]{2,1,0:T(8,128)(2,1)S(1)}, u32[]{:S(2)}, u32[]{:S(2)}) collective-permute-start(bf16[2,288,256]{2,1,0:T(8,128)(2,1)S(1)} %collective-permute-done.27.rest_0_), channel_id=1, source_target_pairs={{0,1},{1,0},{2,3},{3,2},{4,5},{5,4},{6,7},{7,6},{8,9},{9,8},{10,11... | collective-permute-start | bytes 884744 | tf_op jit(solution)/shard_map/ppermute | solution.py:32
  78.3 2.0 %collective-permute-start.37 = (bf16[2,288,256]{2,1,0:T(8,128)(2,1)S(1)}, bf16[2,288,256]{2,1,0:T(8,128)(2,1)S(1)}, u32[]{:S(2)}, u32[]{:S(2)}) collective-permute-start(bf16[2,288,256]{2,1,0:T(8,128)(2,1)S(1)} %collective-permute-done.28.rest_1_), channel_id=1, source_target_pairs={{0,1},{1,0},{2,3},{3,2},{4,5},{5,4},{6,7},{7,6},{8,9},{9,8},{10,11... | collective-permute-start | bytes 884744 | tf_op jit(solution)/shard_map/ppermute | solution.py:32
